TPU v7x, 32 devices: a whole 2x2x4 slice. The times are simulated.
32 devices in a mesh: row: 16 (over z, x, core), col: 2 (over y).
Axes of the slice: x: 2, y: 2, z: 4, core: 2. Of those that a mesh axis runs over, the one named last changes fastest.
Arguments:
- trailing: float32 [8192, 2048], P('row', 'col'), may hold values from -6 to 6
- reflectors: float32 [8192, 256], P('row', 'col'), may hold values from -0.25 to 0.25
- leaf_factor: float32 [4096, 256], P('row', 'col'), may hold values from -0.5 to 0.5
- node_reflect: float32 [4, 4096, 256], P(None, 'row', 'col'), may hold values from -0.375 to 0.375
- node_factor: float32 [4, 4096, 256], P(None, 'row', 'col'), may hold values from -0.5 to 0.5
Outputs:
- updated: float32 [8192, 2048], P('row', 'col')
All inputs are finite; a program needn't handle non-finite values.
Results may differ from a plain program's by a relative error of at most 0.00014.
Values sent between devices are 32-bit elements; how exact they have to be, the bound alone decides.
No kernel may reach another device: no remote copies, remote signals or barrier semaphores. Data moves between devices by JAX's collectives and lax.ppermute only.
A program may use at most 64 MiB of HBM per device.

v0:
```python
import jax
import jax.numpy as jnp
from jax import lax
from jax.sharding import PartitionSpec as P

B = 256


highest = lax.Precision.HIGHEST


def swapped(value, axis, apart):
    mask = 2**apart
    pairs = [(source, source ^ mask) for source in range(lax.axis_size(axis))]
    return lax.ppermute(value, axis, pairs)


def triangle(factor):
    return jnp.triu(factor) + 0.5 * jnp.eye(factor.shape[-1], dtype=factor.dtype)


def combine(upper_rows, partner_rows, other_piece, node_y, node_full, clear):
    chosen_y = jnp.where(clear, other_piece, node_y)
    chosen_tri = triangle(jnp.where(clear, node_full, other_piece))
    leader_rows = jnp.where(clear, upper_rows, partner_rows)
    follower_rows = jnp.where(clear, partner_rows, upper_rows)
    summed = leader_rows + jnp.einsum("kb,kc->bc", chosen_y, follower_rows, precision=highest)
    coupling = jnp.einsum("kb,kc->bc", chosen_tri, summed, precision=highest)
    lowered = upper_rows - jnp.einsum("bk,kc->bc", chosen_y, coupling, precision=highest)
    return jnp.where(clear, upper_rows - coupling, lowered)


def per_device(trailing, reflectors, leaf_factor, node_reflect, node_factor):
    vectors, leaf_full, node_y_all, node_f_all = (
        lax.all_gather(reflectors, "col", axis=1, tiled=True),
        lax.all_gather(leaf_factor, "col", axis=1, tiled=True),
        lax.all_gather(node_reflect, "col", axis=2, tiled=True),
        lax.all_gather(node_factor, "col", axis=2, tiled=True),
    )
    leaf_tri = triangle(leaf_full)
    inner = jnp.einsum("rb,rc->bc", vectors, trailing, precision=highest)
    scaled = jnp.einsum("kb,kc->bc", leaf_tri, inner, precision=highest)
    leafed = trailing - jnp.einsum("rb,bc->rc", vectors, scaled, precision=highest)
    upper_rows = leafed[:B]
    remainder = leafed[B:]
    position = lax.axis_index("row")
    levels = lax.axis_size("row").bit_length() - 1
    clears = []
    pieces = []
    for section in range(levels):
        clear = position // (1 << section) % 2 == 0
        clears.append(clear)
        pieces.append(jnp.where(clear, node_f_all[section], node_y_all[section]))
    for section in range(levels):
        partner_rows, other_piece = swapped((upper_rows, pieces[section]), "row", section)
        upper_rows = combine(
            upper_rows,
            partner_rows,
            other_piece,
            node_y_all[section],
            node_f_all[section],
            clears[section],
        )
    return jnp.concatenate([upper_rows, remainder], axis=0)


def solution(mesh):
    in_specs = (
        P("row", "col"),
        P("row", "col"),
        P("row", "col"),
        P(None, "row", "col"),
        P(None, "row", "col"),
    )
    out_specs = P("row", "col")
    return jax.shard_map(
        per_device, mesh=mesh, in_specs=in_specs, out_specs=out_specs, check_vma=False
    )
```

profile of v0, /device:TPU:0, one launch (start us, length us, event | category | flops | bytes accessed | tf_op | source)
XLA Modules:
  0.0 205.0 jit_solution(11143404956473625070)
XLA Ops:
  6.5 0.0 all-gather.5.cloned.1.call-start
  6.5 0.7 all-gather.5.cloned.1.call-update
  7.3 0.0 all-gather.3.cloned.1.call-start
  7.3 0.7 all-gather.3.cloned.1.call-update
  8.0 7.4 %all_gather.12 = f32[256,256]{1,0:T(8,128)S(1)} all-gather(f32[256,128]{1,0:T(8,128)} %param.7), channel_id=1, replica_groups=mesh['row'=16,'col'=2] {'col'}, dimensions={1}, use_global_device_ids=true | all-gather | bytes 393216 | tf_op jit(solution)/shard_map/all_gather | solution.py:36
  15.4 12.8 %all_gather.13 = f32[512,256]{1,0:T(8,128)S(1)} all-gather(f32[512,128]{1,0:T(8,128)} %param.6), channel_id=1, replica_groups=mesh['row'=16,'col'=2] {'col'}, dimensions={1}, use_global_device_ids=true | all-gather | bytes 786432 | tf_op jit(solution)/shard_map/all_gather | solution.py:35
  28.3 0.0 copy-done.1
  28.3 1.9 fusion.94
  30.2 0.0 copy-start.2
  30.2 1.1 fusion.28
  31.3 0.4 copy-done.2
  31.8 1.9 bitcast_subtract_fusion
  33.7 1.6 fusion.93
  35.3 0.0 collective-permute-start.1
  35.3 23.9 %all-gather.3.cloned.1.call-done = f32[4,256,256]{2,1,0:T(8,128)} async-done(((f32[4,256,128]{2,1,0:T(8,128)}), f32[4,256,256]{2,1,0:T(8,128)}) %all-gather.3.cloned.1.call-update) | async-done | bytes 1048592 | tf_op jit(solution)/shard_map/all_gather | solution.py:38
  59.2 1.6 fusion.44
  60.8 0.0 copy-start.3
  60.8 0.1 collective-permute-start
  60.9 0.0 collective-permute-done.1
  60.9 1.5 collective-permute-done
  62.4 0.0 copy-done
  62.4 2.3 %fusion.17 = f32[256,1024]{1,0:T(8,128)S(1)} fusion(f32[256,1024]{1,0:T(8,128)} %collective-permute-done.1, pred[]{:T(512)S(6)} %eq.35, f32[256,256]{1,0:T(8,128)S(1)} %collective-permute-done, f32[4,256,256]{2,1,0:T(8,128)S(1)} %copy-done, f32[512,1024]{1,0:T(8,128)S(1)} %bitcast_subtract_fusion), kind=kOutput, calls=%fused_computation.27 | convolution fusion | flops 805634048 | bytes 3671040 | tf_op jit(solution)/shard_map/kb,kc->bc/dot_general | solution.py:27
  64.7 0.0 copy-done.3
  64.8 1.2 fusion.15
  65.9 1.2 subtract_select_fusion.3
  67.1 1.5 collective-permute-start.3
  68.6 0.6 collective-permute-start.2
  69.2 28.8 %collective-permute-done.2 = f32[256,256]{1,0:T(8,128)S(1)} collective-permute-done((f32[256,256]{1,0:T(8,128)S(1)}, f32[256,256]{1,0:T(8,128)S(1)}, u32[]{:S(2)}, u32[]{:S(2)}) %collective-permute-start.2) | collective-permute-done | bytes 262176 | tf_op jit(solution)/shard_map/ppermute | solution.py:15
  98.0 0.0 collective-permute-done.3
  98.0 1.1 fusion.12
  99.1 1.2 fusion.10
  100.2 1.4 subtract_select_fusion.2
  101.6 1.6 collective-permute-start.5
  103.1 0.5 collective-permute-start.4
  103.7 28.0 %collective-permute-done.4 = f32[256,256]{1,0:T(8,128)S(1)} collective-permute-done((f32[256,256]{1,0:T(8,128)S(1)}, f32[256,256]{1,0:T(8,128)S(1)}, u32[]{:S(2)}, u32[]{:S(2)}) %collective-permute-start.4) | collective-permute-done | bytes 262176 | tf_op jit(solution)/shard_map/ppermute | solution.py:15
  131.6 0.0 collective-permute-done.5
  131.6 1.1 fusion.7
  132.7 1.2 fusion.5
  133.9 1.2 subtract_select_fusion.1
  135.1 2.5 %collective-permute-start.7 = (f32[256,1024]{1,0:T(8,128)S(1)}, f32[256,1024]{1,0:T(8,128)S(1)}, u32[]{:S(2)}, u32[]{:S(2)}) collective-permute-start(f32[256,1024]{1,0:T(8,128)S(1)} %subtract_select_fusion.1), channel_id=1, source_target_pairs={{0,16},{2,18},{4,20},{6,22},{8,24},{10,26},{12,28},{14,30},{16,0},... | collective-permute-start | bytes 3145736 | tf_op jit(solution)/shard_map/ppermute | solution.py:15
  137.5 0.5 collective-permute-start.6
  138.1 55.1 %collective-permute-done.6 = f32[256,256]{1,0:T(8,128)S(1)} collective-permute-done((f32[256,256]{1,0:T(8,128)S(1)}, f32[256,256]{1,0:T(8,128)S(1)}, u32[]{:S(2)}, u32[]{:S(2)}) %collective-permute-start.6) | collective-permute-done | bytes 262176 | tf_op jit(solution)/shard_map/ppermute | solution.py:15
  193.2 0.0 collective-permute-done.7
  193.2 1.1 fusion.2
  194.3 1.2 fusion
  195.4 1.2 subtract_select_fusion
  196.6 0.0 copy-done.4
  196.7 1.5 pad_maximum_fusion
  (5 shorter events, 0.0 us)
Async XLA Ops:
  6.5 21.7 %copy-start.1 = (f32[512,1024]{1,0:T(8,128)S(1)}, f32[512,1024]{1,0:T(8,128)}, u32[]{:S(2)}) copy-start(f32[512,1024]{1,0:T(8,128)} %param.5) | copy-start | bytes 6291460
  6.5 28.8 %all-gather.5.cloned.1.call-start = ((), (), s32[]{:S(2)}) async-start(), calls=%async_computation.1 | async-start | bytes 1572864 | tf_op jit(solution)/shard_map/all_gather | solution.py:37
  7.3 51.9 %all-gather.3.cloned.1.call-start = ((), (), s32[]{:S(2)}) async-start(), calls=%async_computation | async-start | bytes 1572864 | tf_op jit(solution)/shard_map/all_gather | solution.py:38
  30.2 1.6 copy-start.2
  35.3 25.6 %collective-permute-start.1 = (f32[256,1024]{1,0:T(8,128)}, f32[256,1024]{1,0:T(8,128)}, u32[]{:S(2)}, u32[]{:S(2)}) collective-permute-start(f32[256,1024]{1,0:T(8,128)} %get-tuple-element.9), channel_id=1, source_target_pairs={{0,2},{2,0},{4,6},{6,4},{8,10},{10,8},{12,14},{14,12},{16,18},{18,... | collective-permute-start | bytes 3145736 | tf_op jit(solution)/shard_map/ppermute | solution.py:15
  35.3 27.1 %copy-start = (f32[4,256,256]{2,1,0:T(8,128)S(1)}, f32[4,256,256]{2,1,0:T(8,128)}, u32[]{:S(2)}) copy-start(f32[4,256,256]{2,1,0:T(8,128)} %all-gather.5.cloned.1.call-done) | copy-start | bytes 3145732
  60.8 3.9 %copy-start.3 = (f32[4,256,256]{2,1,0:T(8,128)S(1)}, f32[4,256,256]{2,1,0:T(8,128)}, u32[]{:S(2)}) copy-start(f32[4,256,256]{2,1,0:T(8,128)} %all-gather.3.cloned.1.call-done) | copy-start | bytes 3145732
  60.8 1.6 collective-permute-start
  67.1 30.9 %collective-permute-start.3 = (f32[256,1024]{1,0:T(8,128)S(1)}, f32[256,1024]{1,0:T(8,128)S(1)}, u32[]{:S(2)}, u32[]{:S(2)}) collective-permute-start(f32[256,1024]{1,0:T(8,128)S(1)} %subtract_select_fusion.3), channel_id=1, source_target_pairs={{0,4},{2,6},{4,0},{6,2},{8,12},{10,14},{12,8},{14,10},{16,20},{18,... | collective-permute-start | bytes 3145736 | tf_op jit(solution)/shard_map/ppermute | solution.py:15
  68.6 29.3 %collective-permute-start.2 = (f32[256,256]{1,0:T(8,128)S(1)}, f32[256,256]{1,0:T(8,128)S(1)}, u32[]{:S(2)}, u32[]{:S(2)}) collective-permute-start(f32[256,256]{1,0:T(8,128)S(1)} %get-tuple-element.7), channel_id=1, source_target_pairs={{0,4},{2,6},{4,0},{6,2},{8,12},{10,14},{12,8},{14,10},{16,20},{18,... | collective-permute-start | bytes 786440 | tf_op jit(solution)/shard_map/ppermute | solution.py:15
  101.6 30.0 %collective-permute-start.5 = (f32[256,1024]{1,0:T(8,128)S(1)}, f32[256,1024]{1,0:T(8,128)S(1)}, u32[]{:S(2)}, u32[]{:S(2)}) collective-permute-start(f32[256,1024]{1,0:T(8,128)S(1)} %subtract_select_fusion.2), channel_id=1, source_target_pairs={{0,8},{2,10},{4,12},{6,14},{8,0},{10,2},{12,4},{14,6},{16,24},{18,... | collective-permute-start | bytes 3145736 | tf_op jit(solution)/shard_map/ppermute | solution.py:15
  103.1 28.5 %collective-permute-start.4 = (f32[256,256]{1,0:T(8,128)S(1)}, f32[256,256]{1,0:T(8,128)S(1)}, u32[]{:S(2)}, u32[]{:S(2)}) collective-permute-start(f32[256,256]{1,0:T(8,128)S(1)} %get-tuple-element.6), channel_id=1, source_target_pairs={{0,8},{2,10},{4,12},{6,14},{8,0},{10,2},{12,4},{14,6},{16,24},{18,... | collective-permute-start | bytes 786440 | tf_op jit(solution)/shard_map/ppermute | solution.py:15
  135.1 58.1 %collective-permute-start.7 = (f32[256,1024]{1,0:T(8,128)S(1)}, f32[256,1024]{1,0:T(8,128)S(1)}, u32[]{:S(2)}, u32[]{:S(2)}) collective-permute-start(f32[256,1024]{1,0:T(8,128)S(1)} %subtract_select_fusion.1), channel_id=1, source_target_pairs={{0,16},{2,18},{4,20},{6,22},{8,24},{10,26},{12,28},{14,30},{16,0},... | collective-permute-start | bytes 3145736 | tf_op jit(solution)/shard_map/ppermute | solution.py:15
  137.5 55.6 %collective-permute-start.6 = (f32[256,256]{1,0:T(8,128)S(1)}, f32[256,256]{1,0:T(8,128)S(1)}, u32[]{:S(2)}, u32[]{:S(2)}) collective-permute-start(f32[256,256]{1,0:T(8,128)S(1)} %get-tuple-element.5), channel_id=1, source_target_pairs={{0,16},{2,18},{4,20},{6,22},{8,24},{10,26},{12,28},{14,30},{16,0},... | collective-permute-start | bytes 786440 | tf_op jit(solution)/shard_map/ppermute | solution.py:15
  195.4 1.2 copy-start.4
Sparse Core Ops, SparseCore 0:
  8.9 26.2 all-gather.4
  36.8 22.3 all-gather.2
where the time goes:
time: 205 us
  waiting for transfers between devices  139 us (68%)
  blocking collectives  20.2 us (10%)
  matrix products  20 us (10%)
  between operations  13.6 us (7%)
  starting transfers between devices  7.29 us (4%)
  other arithmetic  3.16 us (2%)
  local copies, waits for them, and re-layouts  2.08 us (1%)
    ppermute x8, waiting for transfers between devices, swapped(): return lax.ppermute(value, axis, pairs)  113 us
    all_gather x1, waiting for transfers between devices, per_device(): lax.all_gather(node_factor, 'col', axis=2, tiled=True)  23.9 us
    all_gather x1, blocking collectives, per_device(): lax.all_gather(reflectors, 'col', axis=1, tiled=True)  12.8 us
    all_gather x1, blocking collectives, per_device(): lax.all_gather(leaf_factor, 'col', axis=1, tiled=True)  7.39 us
    ppermute x8, starting transfers between devices, swapped(): return lax.ppermute(value, axis, pairs)  7.25 us
    dot_general x4, matrix products, combine(): jnp.einsum('kb,kc->bc', chosen_y, follower_rows, precision=highest)  5.5 us
    dot_general x4, matrix products, combine(): jnp.einsum('bk,kc->bc', chosen_y, coupling, precision=highest)  4.83 us
    dot_general x4, matrix products, combine(): coupling = jnp.einsum('kb,kc->bc', chosen_tri, summed, precision=highest)  4.68 us
  transfers between devices with their start and end apart: 10, of which 5 were waited for; matrix products, arithmetic and copies ran while one was open for 4% of the time, Pallas kernels for 0%

commit v1 on v0

v1 whole, which is shorter than its diff:
```python
import functools

import jax
import jax.numpy as jnp
from jax import lax
from jax.experimental import pallas as pl
from jax.experimental.pallas import tpu as pltpu
from jax.sharding import PartitionSpec as P

f32 = jnp.float32
LANES = 128
VMEM_LIMIT = 24 * 2**20


def swapped(value, axis, apart):
    mask = 2**apart
    pairs = [(source, source ^ mask) for source in range(lax.axis_size(axis))]
    return lax.ppermute(value, axis, pairs)


def turned(value, axis):
    size = lax.axis_size(axis)
    return [
        lax.ppermute(value, axis, [((to + step) % size, to) for to in range(size)])
        for step in range(1, size)
    ]


def col_blocks(value):
    if value.shape[-1] % LANES == 0:
        return [value] + turned(value, "col")
    return [lax.all_gather(value, "col", axis=value.ndim - 1, tiled=True)]


def in_vmem(value):
    return pltpu.with_memory_space_constraint(value, pltpu.VMEM)


def whole(blocks):
    if len(blocks) == 1:
        return blocks[0]
    size = len(blocks)
    me = lax.axis_index("col")
    ordered = []
    for at in range(size):
        block = blocks[0]
        for step in range(1, size):
            block = jnp.where((me + step) % size == at, blocks[step], block)
        ordered.append(block)
    return jnp.concatenate(ordered, axis=1)


def triangle(factor):
    row = lax.broadcasted_iota(jnp.int32, factor.shape, 0)
    column = lax.broadcasted_iota(jnp.int32, factor.shape, 1)
    kept = jnp.where(row <= column, factor, 0.0)
    return kept + jnp.where(row == column, 0.5, 0.0)


def parts(value):
    high = value.astype(jnp.bfloat16)
    return high, (value - high.astype(f32)).astype(jnp.bfloat16)


def product(left, right, over):
    def dot(a, b):
        return lax.dot_general(a, b, (over, ((), ())), preferred_element_type=f32)

    return dot(left[0], right[0]) + (dot(left[0], right[1]) + dot(left[1], right[0]))


plain = ((1,), (0,))
across = ((1,), (1,))


def leaf_kernel(n_blocks, has_out, *refs):
    trailing = refs[0]
    vectors = parts(whole([ref[...] for ref in refs[1 : 1 + n_blocks]]))
    factor = parts(triangle(whole([ref[...] for ref in refs[1 + n_blocks : 1 + 2 * n_blocks]])))
    top_ref, rest_ref = refs[-2:]
    size = top_ref.shape[1]
    turned_rows = trailing[...].T
    inner = product(parts(turned_rows), vectors, plain)
    scaled = parts(product(parts(inner), factor, plain))
    upper = [part[:size] for part in vectors]
    lower = [part[size:] for part in vectors]
    top_ref[...] = turned_rows[:, :size] - product(scaled, upper, across)
    rest_ref[...] = trailing[size:, :] - product(lower, scaled, across)


def leaf(trailing, vectors, factor, start, width, out):
    rows, columns = trailing.shape
    size = factor[0].shape[0]
    blocks = [in_vmem(b) for b in vectors + factor]
    operands = [trailing] + blocks
    in_specs = [pl.BlockSpec((rows, width), lambda i: (0, start // width))]
    in_specs += [pl.BlockSpec(memory_space=pltpu.VMEM)] * len(blocks)
    aliases = {}
    if out is not None:
        aliases = {len(operands): 1}
        operands.append(out)
        in_specs.append(pl.BlockSpec(memory_space=pl.ANY))
    lower = rows // size - 1
    return pl.pallas_call(
        functools.partial(leaf_kernel, len(vectors), out is not None),
        grid=(1,),
        out_shape=(
            pltpu.VMEM((width, size), f32),
            jax.ShapeDtypeStruct((rows, columns), f32),
        ),
        in_specs=in_specs,
        out_specs=(
            pl.BlockSpec(memory_space=pltpu.VMEM),
            pl.BlockSpec((rows - size, width), lambda i: (1, start // width)),
        ),
        input_output_aliases=aliases,
        compiler_params=pltpu.CompilerParams(vmem_limit_bytes=VMEM_LIMIT),
        cost_estimate=pl.CostEstimate(
            flops=6 * width * size * (2 * rows + size),
            bytes_accessed=8 * rows * width,
            transcendentals=0,
        ),
        name="leaf",
    )(*operands)


def combine_kernel(section, n_blocks, last, *refs):
    mine = refs[0][...]
    other = refs[1][...]
    own = whole([ref[...] for ref in refs[2 : 2 + n_blocks]])
    partner = whole([ref[...] for ref in refs[2 + n_blocks : 2 + 2 * n_blocks]])
    out_ref = refs[-1]
    clear = lax.axis_index("row") // (1 << section) % 2 == 0
    node_y = parts(jnp.where(clear, partner, own))
    node_t = parts(triangle(jnp.where(clear, own, partner)))
    leader = jnp.where(clear, mine, other)
    follower = jnp.where(clear, other, mine)
    summed = leader + product(parts(follower), node_y, plain)
    coupling = product(parts(summed), node_t, plain)

    def write(value):
        out_ref[...] = value.T if last else value

    @pl.when(clear)
    def _():
        write(mine - coupling)

    @pl.when(jnp.logical_not(clear))
    def _():
        write(mine - product(parts(coupling), node_y, across))


def combine(mine, other, own, partner, section, start, out):
    width, size = mine.shape
    operands = [in_vmem(x) for x in [mine, other] + own + partner]
    in_specs = [pl.BlockSpec(memory_space=pltpu.VMEM)] * len(operands)
    last = out is not None
    if last:
        extra = dict(
            grid=(1,),
            out_shape=jax.ShapeDtypeStruct(out.shape, f32),
            out_specs=pl.BlockSpec((size, width), lambda i: (0, start // width)),
            input_output_aliases={len(operands): 0},
        )
        operands.append(out)
        in_specs.append(pl.BlockSpec(memory_space=pl.ANY))
    else:
        extra = dict(
            out_shape=pltpu.VMEM((width, size), f32),
            out_specs=pl.BlockSpec(memory_space=pltpu.VMEM),
        )
    return pl.pallas_call(
        functools.partial(combine_kernel, section, len(own), last),
        in_specs=in_specs,
        compiler_params=pltpu.CompilerParams(vmem_limit_bytes=VMEM_LIMIT),
        cost_estimate=pl.CostEstimate(
            flops=18 * width * size * size, bytes_accessed=8 * size * width, transcendentals=0
        ),
        name="combine",
        **extra,
    )(*operands)


def widths_of(columns):
    widths = []
    left = columns
    while left:
        width = LANES if len(widths) < 4 or left < 2 * LANES else 2 * LANES
        widths.append(width)
        left -= width
    return widths


def per_device(trailing, reflectors, leaf_factor, node_reflect, node_factor):
    size = leaf_factor.shape[0]
    position = lax.axis_index("row")
    levels = lax.axis_size("row").bit_length() - 1
    pieces = [
        jnp.where(position // (1 << s) % 2 == 0, node_factor[s], node_reflect[s])
        for s in range(levels)
    ]
    vectors = col_blocks(reflectors)
    factor = col_blocks(leaf_factor)
    owns, partners = [], []
    for s in range(levels):
        if s == 0:
            own = col_blocks(pieces[0])
            partner = [swapped(block, "row", 0) for block in own]
        else:
            both = jnp.stack([pieces[s], swapped(pieces[s], "row", s)])
            blocks = col_blocks(both)
            own = [block[0] for block in blocks]
            partner = [block[1] for block in blocks]
        owns.append(own)
        partners.append(partner)

    widths = widths_of(trailing.shape[1])
    starts = [sum(widths[:c]) for c in range(len(widths))]
    tops = []
    out = None
    for start, width in zip(starts, widths):
        top, out = leaf(trailing, vectors, factor, start, width, out)
        tops.append(top)
    for c, start in enumerate(starts):
        for s in range(levels):
            other = swapped(tops[c], "row", s)
            result = combine(
                tops[c], other, owns[s], partners[s], s, start, out if s == levels - 1 else None
            )
            if s == levels - 1:
                out = result
            else:
                tops[c] = result
    return out


def solution(mesh):
    in_specs = (
        P("row", "col"),
        P("row", "col"),
        P("row", "col"),
        P(None, "row", "col"),
        P(None, "row", "col"),
    )
    out_specs = P("row", "col")
    return jax.shard_map(
        per_device, mesh=mesh, in_specs=in_specs, out_specs=out_specs, check_vma=False
    )
```

time: 205 us -> 124 us (0.60)
  waiting for transfers between devices: 139 us -> 53.6 us
  starting transfers between devices: 7.29 us -> 37.6 us
  Pallas kernels: 0 us -> 27.5 us
  blocking collectives: 20.2 us -> 0 us
  matrix products: 20 us -> 0 us
  between operations: 13.6 us -> 0.25 us
    ppermute x8 -> x29, waiting for transfers between devices: 113 us -> 48.4 us  [swapped(): return lax.ppermute(value, axis, pairs)]
    pallas_call x0 -> x30, Pallas kernels: none -> 27.5 us  [the longest x24 17.7 us: combine(): pl.pallas_call(functools.partial(combine_kernel, section, len(own), last)...]
    all_gather x2 -> x0, waiting for transfers between devices: 23.9 us -> none  [the longest x1 23.9 us: per_device(): lax.all_gather(node_factor, 'col', axis=2, tiled=True)]
    ppermute x8 -> x29, starting transfers between devices: 7.25 us -> 29.9 us  [swapped(): return lax.ppermute(value, axis, pairs)]
    all_gather x2 -> x0, blocking collectives: 20.2 us -> none  [the longest x1 12.8 us: per_device(): lax.all_gather(reflectors, 'col', axis=1, tiled=True)]
    dot_general x15 -> x0, matrix products: 20 us -> none  [the longest x4 5.5 us: combine(): jnp.einsum('kb,kc->bc', chosen_y, follower_rows, precision=highest)]
    ppermute x0 -> x6, starting transfers between devices: none -> 7.67 us  [turned(): lax.ppermute(value, axis, [((to + step) % size, to) for to in range(size)])]
    ppermute x0 -> x6, waiting for transfers between devices: none -> 5.24 us  [turned(): lax.ppermute(value, axis, [((to + step) % size, to) for to in range(size)])]
  transfers between devices with their start and end apart: 10 -> 35, of which waited for: 5 -> 13; matrix products, arithmetic and copies ran while one was open for 4% -> 1% of each run, Pallas kernels for 0% -> 21%
where the time goes in v1:
time: 124 us
  waiting for transfers between devices  53.6 us (43%)
  starting transfers between devices  37.6 us (30%)
  Pallas kernels  27.5 us (22%)
  local copies, waits for them, and re-layouts  3.49 us (3%)
  other arithmetic  1.39 us (1%)
    ppermute x29, waiting for transfers between devices, swapped(): return lax.ppermute(value, axis, pairs)  48.4 us
    ppermute x29, starting transfers between devices, swapped(): return lax.ppermute(value, axis, pairs)  29.9 us
    pallas_call x24, Pallas kernels, combine(): pl.pallas_call(functools.partial(combine_kernel, section, len(own), last)...  17.7 us
    pallas_call x6, Pallas kernels, leaf(): pl.pallas_call(functools.partial(leaf_kernel, len(vectors), out is not No...  9.82 us
    ppermute x6, starting transfers between devices, turned(): lax.ppermute(value, axis, [((to + step) % size, to) for to in range(size)])  7.67 us
    ppermute x6, waiting for transfers between devices, turned(): lax.ppermute(value, axis, [((to + step) % size, to) for to in range(size)])  5.24 us
    unnamed x6, local copies, waits for them, and re-layouts  3.44 us
  transfers between devices with their start and end apart: 35, of which 13 were waited for; matrix products, arithmetic and copies ran while one was open for 1% of the time, Pallas kernels for 21%

profile of v1, /device:TPU:0, one launch (start us, length us, event | category | flops | bytes accessed | tf_op | source)
XLA Modules:
  0.0 123.8 jit_solution(16003628603788626697)
XLA Ops:
  0.0 3.0 %collective-permute-start = (f32[512,128]{1,0:T(8,128)}, f32[512,128]{1,0:T(8,128)S(1)}, u32[]{:S(2)}, u32[]{:S(2)}) collective-permute-start(f32[512,128]{1,0:T(8,128)} %refs_1_.11), channel_id=1, source_target_pairs={{1,0},{0,1},{3,2},{2,3},{5,4},{4,5},{7,6},{6,7},{9,8},{8,9},{11,10... | collective-permute-start | bytes 786440 | tf_op jit(solution)/shard_map/ppermute | solution.py:24
  3.0 1.3 %slice_select_fusion = (f32[1,256,128]{2,1,0:T(8,128)S(1)}, f32[1,256,128]{2,1,0:T(8,128)S(1)}, f32[256,128]{1,0:T(8,128)S(1)}, f32[1,256,128]{2,1,0:T(8,128)S(1)}) fusion(f32[4,256,128]{2,1,0:T(8,128)} %param.8, f32[4,256,128]{2,1,0:T(8,128)} %param.9, pred[]{:T(512)S(6)} %eq.20, pred[]{:T(512)S(6)} %eq.18, pred[]{:T(512)S(6)} %eq.17, pred[]{:T(512)S(6)} %eq.19), kind=kLoop, calls=%fused_computation.9 | loop fusion | flops 131072 | bytes 1572868 | tf_op jit(solution)/shard_map/jit(_where)/select_n | solution.py:199
  4.3 2.1 %collective-permute-start.3 = (f32[256,128]{1,0:T(8,128)S(1)}, f32[256,128]{1,0:T(8,128)S(1)}, u32[]{:S(2)}, u32[]{:S(2)}) collective-permute-start(f32[256,128]{1,0:T(8,128)S(1)} %get-tuple-element.31.refs_2_), channel_id=1, source_target_pairs={{1,0},{0,1},{3,2},{2,3},{5,4},{4,5},{7,6},{6,7},{9,8},{8,9},{11,10... | collective-permute-start | bytes 393224 | tf_op jit(solution)/shard_map/ppermute | solution.py:24
  6.4 1.5 %collective-permute-start.7 = (f32[256,128]{1,0:T(8,128)S(1)}, f32[256,128]{1,0:T(8,128)S(1)}, u32[]{:S(2)}, u32[]{:S(2)}) collective-permute-start(f32[256,128]{1,0:T(8,128)S(1)} %bitcast.34), channel_id=1, source_target_pairs={{0,4},{2,6},{4,0},{6,2},{8,12},{10,14},{12,8},{14,10},{16,20},{18,... | collective-permute-start | bytes 393224 | tf_op jit(solution)/shard_map/ppermute | solution.py:18
  7.9 5.2 %collective-permute-done.1.refs_4_ = f32[256,128]{1,0:T(8,128)S(1)} collective-permute-done((f32[256,128]{1,0:T(8,128)}, f32[256,128]{1,0:T(8,128)S(1)}, u32[]{:S(2)}, u32[]{:S(2)}) %collective-permute-start.1) | collective-permute-done | bytes 131104 | tf_op jit(solution)/shard_map/ppermute | solution.py:24
  13.1 2.1 %collective-permute-start.10 = (f32[256,128]{1,0:T(8,128)S(1)}, f32[256,128]{1,0:T(8,128)S(1)}, u32[]{:S(2)}, u32[]{:S(2)}) collective-permute-start(f32[256,128]{1,0:T(8,128)S(1)} %bitcast.27), channel_id=1, source_target_pairs={{0,8},{2,10},{4,12},{6,14},{8,0},{10,2},{12,4},{14,6},{16,24},{18,... | collective-permute-start | bytes 393224 | tf_op jit(solution)/shard_map/ppermute | solution.py:18
  15.3 1.6 %copy-done = f32[512,1024]{1,0:T(8,128)S(1)} copy-done((f32[512,1024]{1,0:T(8,128)S(1)}, f32[512,1024]{1,0:T(8,128)}, u32[]{:S(2)}) %copy-start) | copy-done | bytes 2097176
  16.8 0.9 copy-done.1
  17.8 0.9 copy-done.2
  18.7 1.6 %leaf.6 = (f32[128,256]{1,0:T(8,128)S(1)}, f32[512,1024]{1,0:T(8,128)}) custom-call(f32[512,1024]{1,0:T(8,128)S(1)} %copy-done, f32[512,128]{1,0:T(8,128)S(1)} %copy-done.1, f32[512,128]{1,0:T(8,128)S(1)} %collective-permute-done.refs_2_, f32[256,128]{1,0:T(8,128)S(1)} %copy-done.2, f32[256,128]{1,0:T(8,128)S(1)} %collective-permute-done.1.refs_4_), custom_call_target="tpu_custom_call" | custom-call | flops 251658240 | bytes 524288 | tf_op jit(solution)/shard_map/leaf/pallas_call | solution.py:104
  20.3 1.6 %leaf.7 = (f32[128,256]{1,0:T(8,128)S(1)}, f32[512,1024]{1,0:T(8,128)}) custom-call(f32[512,1024]{1,0:T(8,128)S(1)} %copy-done, f32[512,128]{1,0:T(8,128)S(1)} %copy-done.1, f32[512,128]{1,0:T(8,128)S(1)} %collective-permute-done.refs_2_, f32[256,128]{1,0:T(8,128)S(1)} %copy-done.2, ...), custom_call_target="tpu_custom_call", output_to_operand_aliasing={{1}: (5, {})} | custom-call | flops 251658240 | bytes 524288 | tf_op jit(solution)/shard_map/leaf/pallas_call | solution.py:104
  21.8 1.6 %leaf.8 = (f32[128,256]{1,0:T(8,128)S(1)}, f32[512,1024]{1,0:T(8,128)}) custom-call(f32[512,1024]{1,0:T(8,128)S(1)} %copy-done, f32[512,128]{1,0:T(8,128)S(1)} %copy-done.1, f32[512,128]{1,0:T(8,128)S(1)} %collective-permute-done.refs_2_, f32[256,128]{1,0:T(8,128)S(1)} %copy-done.2, ...), custom_call_target="tpu_custom_call", output_to_operand_aliasing={{1}: (5, {})} | custom-call | flops 251658240 | bytes 524288 | tf_op jit(solution)/shard_map/leaf/pallas_call | solution.py:104
  23.4 1.6 %leaf.9 = (f32[128,256]{1,0:T(8,128)S(1)}, f32[512,1024]{1,0:T(8,128)}) custom-call(f32[512,1024]{1,0:T(8,128)S(1)} %copy-done, f32[512,128]{1,0:T(8,128)S(1)} %copy-done.1, f32[512,128]{1,0:T(8,128)S(1)} %collective-permute-done.refs_2_, f32[256,128]{1,0:T(8,128)S(1)} %copy-done.2, ...), custom_call_target="tpu_custom_call", output_to_operand_aliasing={{1}: (5, {})} | custom-call | flops 251658240 | bytes 524288 | tf_op jit(solution)/shard_map/leaf/pallas_call | solution.py:104
  25.4 1.8 %leaf.10 = (f32[256,256]{1,0:T(8,128)S(1)}, f32[512,1024]{1,0:T(8,128)}) custom-call(f32[512,1024]{1,0:T(8,128)S(1)} %copy-done, f32[512,128]{1,0:T(8,128)S(1)} %copy-done.1, f32[512,128]{1,0:T(8,128)S(1)} %collective-permute-done.refs_2_, f32[256,128]{1,0:T(8,128)S(1)} %copy-done.2, ...), custom_call_target="tpu_custom_call", output_to_operand_aliasing={{1}: (5, {})} | custom-call | flops 503316480 | bytes 1048576 | tf_op jit(solution)/shard_map/leaf/pallas_call | solution.py:104
  27.2 1.8 %leaf.11 = (f32[256,256]{1,0:T(8,128)S(1)}, f32[512,1024]{1,0:T(8,128)}) custom-call(f32[512,1024]{1,0:T(8,128)S(1)} %copy-done, f32[512,128]{1,0:T(8,128)S(1)} %copy-done.1, f32[512,128]{1,0:T(8,128)S(1)} %collective-permute-done.refs_2_, f32[256,128]{1,0:T(8,128)S(1)} %copy-done.2, ...), custom_call_target="tpu_custom_call", output_to_operand_aliasing={{1}: (5, {})} | custom-call | flops 503316480 | bytes 1048576 | tf_op jit(solution)/shard_map/leaf/pallas_call | solution.py:104
  30.8 1.6 %collective-permute-start.8 = (f32[2,256,128]{2,1,0:T(8,128)S(1)}, f32[2,256,128]{2,1,0:T(8,128)S(1)}, u32[]{:S(2)}, u32[]{:S(2)}) collective-permute-start(f32[2,256,128]{2,1,0:T(8,128)S(1)} %pad_maximum_fusion), channel_id=1, source_target_pairs={{1,0},{0,1},{3,2},{2,3},{5,4},{4,5},{7,6},{6,7},{9,8},{8,9},{11,10... | collective-permute-start | bytes 786440 | tf_op jit(solution)/shard_map/ppermute | solution.py:24
  33.3 2.7 %collective-permute-start.13 = (f32[256,128]{1,0:T(8,128)S(1)}, f32[256,128]{1,0:T(8,128)S(1)}, u32[]{:S(2)}, u32[]{:S(2)}) collective-permute-start(f32[256,128]{1,0:T(8,128)S(1)} %bitcast.20), channel_id=1, source_target_pairs={{0,16},{2,18},{4,20},{6,22},{8,24},{10,26},{12,28},{14,30},{16,0},... | collective-permute-start | bytes 393224 | tf_op jit(solution)/shard_map/ppermute | solution.py:18
  36.0 1.5 %collective-permute-start.20 = (f32[128,256]{1,0:T(8,128)S(1)}, f32[128,256]{1,0:T(8,128)S(1)}, u32[]{:S(2)}, u32[]{:S(2)}) collective-permute-start(f32[128,256]{1,0:T(8,128)S(1)} %combine.30.refs_0_), channel_id=1, source_target_pairs={{0,4},{2,6},{4,0},{6,2},{8,12},{10,14},{12,8},{14,10},{16,20},{18,... | collective-permute-start | bytes 393224 | tf_op jit(solution)/shard_map/ppermute | solution.py:18
  39.0 0.7 combine.24.refs_0_
  40.9 2.0 %collective-permute-done.13.refs_4_ = f32[256,128]{1,0:T(8,128)S(1)} collective-permute-done((f32[256,128]{1,0:T(8,128)S(1)}, f32[256,128]{1,0:T(8,128)S(1)}, u32[]{:S(2)}, u32[]{:S(2)}) %collective-permute-start.13) | collective-permute-done | bytes 131104 | tf_op jit(solution)/shard_map/ppermute | solution.py:18
  42.9 1.5 %collective-permute-start.24 = (f32[128,256]{1,0:T(8,128)S(1)}, f32[128,256]{1,0:T(8,128)S(1)}, u32[]{:S(2)}, u32[]{:S(2)}) collective-permute-start(f32[128,256]{1,0:T(8,128)S(1)} %combine.33.refs_0_), channel_id=1, source_target_pairs={{0,4},{2,6},{4,0},{6,2},{8,12},{10,14},{12,8},{14,10},{16,20},{18,... | collective-permute-start | bytes 393224 | tf_op jit(solution)/shard_map/ppermute | solution.py:18
  45.0 1.5 %collective-permute-start.6 = (f32[256,256]{1,0:T(8,128)S(1)}, f32[256,256]{1,0:T(8,128)S(1)}, u32[]{:S(2)}, u32[]{:S(2)}) collective-permute-start(f32[256,256]{1,0:T(8,128)S(1)} %combine.24.refs_0_), channel_id=1, source_target_pairs={{0,4},{2,6},{4,0},{6,2},{8,12},{10,14},{12,8},{14,10},{16,20},{18,... | collective-permute-start | bytes 786440 | tf_op jit(solution)/shard_map/ppermute | solution.py:18
  48.0 1.3 %collective-permute-done.24.refs_1_ = f32[128,256]{1,0:T(8,128)S(1)} collective-permute-done((f32[128,256]{1,0:T(8,128)S(1)}, f32[128,256]{1,0:T(8,128)S(1)}, u32[]{:S(2)}, u32[]{:S(2)}) %collective-permute-start.24) | collective-permute-done | bytes 131104 | tf_op jit(solution)/shard_map/ppermute | solution.py:18
  50.0 2.2 %collective-permute-done.28.refs_1_ = f32[128,256]{1,0:T(8,128)S(1)} collective-permute-done((f32[128,256]{1,0:T(8,128)S(1)}, f32[128,256]{1,0:T(8,128)S(1)}, u32[]{:S(2)}, u32[]{:S(2)}) %collective-permute-start.28) | collective-permute-done | bytes 131104 | tf_op jit(solution)/shard_map/ppermute | solution.py:18
  53.8 4.0 %collective-permute-done.6.refs_1_ = f32[256,256]{1,0:T(8,128)S(1)} collective-permute-done((f32[256,256]{1,0:T(8,128)S(1)}, f32[256,256]{1,0:T(8,128)S(1)}, u32[]{:S(2)}, u32[]{:S(2)}) %collective-permute-start.6) | collective-permute-done | bytes 262176 | tf_op jit(solution)/shard_map/ppermute | solution.py:18
  58.2 0.7 combine.25.refs_0_
  58.9 3.2 %collective-permute-done.16.refs_1_ = f32[256,256]{1,0:T(8,128)S(1)} collective-permute-done((f32[256,256]{1,0:T(8,128)S(1)}, f32[256,256]{1,0:T(8,128)S(1)}, u32[]{:S(2)}, u32[]{:S(2)}) %collective-permute-start.16) | collective-permute-done | bytes 262176 | tf_op jit(solution)/shard_map/ppermute | solution.py:18
  62.0 1.1 collective-permute-start.25
  63.1 0.8 combine.28.refs_0_
  64.0 1.0 collective-permute-start.29
  65.0 1.1 collective-permute-start.9
  66.1 0.9 collective-permute-start.17
  67.5 0.9 collective-permute-done.25.refs_1_
  68.4 2.1 %collective-permute-start.34 = (f32[128,256]{1,0:T(8,128)S(1)}, f32[128,256]{1,0:T(8,128)S(1)}, u32[]{:S(2)}, u32[]{:S(2)}) collective-permute-start(f32[128,256]{1,0:T(8,128)S(1)} %combine.41.refs_0_), channel_id=1, source_target_pairs={{0,16},{2,18},{4,20},{6,22},{8,24},{10,26},{12,28},{14,30},{16,0},... | collective-permute-start | bytes 393224 | tf_op jit(solution)/shard_map/ppermute | solution.py:18
  71.4 1.2 collective-permute-done.29.refs_1_
  72.6 4.9 %collective-permute-start.22 = (f32[128,256]{1,0:T(8,128)S(1)}, f32[128,256]{1,0:T(8,128)S(1)}, u32[]{:S(2)}, u32[]{:S(2)}) collective-permute-start(f32[128,256]{1,0:T(8,128)S(1)} %combine.32.refs_0_), channel_id=1, source_target_pairs={{0,16},{2,18},{4,20},{6,22},{8,24},{10,26},{12,28},{14,30},{16,0},... | collective-permute-start | bytes 393224 | tf_op jit(solution)/shard_map/ppermute | solution.py:18
  78.0 5.1 %collective-permute-done.9.refs_1_ = f32[256,256]{1,0:T(8,128)S(1)} collective-permute-done((f32[256,256]{1,0:T(8,128)S(1)}, f32[256,256]{1,0:T(8,128)S(1)}, u32[]{:S(2)}, u32[]{:S(2)}) %collective-permute-start.9) | collective-permute-done | bytes 262176 | tf_op jit(solution)/shard_map/ppermute | solution.py:18
  84.4 3.7 %collective-permute-done.17.refs_1_ = f32[256,256]{1,0:T(8,128)S(1)} collective-permute-done((f32[256,256]{1,0:T(8,128)S(1)}, f32[256,256]{1,0:T(8,128)S(1)}, u32[]{:S(2)}, u32[]{:S(2)}) %collective-permute-start.17) | collective-permute-done | bytes 262176 | tf_op jit(solution)/shard_map/ppermute | solution.py:18
  88.1 0.7 combine.29.refs_0_
  88.8 3.0 %collective-permute-start.12 = (f32[256,256]{1,0:T(8,128)S(1)}, f32[256,256]{1,0:T(8,128)S(1)}, u32[]{:S(2)}, u32[]{:S(2)}) collective-permute-start(f32[256,256]{1,0:T(8,128)S(1)} %combine.26.refs_0_), channel_id=1, source_target_pairs={{0,16},{2,18},{4,20},{6,22},{8,24},{10,26},{12,28},{14,30},{16,0},... | collective-permute-start | bytes 786440 | tf_op jit(solution)/shard_map/ppermute | solution.py:18
  91.9 1.2 combine.42.refs_6_
  93.1 17.9 %collective-permute-done.30.refs_1_ = f32[128,256]{1,0:T(8,128)S(1)} collective-permute-done((f32[128,256]{1,0:T(8,128)S(1)}, f32[128,256]{1,0:T(8,128)S(1)}, u32[]{:S(2)}, u32[]{:S(2)}) %collective-permute-start.30) | collective-permute-done | bytes 131104 | tf_op jit(solution)/shard_map/ppermute | solution.py:18
  111.0 1.2 combine.43.refs_6_
  112.2 1.2 combine.44.refs_6_
  113.4 1.2 combine.45.refs_6_
  114.6 6.3 %collective-permute-done.18.refs_1_ = f32[256,256]{1,0:T(8,128)S(1)} collective-permute-done((f32[256,256]{1,0:T(8,128)S(1)}, f32[256,256]{1,0:T(8,128)S(1)}, u32[]{:S(2)}, u32[]{:S(2)}) %collective-permute-start.18) | collective-permute-done | bytes 262176 | tf_op jit(solution)/shard_map/ppermute | solution.py:18
  120.9 1.5 %combine.46.refs_6_ = f32[512,1024]{1,0:T(8,128)} custom-call(f32[256,256]{1,0:T(8,128)S(1)} %combine.29.refs_0_, f32[256,256]{1,0:T(8,128)S(1)} %collective-permute-done.18.refs_1_, f32[256,128]{1,0:T(8,128)S(1)} %bitcast.25, f32[256,128]{1,0:T(8,128)S(1)} %get-tuple-element.34.refs_3_, ...), custom_call_target="tpu_custom_call", output_to_operand_aliasing={{}: (6, {})} | custom-call | flops 301989888 | bytes 524288 | tf_op jit(solution)/shard_map/combine/pallas_call | solution.py:172
  122.4 1.5 %combine.47 = f32[512,1024]{1,0:T(8,128)} custom-call(f32[256,256]{1,0:T(8,128)S(1)} %combine.26.refs_0_, f32[256,256]{1,0:T(8,128)S(1)} %collective-permute-done.12.refs_1_, f32[256,128]{1,0:T(8,128)S(1)} %bitcast.26, f32[256,128]{1,0:T(8,128)S(1)} %get-tuple-element.34.refs_3_, ...), custom_call_target="tpu_custom_call", output_to_operand_aliasing={{}: (6, {})} | custom-call | flops 301989888 | bytes 524288 | tf_op jit(solution)/shard_map/combine/pallas_call | solution.py:172
  (65 shorter events, 14.1 us)
Async XLA Ops:
  0.0 15.2 %collective-permute-start = (f32[512,128]{1,0:T(8,128)}, f32[512,128]{1,0:T(8,128)S(1)}, u32[]{:S(2)}, u32[]{:S(2)}) collective-permute-start(f32[512,128]{1,0:T(8,128)} %refs_1_.11), channel_id=1, source_target_pairs={{1,0},{0,1},{3,2},{2,3},{5,4},{4,5},{7,6},{6,7},{9,8},{8,9},{11,10... | collective-permute-start | bytes 786440 | tf_op jit(solution)/shard_map/ppermute | solution.py:24
  3.0 10.2 %collective-permute-start.1 = (f32[256,128]{1,0:T(8,128)}, f32[256,128]{1,0:T(8,128)S(1)}, u32[]{:S(2)}, u32[]{:S(2)}) collective-permute-start(f32[256,128]{1,0:T(8,128)} %refs_3_.11), channel_id=1, source_target_pairs={{1,0},{0,1},{3,2},{2,3},{5,4},{4,5},{7,6},{6,7},{9,8},{8,9},{11,10... | collective-permute-start | bytes 393224 | tf_op jit(solution)/shard_map/ppermute | solution.py:24
  4.3 10.9 %collective-permute-start.3 = (f32[256,128]{1,0:T(8,128)S(1)}, f32[256,128]{1,0:T(8,128)S(1)}, u32[]{:S(2)}, u32[]{:S(2)}) collective-permute-start(f32[256,128]{1,0:T(8,128)S(1)} %get-tuple-element.31.refs_2_), channel_id=1, source_target_pairs={{1,0},{0,1},{3,2},{2,3},{5,4},{4,5},{7,6},{6,7},{9,8},{8,9},{11,10... | collective-permute-start | bytes 393224 | tf_op jit(solution)/shard_map/ppermute | solution.py:24
  6.4 22.6 %collective-permute-start.4 = (f32[256,128]{1,0:T(8,128)S(1)}, f32[256,128]{1,0:T(8,128)S(1)}, u32[]{:S(2)}, u32[]{:S(2)}) collective-permute-start(f32[256,128]{1,0:T(8,128)S(1)} %get-tuple-element.31.refs_2_), channel_id=1, source_target_pairs={{0,2},{2,0},{4,6},{6,4},{8,10},{10,8},{12,14},{14,12},{16,18},{18,... | collective-permute-start | bytes 393224 | tf_op jit(solution)/shard_map/ppermute | solution.py:18
  6.4 22.6 %collective-permute-start.7 = (f32[256,128]{1,0:T(8,128)S(1)}, f32[256,128]{1,0:T(8,128)S(1)}, u32[]{:S(2)}, u32[]{:S(2)}) collective-permute-start(f32[256,128]{1,0:T(8,128)S(1)} %bitcast.34), channel_id=1, source_target_pairs={{0,4},{2,6},{4,0},{6,2},{8,12},{10,14},{12,8},{14,10},{16,20},{18,... | collective-permute-start | bytes 393224 | tf_op jit(solution)/shard_map/ppermute | solution.py:18
  13.1 16.4 %collective-permute-start.10 = (f32[256,128]{1,0:T(8,128)S(1)}, f32[256,128]{1,0:T(8,128)S(1)}, u32[]{:S(2)}, u32[]{:S(2)}) collective-permute-start(f32[256,128]{1,0:T(8,128)S(1)} %bitcast.27), channel_id=1, source_target_pairs={{0,8},{2,10},{4,12},{6,14},{8,0},{10,2},{12,4},{14,6},{16,24},{18,... | collective-permute-start | bytes 393224 | tf_op jit(solution)/shard_map/ppermute | solution.py:18
  15.2 14.4 %collective-permute-start.5 = (f32[256,128]{1,0:T(8,128)S(1)}, f32[256,128]{1,0:T(8,128)S(1)}, u32[]{:S(2)}, u32[]{:S(2)}) collective-permute-start(f32[256,128]{1,0:T(8,128)S(1)} %collective-permute-done.3.refs_3_), channel_id=1, source_target_pairs={{0,2},{2,0},{4,6},{6,4},{8,10},{10,8},{12,14},{14,12},{16,18},{18,... | collective-permute-start | bytes 393224 | tf_op jit(solution)/shard_map/ppermute | solution.py:18
  15.2 1.6 %copy-start = (f32[512,1024]{1,0:T(8,128)S(1)}, f32[512,1024]{1,0:T(8,128)}, u32[]{:S(2)}) copy-start(f32[512,1024]{1,0:T(8,128)} %refs_0_.11) | copy-start | bytes 6291460
  16.8 0.9 copy-start.1
  17.8 0.9 copy-start.2
  24.9 5.1 %collective-permute-start.19 = (f32[128,256]{1,0:T(8,128)S(1)}, f32[128,256]{1,0:T(8,128)S(1)}, u32[]{:S(2)}, u32[]{:S(2)}) collective-permute-start(f32[128,256]{1,0:T(8,128)S(1)} %get-tuple-element.24.refs_0_), channel_id=1, source_target_pairs={{0,2},{2,0},{4,6},{6,4},{8,10},{10,8},{12,14},{14,12},{16,18},{18,... | collective-permute-start | bytes 393224 | tf_op jit(solution)/shard_map/ppermute | solution.py:18
  29.0 8.5 %collective-permute-start.2 = (f32[256,256]{1,0:T(8,128)S(1)}, f32[256,256]{1,0:T(8,128)S(1)}, u32[]{:S(2)}, u32[]{:S(2)}) collective-permute-start(f32[256,256]{1,0:T(8,128)S(1)} %get-tuple-element.22.refs_0_), channel_id=1, source_target_pairs={{0,2},{2,0},{4,6},{6,4},{8,10},{10,8},{12,14},{14,12},{16,18},{18,... | collective-permute-start | bytes 786440 | tf_op jit(solution)/shard_map/ppermute | solution.py:18
  29.0 1.7 %collective-permute-start.31 = (f32[128,256]{1,0:T(8,128)S(1)}, f32[128,256]{1,0:T(8,128)S(1)}, u32[]{:S(2)}, u32[]{:S(2)}) collective-permute-start(f32[128,256]{1,0:T(8,128)S(1)} %get-tuple-element.27.refs_0_), channel_id=1, source_target_pairs={{0,2},{2,0},{4,6},{6,4},{8,10},{10,8},{12,14},{14,12},{16,18},{18,... | collective-permute-start | bytes 393224 | tf_op jit(solution)/shard_map/ppermute | solution.py:18
  29.5 10.1 %collective-permute-start.15 = (f32[256,256]{1,0:T(8,128)S(1)}, f32[256,256]{1,0:T(8,128)S(1)}, u32[]{:S(2)}, u32[]{:S(2)}) collective-permute-start(f32[256,256]{1,0:T(8,128)S(1)} %get-tuple-element.23.refs_0_), channel_id=1, source_target_pairs={{0,2},{2,0},{4,6},{6,4},{8,10},{10,8},{12,14},{14,12},{16,18},{18,... | collective-permute-start | bytes 786440 | tf_op jit(solution)/shard_map/ppermute | solution.py:18
  29.6 3.7 %collective-permute-start.23 = (f32[128,256]{1,0:T(8,128)S(1)}, f32[128,256]{1,0:T(8,128)S(1)}, u32[]{:S(2)}, u32[]{:S(2)}) collective-permute-start(f32[128,256]{1,0:T(8,128)S(1)} %get-tuple-element.25.refs_0_), channel_id=1, source_target_pairs={{0,2},{2,0},{4,6},{6,4},{8,10},{10,8},{12,14},{14,12},{16,18},{18,... | collective-permute-start | bytes 393224 | tf_op jit(solution)/shard_map/ppermute | solution.py:18
  30.1 5.9 %collective-permute-start.27 = (f32[128,256]{1,0:T(8,128)S(1)}, f32[128,256]{1,0:T(8,128)S(1)}, u32[]{:S(2)}, u32[]{:S(2)}) collective-permute-start(f32[128,256]{1,0:T(8,128)S(1)} %get-tuple-element.26.refs_0_), channel_id=1, source_target_pairs={{0,2},{2,0},{4,6},{6,4},{8,10},{10,8},{12,14},{14,12},{16,18},{18,... | collective-permute-start | bytes 393224 | tf_op jit(solution)/shard_map/ppermute | solution.py:18
  30.8 13.7 %collective-permute-start.8 = (f32[2,256,128]{2,1,0:T(8,128)S(1)}, f32[2,256,128]{2,1,0:T(8,128)S(1)}, u32[]{:S(2)}, u32[]{:S(2)}) collective-permute-start(f32[2,256,128]{2,1,0:T(8,128)S(1)} %pad_maximum_fusion), channel_id=1, source_target_pairs={{1,0},{0,1},{3,2},{2,3},{5,4},{4,5},{7,6},{6,7},{9,8},{8,9},{11,10... | collective-permute-start | bytes 786440 | tf_op jit(solution)/shard_map/ppermute | solution.py:24
  33.3 9.6 %collective-permute-start.13 = (f32[256,128]{1,0:T(8,128)S(1)}, f32[256,128]{1,0:T(8,128)S(1)}, u32[]{:S(2)}, u32[]{:S(2)}) collective-permute-start(f32[256,128]{1,0:T(8,128)S(1)} %bitcast.20), channel_id=1, source_target_pairs={{0,16},{2,18},{4,20},{6,22},{8,24},{10,26},{12,28},{14,30},{16,0},... | collective-permute-start | bytes 393224 | tf_op jit(solution)/shard_map/ppermute | solution.py:18
  36.0 9.0 %collective-permute-start.20 = (f32[128,256]{1,0:T(8,128)S(1)}, f32[128,256]{1,0:T(8,128)S(1)}, u32[]{:S(2)}, u32[]{:S(2)}) collective-permute-start(f32[128,256]{1,0:T(8,128)S(1)} %combine.30.refs_0_), channel_id=1, source_target_pairs={{0,4},{2,6},{4,0},{6,2},{8,12},{10,14},{12,8},{14,10},{16,20},{18,... | collective-permute-start | bytes 393224 | tf_op jit(solution)/shard_map/ppermute | solution.py:18
  37.5 9.0 %collective-permute-start.32 = (f32[128,256]{1,0:T(8,128)S(1)}, f32[128,256]{1,0:T(8,128)S(1)}, u32[]{:S(2)}, u32[]{:S(2)}) collective-permute-start(f32[128,256]{1,0:T(8,128)S(1)} %combine.39.refs_0_), channel_id=1, source_target_pairs={{0,4},{2,6},{4,0},{6,2},{8,12},{10,14},{12,8},{14,10},{16,20},{18,... | collective-permute-start | bytes 393224 | tf_op jit(solution)/shard_map/ppermute | solution.py:18
  39.7 24.3 %collective-permute-start.11 = (f32[2,256,128]{2,1,0:T(8,128)S(1)}, f32[2,256,128]{2,1,0:T(8,128)S(1)}, u32[]{:S(2)}, u32[]{:S(2)}) collective-permute-start(f32[2,256,128]{2,1,0:T(8,128)S(1)} %pad_maximum_fusion.1), channel_id=1, source_target_pairs={{1,0},{0,1},{3,2},{2,3},{5,4},{4,5},{7,6},{6,7},{9,8},{8,9},{11,10... | collective-permute-start | bytes 786440 | tf_op jit(solution)/shard_map/ppermute | solution.py:24
  42.9 6.4 %collective-permute-start.24 = (f32[128,256]{1,0:T(8,128)S(1)}, f32[128,256]{1,0:T(8,128)S(1)}, u32[]{:S(2)}, u32[]{:S(2)}) collective-permute-start(f32[128,256]{1,0:T(8,128)S(1)} %combine.33.refs_0_), channel_id=1, source_target_pairs={{0,4},{2,6},{4,0},{6,2},{8,12},{10,14},{12,8},{14,10},{16,20},{18,... | collective-permute-start | bytes 393224 | tf_op jit(solution)/shard_map/ppermute | solution.py:18
  44.4 7.7 %collective-permute-start.28 = (f32[128,256]{1,0:T(8,128)S(1)}, f32[128,256]{1,0:T(8,128)S(1)}, u32[]{:S(2)}, u32[]{:S(2)}) collective-permute-start(f32[128,256]{1,0:T(8,128)S(1)} %combine.36.refs_0_), channel_id=1, source_target_pairs={{0,4},{2,6},{4,0},{6,2},{8,12},{10,14},{12,8},{14,10},{16,20},{18,... | collective-permute-start | bytes 393224 | tf_op jit(solution)/shard_map/ppermute | solution.py:18
  45.0 12.8 %collective-permute-start.6 = (f32[256,256]{1,0:T(8,128)S(1)}, f32[256,256]{1,0:T(8,128)S(1)}, u32[]{:S(2)}, u32[]{:S(2)}) collective-permute-start(f32[256,256]{1,0:T(8,128)S(1)} %combine.24.refs_0_), channel_id=1, source_target_pairs={{0,4},{2,6},{4,0},{6,2},{8,12},{10,14},{12,8},{14,10},{16,20},{18,... | collective-permute-start | bytes 786440 | tf_op jit(solution)/shard_map/ppermute | solution.py:18
  46.5 15.6 %collective-permute-start.16 = (f32[256,256]{1,0:T(8,128)S(1)}, f32[256,256]{1,0:T(8,128)S(1)}, u32[]{:S(2)}, u32[]{:S(2)}) collective-permute-start(f32[256,256]{1,0:T(8,128)S(1)} %combine.27.refs_0_), channel_id=1, source_target_pairs={{0,4},{2,6},{4,0},{6,2},{8,12},{10,14},{12,8},{14,10},{16,20},{18,... | collective-permute-start | bytes 786440 | tf_op jit(solution)/shard_map/ppermute | solution.py:18
  49.4 15.6 %collective-permute-start.21 = (f32[128,256]{1,0:T(8,128)S(1)}, f32[128,256]{1,0:T(8,128)S(1)}, u32[]{:S(2)}, u32[]{:S(2)}) collective-permute-start(f32[128,256]{1,0:T(8,128)S(1)} %combine.31.refs_0_), channel_id=1, source_target_pairs={{0,8},{2,10},{4,12},{6,14},{8,0},{10,2},{12,4},{14,6},{16,24},{18,... | collective-permute-start | bytes 393224 | tf_op jit(solution)/shard_map/ppermute | solution.py:18
  52.2 13.9 %collective-permute-start.33 = (f32[128,256]{1,0:T(8,128)S(1)}, f32[128,256]{1,0:T(8,128)S(1)}, u32[]{:S(2)}, u32[]{:S(2)}) collective-permute-start(f32[128,256]{1,0:T(8,128)S(1)} %combine.40.refs_0_), channel_id=1, source_target_pairs={{0,8},{2,10},{4,12},{6,14},{8,0},{10,2},{12,4},{14,6},{16,24},{18,... | collective-permute-start | bytes 393224 | tf_op jit(solution)/shard_map/ppermute | solution.py:18
  57.8 31.0 %collective-permute-start.14 = (f32[2,256,128]{2,1,0:T(8,128)S(1)}, f32[2,256,128]{2,1,0:T(8,128)S(1)}, u32[]{:S(2)}, u32[]{:S(2)}) collective-permute-start(f32[2,256,128]{2,1,0:T(8,128)S(1)} %pad_maximum_fusion.2), channel_id=1, source_target_pairs={{1,0},{0,1},{3,2},{2,3},{5,4},{4,5},{7,6},{6,7},{9,8},{8,9},{11,10... | collective-permute-start | bytes 786440 | tf_op jit(solution)/shard_map/ppermute | solution.py:24
  62.0 6.4 %collective-permute-start.25 = (f32[128,256]{1,0:T(8,128)S(1)}, f32[128,256]{1,0:T(8,128)S(1)}, u32[]{:S(2)}, u32[]{:S(2)}) collective-permute-start(f32[128,256]{1,0:T(8,128)S(1)} %combine.34.refs_0_), channel_id=1, source_target_pairs={{0,8},{2,10},{4,12},{6,14},{8,0},{10,2},{12,4},{14,6},{16,24},{18,... | collective-permute-start | bytes 393224 | tf_op jit(solution)/shard_map/ppermute | solution.py:18
  64.0 8.6 %collective-permute-start.29 = (f32[128,256]{1,0:T(8,128)S(1)}, f32[128,256]{1,0:T(8,128)S(1)}, u32[]{:S(2)}, u32[]{:S(2)}) collective-permute-start(f32[128,256]{1,0:T(8,128)S(1)} %combine.37.refs_0_), channel_id=1, source_target_pairs={{0,8},{2,10},{4,12},{6,14},{8,0},{10,2},{12,4},{14,6},{16,24},{18,... | collective-permute-start | bytes 393224 | tf_op jit(solution)/shard_map/ppermute | solution.py:18
  65.0 18.1 %collective-permute-start.9 = (f32[256,256]{1,0:T(8,128)S(1)}, f32[256,256]{1,0:T(8,128)S(1)}, u32[]{:S(2)}, u32[]{:S(2)}) collective-permute-start(f32[256,256]{1,0:T(8,128)S(1)} %combine.25.refs_0_), channel_id=1, source_target_pairs={{0,8},{2,10},{4,12},{6,14},{8,0},{10,2},{12,4},{14,6},{16,24},{18,... | collective-permute-start | bytes 786440 | tf_op jit(solution)/shard_map/ppermute | solution.py:18
  66.1 22.0 %collective-permute-start.17 = (f32[256,256]{1,0:T(8,128)S(1)}, f32[256,256]{1,0:T(8,128)S(1)}, u32[]{:S(2)}, u32[]{:S(2)}) collective-permute-start(f32[256,256]{1,0:T(8,128)S(1)} %combine.28.refs_0_), channel_id=1, source_target_pairs={{0,8},{2,10},{4,12},{6,14},{8,0},{10,2},{12,4},{14,6},{16,24},{18,... | collective-permute-start | bytes 786440 | tf_op jit(solution)/shard_map/ppermute | solution.py:18
  68.4 23.4 %collective-permute-start.34 = (f32[128,256]{1,0:T(8,128)S(1)}, f32[128,256]{1,0:T(8,128)S(1)}, u32[]{:S(2)}, u32[]{:S(2)}) collective-permute-start(f32[128,256]{1,0:T(8,128)S(1)} %combine.41.refs_0_), channel_id=1, source_target_pairs={{0,16},{2,18},{4,20},{6,22},{8,24},{10,26},{12,28},{14,30},{16,0},... | collective-permute-start | bytes 393224 | tf_op jit(solution)/shard_map/ppermute | solution.py:18
  72.6 40.8 %collective-permute-start.22 = (f32[128,256]{1,0:T(8,128)S(1)}, f32[128,256]{1,0:T(8,128)S(1)}, u32[]{:S(2)}, u32[]{:S(2)}) collective-permute-start(f32[128,256]{1,0:T(8,128)S(1)} %combine.32.refs_0_), channel_id=1, source_target_pairs={{0,16},{2,18},{4,20},{6,22},{8,24},{10,26},{12,28},{14,30},{16,0},... | collective-permute-start | bytes 393224 | tf_op jit(solution)/shard_map/ppermute | solution.py:18
  83.1 29.1 %collective-permute-start.26 = (f32[128,256]{1,0:T(8,128)S(1)}, f32[128,256]{1,0:T(8,128)S(1)}, u32[]{:S(2)}, u32[]{:S(2)}) collective-permute-start(f32[128,256]{1,0:T(8,128)S(1)} %combine.35.refs_0_), channel_id=1, source_target_pairs={{0,16},{2,18},{4,20},{6,22},{8,24},{10,26},{12,28},{14,30},{16,0},... | collective-permute-start | bytes 393224 | tf_op jit(solution)/shard_map/ppermute | solution.py:18
  88.1 22.9 %collective-permute-start.30 = (f32[128,256]{1,0:T(8,128)S(1)}, f32[128,256]{1,0:T(8,128)S(1)}, u32[]{:S(2)}, u32[]{:S(2)}) collective-permute-start(f32[128,256]{1,0:T(8,128)S(1)} %combine.38.refs_0_), channel_id=1, source_target_pairs={{0,16},{2,18},{4,20},{6,22},{8,24},{10,26},{12,28},{14,30},{16,0},... | collective-permute-start | bytes 393224 | tf_op jit(solution)/shard_map/ppermute | solution.py:18
  88.8 33.6 %collective-permute-start.12 = (f32[256,256]{1,0:T(8,128)S(1)}, f32[256,256]{1,0:T(8,128)S(1)}, u32[]{:S(2)}, u32[]{:S(2)}) collective-permute-start(f32[256,256]{1,0:T(8,128)S(1)} %combine.26.refs_0_), channel_id=1, source_target_pairs={{0,16},{2,18},{4,20},{6,22},{8,24},{10,26},{12,28},{14,30},{16,0},... | collective-permute-start | bytes 786440 | tf_op jit(solution)/shard_map/ppermute | solution.py:18
  91.8 29.1 %collective-permute-start.18 = (f32[256,256]{1,0:T(8,128)S(1)}, f32[256,256]{1,0:T(8,128)S(1)}, u32[]{:S(2)}, u32[]{:S(2)}) collective-permute-start(f32[256,256]{1,0:T(8,128)S(1)} %combine.29.refs_0_), channel_id=1, source_target_pairs={{0,16},{2,18},{4,20},{6,22},{8,24},{10,26},{12,28},{14,30},{16,0},... | collective-permute-start | bytes 786440 | tf_op jit(solution)/shard_map/ppermute | solution.py:18

commit v2 on v0

v2 whole, which is shorter than its diff:
```python
import functools

import jax
import jax.numpy as jnp
from jax import lax
from jax.experimental import pallas as pl
from jax.experimental.pallas import tpu as pltpu
from jax.sharding import PartitionSpec as P

f32 = jnp.float32
bf16 = jnp.bfloat16
LANES = 128
VMEM_LIMIT = 32 * 2**20
MICROSECOND = 3.69e6
SCALE = 10.0
USUAL = dict(
    pick=1.1,
    inner=1.0,
    later=2.4,
    first=0.6,
    tops=1.0,
    stack=0.1,
    node=0.15,
    combine=0.6,
    rest=1.7,
    finish=1.3,
)


def swapped(value, axis, apart):
    mask = 2**apart
    pairs = [(source, source ^ mask) for source in range(lax.axis_size(axis))]
    return lax.ppermute(value, axis, pairs)


def turned(value, axis):
    size = lax.axis_size(axis)
    return [
        lax.ppermute(value, axis, [((to + step) % size, to) for to in range(size)])
        for step in range(1, size)
    ]


def col_blocks(value):
    if value.shape[-1] % LANES == 0:
        return [value] + turned(value, "col")
    return [lax.all_gather(value, "col", axis=value.ndim - 1, tiled=True)]


def whole(blocks):
    if len(blocks) == 1:
        return blocks[0]
    size = len(blocks)
    me = lax.axis_index("col")
    ordered = []
    for at in range(size):
        block = blocks[0]
        for step in range(1, size):
            block = jnp.where((me + step) % size == at, blocks[step], block)
        ordered.append(block)
    return jnp.concatenate(ordered, axis=1)


def triangle(factor):
    row = lax.broadcasted_iota(jnp.int32, factor.shape, 0)
    column = lax.broadcasted_iota(jnp.int32, factor.shape, 1)
    kept = jnp.where(row <= column, factor, 0.0)
    return kept + jnp.where(row == column, 0.5, 0.0)


def parts(value):
    high = value.astype(bf16)
    return high, (value - high.astype(f32)).astype(bf16)


def put(refs, value, at=...):
    for ref, part in zip(refs, parts(value)):
        ref[at] = part


def product(left, right, over):
    def dot(a, b):
        return lax.dot_general(a, b, (over, ((), ())), preferred_element_type=f32)

    return dot(left[0], right[0]) + (dot(left[0], right[1]) + dot(left[1], right[0]))


plain = ((1,), (0,))
across = ((1,), (1,))


class Line:
    def __init__(self):
        self.token = None

    def __call__(self, body, name, inputs, outputs, grid=(1,), alias=None, scratch=()):
        operands, in_specs = [], []
        for value in inputs:
            if isinstance(value, tuple):
                operands.append(value[0])
                in_specs.append(value[1])
            else:
                operands.append(pltpu.with_memory_space_constraint(value, pltpu.VMEM))
                in_specs.append(pl.BlockSpec(memory_space=pltpu.VMEM))
        n_in = len(operands)
        if self.token is not None:
            operands.append(pltpu.with_memory_space_constraint(self.token, pltpu.VMEM))
            in_specs.append(pl.BlockSpec(memory_space=pltpu.VMEM))
        aliases = {}
        if alias is not None:
            aliases = {len(operands): alias[1]}
            operands.append(alias[0])
            in_specs.append(pl.BlockSpec(memory_space=pl.ANY))
        out_shape, out_specs = [], []
        for shape, spec in outputs:
            out_shape.append(shape)
            out_specs.append(spec)
        out_shape.append(pltpu.VMEM((8, LANES), f32))
        out_specs.append(pl.BlockSpec(memory_space=pltpu.VMEM))
        n_all = len(operands)
        at_token = n_all + len(outputs)

        def kernel(*refs):
            refs[at_token][...] = jnp.zeros((8, LANES), f32)
            body(refs[:n_in], refs[n_all:at_token] + refs[at_token + 1 :])

        *results, self.token = pl.pallas_call(
            kernel,
            grid=grid,
            out_shape=out_shape,
            in_specs=in_specs,
            out_specs=out_specs,
            scratch_shapes=scratch,
            input_output_aliases=aliases,
            compiler_params=pltpu.CompilerParams(vmem_limit_bytes=VMEM_LIMIT),
            cost_estimate=pl.CostEstimate(
                flops=int(SCALE * 312 * MICROSECOND * USUAL[name]), bytes_accessed=int(SCALE * MICROSECOND * USUAL[name]), transcendentals=0
            ),
            name=name,
        )(*operands)
        return results


def in_hbm(value):
    return pltpu.with_memory_space_constraint(value, pltpu.HBM)


def held(*shape, dtype=f32):
    return pltpu.VMEM(shape, dtype), pl.BlockSpec(memory_space=pltpu.VMEM)


def held_parts(*shape):
    return [held(*shape, dtype=bf16)] * 2


def pick_body(levels, ins, outs):
    leaf, reflect, factor, sems = ins[0], ins[1], ins[2], outs[levels]
    size = leaf.shape[0]
    position = lax.axis_index("row")
    targets = [outs[0].at[pl.ds(size, size)]] + list(outs[1:levels])
    pltpu.make_async_copy(leaf, outs[0].at[pl.ds(0, size)], sems.at[levels]).start()
    for s in range(levels):
        clear = position // (1 << s) % 2 == 0

        @pl.when(clear)
        def _(s=s):
            pltpu.make_async_copy(factor.at[s], targets[s], sems.at[s]).start()

        @pl.when(jnp.logical_not(clear))
        def _(s=s):
            pltpu.make_async_copy(reflect.at[s], targets[s], sems.at[s]).start()

    for s in range(levels):
        pltpu.make_async_copy(factor.at[s], targets[s], sems.at[s]).wait()
    pltpu.make_async_copy(leaf, outs[0].at[pl.ds(0, size)], sems.at[levels]).wait()


def inner_body(n, ins, outs):
    trailing = ins[n]
    full = whole([ref[...] for ref in ins[:n]])
    put(outs[:2], full)
    turned_parts = parts(full.T)
    for ref, part in zip(outs[2:4], turned_parts):
        ref[...] = part
    width = outs[4].shape[1]
    put(outs[4:6], product(turned_parts, parts(trailing[:, :width]), plain))


def later_body(start, ins, outs):
    trailing = ins[2][:, start:]
    put(outs[:2], product((ins[0][...], ins[1][...]), parts(trailing), plain))


def first_body(n, ins, outs):
    size = outs[0].shape[1]
    given = ins[5 : 5 + n]
    put(outs[3:5], triangle(whole([ref[:size] for ref in given])).T)
    outs[5][...] = whole([ref[size:] for ref in given])
    tops_body(0, 0, list(ins[:5]) + list(outs[3:5]), outs[:3])
    for i, out in enumerate(outs[6:]):
        stack(out, ins[5 + n + 2 * i : 7 + n + 2 * i])


def tops_body(start, inner_start, ins, outs):
    inn_h, inn_l, vec_h, vec_l, trailing, tri_h, tri_l = ins[:7]
    width, size = outs[0].shape
    at = slice(inner_start, inner_start + width)
    scaled = parts(product((tri_h[...], tri_l[...]), (inn_h[:, at], inn_l[:, at]), plain))
    outs[1][...] = scaled[0]
    outs[2][...] = scaled[1]
    taken = product((vec_h[:size], vec_l[:size]), scaled, plain)
    outs[0][...] = (trailing[:size, start : start + width] - taken).T
    for i, out in enumerate(outs[3:]):
        stack(out, ins[7 + 2 * i : 9 + 2 * i])


def rest_body(ins, outs):
    trailing, vec_h, vec_l = ins[:3]
    size = vec_h.shape[1]
    pieces = ins[3:]
    start = 0
    for high, low in zip(pieces[::2], pieces[1::2]):
        width = high.shape[1]
        at = slice(start, start + width)
        taken = product((vec_h[size:], vec_l[size:]), (high[...], low[...]), plain)
        outs[0][:, at] = trailing[size:, at] - taken
        start += width


def stack(out, ins):
    size = ins[0].shape[0]
    for i, ref in enumerate(ins):
        out[i * size : (i + 1) * size] = ref[...]


def node_body(section, n, ins, outs):
    clear = lax.axis_index("row") // (1 << section) % 2 == 0
    if section:
        size = ins[0].shape[0] // 2
        own = whole([ref[:size] for ref in ins[:n]])
        partner = whole([ref[size:] for ref in ins[:n]])
    else:
        own, partner = ins[0][...], ins[1][...]
    put(outs[:2], jnp.where(clear, partner, own))
    put(outs[2:4], triangle(jnp.where(clear, own, partner)))
    for ref, value in zip(outs[4:], ins[n:]):
        ref[...] = value[...]


def combine_body(section, last, mine_at, other_at, ins, outs):
    width = outs[0].shape[1 if last else 0]
    mine, other = ins[0][mine_at : mine_at + width], ins[1][other_at : other_at + width]
    node_y = ins[2][...], ins[3][...]
    node_t = ins[4][...], ins[5][...]
    clear = lax.axis_index("row") // (1 << section) % 2 == 0
    leader = jnp.where(clear, mine, other)
    follower = jnp.where(clear, other, mine)
    summed = leader + product(parts(follower), node_y, plain)
    coupling = product(parts(summed), node_t, plain)

    def write(value):
        outs[0][...] = value.T if last else value

    @pl.when(clear)
    def _():
        write(mine - coupling)

    @pl.when(jnp.logical_not(clear))
    def _():
        write(mine - product(parts(coupling), node_y, across))


def widths_of(columns):
    if columns % LANES:
        return [columns]
    units = columns // LANES
    short = min(units, 2 + units % 2)
    doubles = (units - short) // 2
    return [LANES] + [2 * LANES] * doubles + [LANES] * (short - 1)


def groups_of(widths):
    chunks = list(range(len(widths)))
    return [group for group in (chunks[:1], chunks[1:2], chunks[2:]) if group]


def order_of(chunks, levels):
    order = [(s, c) for s in range(levels) for c in range(chunks)]
    return sorted(order, key=lambda at: (sum(at), at[0]))


def per_device(trailing, reflectors, leaf_factor, node_reflect, node_factor):
    line = Line()
    rows, columns = trailing.shape
    size, piece = leaf_factor.shape
    levels = node_factor.shape[0]
    widths = widths_of(columns)
    starts = [sum(widths[:c]) for c in range(len(widths))]
    groups = groups_of(widths)
    early = sum(widths[c] for group in groups[:2] for c in group)
    copied = pl.BlockSpec(memory_space=pltpu.VMEM)
    far_away = pl.BlockSpec(memory_space=pl.ANY)

    vectors = col_blocks(reflectors)
    n = len(vectors)
    zeroth, *pieces = line(
        functools.partial(pick_body, levels),
        "pick",
        [(in_hbm(x), far_away) for x in (leaf_factor, node_reflect, node_factor)],
        [held(2 * size, piece)] + [held(size, piece)] * (levels - 1),
        scratch=[pltpu.SemaphoreType.DMA((levels + 1,))],
    )
    pieces = [None] + pieces
    zeroth = col_blocks(zeroth)
    far = [None] + [swapped(pieces[s], "row", s) for s in range(1, levels)]

    def stacked(*sections):
        given, made = [], []
        for s in sections:
            if s < levels:
                given += [pieces[s], far[s]]
                made.append(held(2 * size, piece))
        return given, made

    vec_h, vec_l, vect_h, vect_l, inn_h, inn_l = line(
        functools.partial(inner_body, n),
        "inner",
        [(vectors[0], copied)] + vectors[1:] + [trailing],
        held_parts(rows, size) + held_parts(size, rows) + held_parts(size, early),
    )
    sources = [(inn_h, inn_l)] * 2
    if columns > early:
        sources.append(
            line(
                functools.partial(later_body, early),
                "later",
                [vect_h, vect_l, trailing],
                held_parts(size, columns - early),
            )
        )
    given, made = stacked(1, 2)
    top, high, low, tri_h, tri_l, own, *stacks = line(
        functools.partial(first_body, n),
        "first",
        list(sources[0]) + [vec_h, vec_l, trailing] + zeroth + given,
        [held(widths[0], size)]
        + held_parts(size, widths[0])
        + held_parts(size, size)
        + [held(size, size)]
        + made,
    )
    stacks = [None] + stacks
    other = swapped(top, "row", 0)
    partner = swapped(own, "row", 0)
    tops, others, scaled = {0: (top, 0)}, {0: (other, 0)}, [high, low]
    nodes = [None] * levels
    out = None

    def tops_of(g):
        group = groups[g]
        start, width = starts[group[0]], sum(widths[c] for c in group)
        given, made = stacked(*range(3, levels)) if g == 1 else ([], [])
        top, high, low, *more = line(
            functools.partial(tops_body, start, start if g < 2 else 0),
            "tops",
            list(sources[g]) + [vec_h, vec_l, trailing, tri_h, tri_l] + given,
            [held(width, size)] + held_parts(size, width) + made,
        )
        stacks.extend(more)
        scaled.extend([high, low])
        other = swapped(top, "row", 0)
        for c in group:
            tops[c] = top, starts[c] - start
            others[c] = other, starts[c] - start

    if len(groups) > 1:
        tops_of(1)
    for s in range(len(stacks), levels):
        given, made = stacked(s)
        stacks += line(lambda ins, outs: stack(outs[0], ins), "stack", given, made)

    def node_of(s):
        inputs = col_blocks(stacks[s]) if s else [own, partner]
        held_back = [t for t in range(2, levels) if s == (0 if t == 2 else t - 1)]
        *nodes[s], = line(
            functools.partial(node_body, s, len(inputs)),
            "node",
            inputs + [stacks[t] for t in held_back],
            held_parts(size, size) * 2 + [held(2 * size, piece)] * len(held_back),
        )
        for t in held_back:
            stacks[t] = nodes[s].pop()

    for s, c in order_of(len(widths), levels):
        if (s, c) == (1, 0) and len(groups) > 2:
            tops_of(2)
        if nodes[s] is None:
            node_of(s)
        mine, mine_at = tops[c]
        other, other_at = others[c]
        inputs = [mine, other] + nodes[s]
        last = s == levels - 1
        body = functools.partial(combine_body, s, last, mine_at, other_at)
        if not last:
            (top,) = line(body, "combine", inputs, [held(widths[c], size)])
            tops[c] = top, 0
            others[c] = swapped(top, "row", s + 1), 0
        else:
            if out is None:
                (out,) = line(
                    rest_body,
                    "rest",
                    [trailing, vec_h, vec_l] + scaled,
                    [
                        (
                            jax.ShapeDtypeStruct((rows, columns), f32),
                            pl.BlockSpec((rows - size, columns), lambda i: (1, 0)),
                        )
                    ],
                )
            block = pl.BlockSpec((size, LANES), lambda i, at=starts[c] // LANES: (0, at))
            if widths[c] != LANES:
                block = pl.BlockSpec(
                    (pl.Element(size), pl.Element(widths[c])), lambda i, at=starts[c]: (0, at)
                )
            (out,) = line(
                body,
                "finish",
                inputs,
                [(jax.ShapeDtypeStruct((rows, columns), f32), block)],
                alias=(out, 0),
            )
    return out


def solution(mesh):
    in_specs = (
        P("row", "col"),
        P("row", "col"),
        P("row", "col"),
        P(None, "row", "col"),
        P(None, "row", "col"),
    )
    out_specs = P("row", "col")
    return jax.shard_map(
        per_device, mesh=mesh, in_specs=in_specs, out_specs=out_specs, check_vma=False
    )
```

time: 205 us -> 88.6 us (0.43)
  waiting for transfers between devices: 139 us -> 26.3 us
  starting transfers between devices: 7.29 us -> 39.1 us
  Pallas kernels: 0 us -> 22.7 us
  blocking collectives: 20.2 us -> 0 us
  matrix products: 20 us -> 0 us
  between operations: 13.6 us -> 0.28 us
  other arithmetic: 3.16 us -> 0 us
  local copies, waits for them, and re-layouts: 2.08 us -> 0.01 us
    ppermute x8 -> x22, waiting for transfers between devices: 113 us -> 22.6 us  [swapped(): return lax.ppermute(value, axis, pairs)]
    ppermute x8 -> x22, starting transfers between devices: 7.25 us -> 33.8 us  [swapped(): return lax.ppermute(value, axis, pairs)]
    all_gather x2 -> x0, waiting for transfers between devices: 23.9 us -> none  [the longest x1 23.9 us: per_device(): lax.all_gather(node_factor, 'col', axis=2, tiled=True)]
    pallas_call x0 -> x31, Pallas kernels: none -> 22.7 us  [__call__(): pl.pallas_call(kernel, grid=grid, out_shape=out_shape, in_specs=in_specs,...]
    all_gather x2 -> x0, blocking collectives: 20.2 us -> none  [the longest x1 12.8 us: per_device(): lax.all_gather(reflectors, 'col', axis=1, tiled=True)]
    dot_general x15 -> x0, matrix products: 20 us -> none  [the longest x4 5.5 us: combine(): jnp.einsum('kb,kc->bc', chosen_y, follower_rows, precision=highest)]
    ppermute x0 -> x5, starting transfers between devices: none -> 5.28 us  [turned(): lax.ppermute(value, axis, [((to + step) % size, to) for to in range(size)])]
    ppermute x0 -> x5, waiting for transfers between devices: none -> 3.79 us  [turned(): lax.ppermute(value, axis, [((to + step) % size, to) for to in range(size)])]
  transfers between devices with their start and end apart: 10 -> 27, of which waited for: 5 -> 10; matrix products, arithmetic and copies ran while one was open for 4% -> 0% of each run, Pallas kernels for 0% -> 24%
where the time goes in v2:
time: 88.6 us; the launch traced here: 88.5 us
  starting transfers between devices  39.1 us (44%)
  waiting for transfers between devices  26.3 us (30%)
  Pallas kernels  22.7 us (26%)
    ppermute x22, starting transfers between devices, swapped(): return lax.ppermute(value, axis, pairs)  33.8 us
    pallas_call x31, Pallas kernels, __call__(): pl.pallas_call(kernel, grid=grid, out_shape=out_shape, in_specs=in_specs,...  22.7 us
    ppermute x22, waiting for transfers between devices, swapped(): return lax.ppermute(value, axis, pairs)  22.6 us
    ppermute x5, starting transfers between devices, turned(): lax.ppermute(value, axis, [((to + step) % size, to) for to in range(size)])  5.28 us
    ppermute x5, waiting for transfers between devices, turned(): lax.ppermute(value, axis, [((to + step) % size, to) for to in range(size)])  3.79 us
  transfers between devices with their start and end apart: 27, of which 10 were waited for; matrix products, arithmetic and copies ran while one was open for 0% of the time, Pallas kernels for 24%

profile of v2, /device:TPU:0, one launch (start us, length us, event | category | flops | bytes accessed | tf_op | source)
XLA Modules:
  0.0 88.5 jit_solution(4153771696419142916)
XLA Ops:
  0.0 3.0 %collective-permute-start = (f32[512,128]{1,0:T(8,128)}, f32[512,128]{1,0:T(8,128)S(1)}, u32[]{:S(2)}, u32[]{:S(2)}) collective-permute-start(f32[512,128]{1,0:T(8,128)} %refs_0_.4), channel_id=1, source_target_pairs={{1,0},{0,1},{3,2},{2,3},{5,4},{4,5},{7,6},{6,7},{9,8},{8,9},{11,10... | collective-permute-start | bytes 786440 | tf_op jit(solution)/shard_map/ppermute | solution.py:39
  3.0 1.2 %pick.1 = (f32[512,128]{1,0:T(8,128)S(1)}, f32[256,128]{1,0:T(8,128)S(1)}, f32[256,128]{1,0:T(8,128)S(1)}, f32[256,128]{1,0:T(8,128)S(1)}, f32[8,128]{1,0:T(8,128)S(1)}) custom-call(f32[256,128]{1,0:T(8,128)} %refs_0_.3, f32[4,256,128]{2,1,0:T(8,128)} %refs_1_.1, f32[4,256,128]{2,1,0:T(8,128)} %refs_2_.3), custom_call_target="tpu_custom_call" | custom-call | flops 12664080384 | bytes 40590000 | tf_op jit(solution)/shard_map/pick/pallas_call | solution.py:127
  4.4 2.0 %collective-permute-start.2 = (f32[256,128]{1,0:T(8,128)S(1)}, f32[256,128]{1,0:T(8,128)S(1)}, u32[]{:S(2)}, u32[]{:S(2)}) collective-permute-start(f32[256,128]{1,0:T(8,128)S(1)} %get-tuple-element.112.refs_7_), channel_id=1, source_target_pairs={{0,4},{2,6},{4,0},{6,2},{8,12},{10,14},{12,8},{14,10},{16,20},{18,... | collective-permute-start | bytes 393224 | tf_op jit(solution)/shard_map/ppermute | solution.py:33
  6.4 1.6 %collective-permute-start.3 = (f32[256,128]{1,0:T(8,128)S(1)}, f32[256,128]{1,0:T(8,128)S(1)}, u32[]{:S(2)}, u32[]{:S(2)}) collective-permute-start(f32[256,128]{1,0:T(8,128)S(1)} %get-tuple-element.113.refs_9_), channel_id=1, source_target_pairs={{0,8},{2,10},{4,12},{6,14},{8,0},{10,2},{12,4},{14,6},{16,24},{18,... | collective-permute-start | bytes 393224 | tf_op jit(solution)/shard_map/ppermute | solution.py:33
  8.0 2.6 %collective-permute-start.4 = (f32[256,128]{1,0:T(8,128)S(1)}, f32[256,128]{1,0:T(8,128)S(1)}, u32[]{:S(2)}, u32[]{:S(2)}) collective-permute-start(f32[256,128]{1,0:T(8,128)S(1)} %get-tuple-element.117.refs_7_), channel_id=1, source_target_pairs={{0,16},{2,18},{4,20},{6,22},{8,24},{10,26},{12,28},{14,30},{16,0},... | collective-permute-start | bytes 393224 | tf_op jit(solution)/shard_map/ppermute | solution.py:33
  10.6 0.7 inner.1
  11.3 0.9 later.1
  12.2 0.9 collective-permute-done.3.refs_10_
  13.1 2.1 %collective-permute-done.1.refs_6_ = f32[512,128]{1,0:T(8,128)S(1)} collective-permute-done((f32[512,128]{1,0:T(8,128)S(1)}, f32[512,128]{1,0:T(8,128)S(1)}, u32[]{:S(2)}, u32[]{:S(2)}) %collective-permute-start.1) | collective-permute-done | bytes 262176 | tf_op jit(solution)/shard_map/ppermute | solution.py:39
  15.2 0.7 first.1
  16.5 0.7 tops.2
  17.4 1.7 %collective-permute-start.10 = (f32[512,128]{1,0:T(8,128)S(1)}, f32[512,128]{1,0:T(8,128)S(1)}, u32[]{:S(2)}, u32[]{:S(2)}) collective-permute-start(f32[512,128]{1,0:T(8,128)S(1)} %get-tuple-element.133.refs_0_), channel_id=1, source_target_pairs={{1,0},{0,1},{3,2},{2,3},{5,4},{4,5},{7,6},{6,7},{9,8},{8,9},{11,10... | collective-permute-start | bytes 786440 | tf_op jit(solution)/shard_map/ppermute | solution.py:39
  19.7 1.6 %collective-permute-start.9 = (f32[128,256]{1,0:T(8,128)S(1)}, f32[128,256]{1,0:T(8,128)S(1)}, u32[]{:S(2)}, u32[]{:S(2)}) collective-permute-start(f32[128,256]{1,0:T(8,128)S(1)} %get-tuple-element.132.refs_0_), channel_id=1, source_target_pairs={{0,4},{2,6},{4,0},{6,2},{8,12},{10,14},{12,8},{14,10},{16,20},{18,... | collective-permute-start | bytes 393224 | tf_op jit(solution)/shard_map/ppermute | solution.py:33
  21.2 0.6 combine.16
  21.9 1.0 %tops.3 = (f32[640,256]{1,0:T(8,128)S(1)}, bf16[256,640]{1,0:T(8,128)(2,1)S(1)}, bf16[256,640]{1,0:T(8,128)(2,1)S(1)}, f32[8,128]{1,0:T(8,128)S(1)}) custom-call(bf16[256,640]{1,0:T(8,128)(2,1)S(1)} %get-tuple-element.105.refs_0_, bf16[256,640]{1,0:T(8,128)(2,1)S(1)} %get-tuple-element.106.refs_1_, bf16[512,256]{1,0:T(8,128)(2,1)S(1)} %get-tuple-element.107.refs_2_.refs_1_, ...), custom_call_target="tpu_custom_call" | custom-call | flops 11512800256 | bytes 36900000 | tf_op jit(solution)/shard_map/tops/pallas_call | solution.py:127
  23.4 0.5 collective-permute-start.13
  24.3 1.7 %collective-permute-done.10.refs_1_ = f32[512,128]{1,0:T(8,128)S(1)} collective-permute-done((f32[512,128]{1,0:T(8,128)S(1)}, f32[512,128]{1,0:T(8,128)S(1)}, u32[]{:S(2)}, u32[]{:S(2)}) %collective-permute-start.10) | collective-permute-done | bytes 262176 | tf_op jit(solution)/shard_map/ppermute | solution.py:39
  26.6 1.8 %collective-permute-start.11 = (f32[128,256]{1,0:T(8,128)S(1)}, f32[128,256]{1,0:T(8,128)S(1)}, u32[]{:S(2)}, u32[]{:S(2)}) collective-permute-start(f32[128,256]{1,0:T(8,128)S(1)} %get-tuple-element.140.refs_0_), channel_id=1, source_target_pairs={{0,8},{2,10},{4,12},{6,14},{8,0},{10,2},{12,4},{14,6},{16,24},{18,... | collective-permute-start | bytes 393224 | tf_op jit(solution)/shard_map/ppermute | solution.py:33
  28.4 0.6 combine.18
  29.1 1.8 %collective-permute-start.17 = (f32[256,256]{1,0:T(8,128)S(1)}, f32[256,256]{1,0:T(8,128)S(1)}, u32[]{:S(2)}, u32[]{:S(2)}) collective-permute-start(f32[256,256]{1,0:T(8,128)S(1)} %get-tuple-element.155.refs_0_), channel_id=1, source_target_pairs={{0,4},{2,6},{4,0},{6,2},{8,12},{10,14},{12,8},{14,10},{16,20},{18,... | collective-permute-start | bytes 786440 | tf_op jit(solution)/shard_map/ppermute | solution.py:33
  30.9 1.0 %collective-permute-done.13.refs_1_ = f32[256,256]{1,0:T(8,128)S(1)} collective-permute-done((f32[256,256]{1,0:T(8,128)S(1)}, f32[256,256]{1,0:T(8,128)S(1)}, u32[]{:S(2)}, u32[]{:S(2)}) %collective-permute-start.13) | collective-permute-done | bytes 262176 | tf_op jit(solution)/shard_map/ppermute | solution.py:33
  31.9 0.6 combine.19
  32.6 2.3 %collective-permute-start.16 = (f32[256,256]{1,0:T(8,128)S(1)}, f32[256,256]{1,0:T(8,128)S(1)}, u32[]{:S(2)}, u32[]{:S(2)}) collective-permute-start(f32[256,256]{1,0:T(8,128)S(1)} %get-tuple-element.154.refs_0_), channel_id=1, source_target_pairs={{0,8},{2,10},{4,12},{6,14},{8,0},{10,2},{12,4},{14,6},{16,24},{18,... | collective-permute-start | bytes 786440 | tf_op jit(solution)/shard_map/ppermute | solution.py:33
  35.6 2.7 %collective-permute-start.14 = (f32[128,256]{1,0:T(8,128)S(1)}, f32[128,256]{1,0:T(8,128)S(1)}, u32[]{:S(2)}, u32[]{:S(2)}) collective-permute-start(f32[128,256]{1,0:T(8,128)S(1)} %get-tuple-element.152.refs_0_), channel_id=1, source_target_pairs={{0,16},{2,18},{4,20},{6,22},{8,24},{10,26},{12,28},{14,30},{16,0},... | collective-permute-start | bytes 393224 | tf_op jit(solution)/shard_map/ppermute | solution.py:33
  38.2 0.6 combine.21
  38.9 0.9 %collective-permute-start.21 = (f32[256,256]{1,0:T(8,128)S(1)}, f32[256,256]{1,0:T(8,128)S(1)}, u32[]{:S(2)}, u32[]{:S(2)}) collective-permute-start(f32[256,256]{1,0:T(8,128)S(1)} %get-tuple-element.177.refs_0_), channel_id=1, source_target_pairs={{0,4},{2,6},{4,0},{6,2},{8,12},{10,14},{12,8},{14,10},{16,20},{18,... | collective-permute-start | bytes 786440 | tf_op jit(solution)/shard_map/ppermute | solution.py:33
  39.8 0.6 combine.22
  40.4 1.0 %collective-permute-start.20 = (f32[256,256]{1,0:T(8,128)S(1)}, f32[256,256]{1,0:T(8,128)S(1)}, u32[]{:S(2)}, u32[]{:S(2)}) collective-permute-start(f32[256,256]{1,0:T(8,128)S(1)} %get-tuple-element.176.refs_0_), channel_id=1, source_target_pairs={{0,8},{2,10},{4,12},{6,14},{8,0},{10,2},{12,4},{14,6},{16,24},{18,... | collective-permute-start | bytes 786440 | tf_op jit(solution)/shard_map/ppermute | solution.py:33
  41.4 1.5 %collective-permute-done.16.refs_1_ = f32[256,256]{1,0:T(8,128)S(1)} collective-permute-done((f32[256,256]{1,0:T(8,128)S(1)}, f32[256,256]{1,0:T(8,128)S(1)}, u32[]{:S(2)}, u32[]{:S(2)}) %collective-permute-start.16) | collective-permute-done | bytes 262176 | tf_op jit(solution)/shard_map/ppermute | solution.py:33
  42.9 0.6 combine.23
  43.5 5.6 %collective-permute-start.19 = (f32[256,256]{1,0:T(8,128)S(1)}, f32[256,256]{1,0:T(8,128)S(1)}, u32[]{:S(2)}, u32[]{:S(2)}) collective-permute-start(f32[256,256]{1,0:T(8,128)S(1)} %get-tuple-element.175.refs_0_), channel_id=1, source_target_pairs={{0,16},{2,18},{4,20},{6,22},{8,24},{10,26},{12,28},{14,30},{16,0},... | collective-permute-start | bytes 786440 | tf_op jit(solution)/shard_map/ppermute | solution.py:33
  49.3 1.7 %rest.1 = (f32[512,1024]{1,0:T(8,128)}, f32[8,128]{1,0:T(8,128)S(1)}) custom-call(f32[512,1024]{1,0:T(8,128)S(1)} %copy-done, bf16[512,256]{1,0:T(8,128)(2,1)S(1)} %get-tuple-element.107.refs_2_.refs_1_, bf16[512,256]{1,0:T(8,128)(2,1)S(1)} %get-tuple-element.108.refs_3_.refs_2_, bf16[256,128]{1,0:T(8,128)(2,1)S(1)} %get-tuple-element.164.refs_3_, ...), custom_call_target="tpu_custom_call" | custom-call | flops 19571759104 | bytes 62730000 | tf_op jit(solution)/shard_map/rest/pallas_call | solution.py:127
  51.0 1.2 %finish.5 = (f32[512,1024]{1,0:T(8,128)}, f32[8,128]{1,0:T(8,128)S(1)}) custom-call(f32[128,256]{1,0:T(8,128)S(1)} %get-tuple-element.152.refs_0_, f32[128,256]{1,0:T(8,128)S(1)} %collective-permute-done.14.refs_1_, bf16[256,256]{1,0:T(8,128)(2,1)S(1)} %get-tuple-element.160.refs_2_, ...), custom_call_target="tpu_custom_call", output_to_operand_aliasing={{0}: (7, {})} | custom-call | flops 14966639616 | bytes 47970000 | tf_op jit(solution)/shard_map/finish/pallas_call | solution.py:127
  52.7 0.6 combine.25
  53.3 2.8 %collective-permute-start.24 = (f32[256,256]{1,0:T(8,128)S(1)}, f32[256,256]{1,0:T(8,128)S(1)}, u32[]{:S(2)}, u32[]{:S(2)}) collective-permute-start(f32[256,256]{1,0:T(8,128)S(1)} %get-tuple-element.185.refs_0_), channel_id=1, source_target_pairs={{0,8},{2,10},{4,12},{6,14},{8,0},{10,2},{12,4},{14,6},{16,24},{18,... | collective-permute-start | bytes 786440 | tf_op jit(solution)/shard_map/ppermute | solution.py:33
  56.2 0.8 combine.26
  57.4 1.6 %collective-permute-done.19.refs_1_ = f32[256,256]{1,0:T(8,128)S(1)} collective-permute-done((f32[256,256]{1,0:T(8,128)S(1)}, f32[256,256]{1,0:T(8,128)S(1)}, u32[]{:S(2)}, u32[]{:S(2)}) %collective-permute-start.19) | collective-permute-done | bytes 262176 | tf_op jit(solution)/shard_map/ppermute | solution.py:33
  59.0 1.4 %finish.6 = (f32[512,1024]{1,0:T(8,128)}, f32[8,128]{1,0:T(8,128)S(1)}) custom-call(f32[256,256]{1,0:T(8,128)S(1)} %get-tuple-element.175.refs_0_, f32[256,256]{1,0:T(8,128)S(1)} %collective-permute-done.19.refs_1_, bf16[256,256]{1,0:T(8,128)(2,1)S(1)} %get-tuple-element.160.refs_2_, ...), custom_call_target="tpu_custom_call", output_to_operand_aliasing={{0}: (7, {})} | custom-call | flops 14966639616 | bytes 47970000 | tf_op jit(solution)/shard_map/finish/pallas_call | solution.py:127
  60.9 3.0 %collective-permute-start.22 = (f32[128,256]{1,0:T(8,128)S(1)}, f32[128,256]{1,0:T(8,128)S(1)}, u32[]{:S(2)}, u32[]{:S(2)}) collective-permute-start(f32[128,256]{1,0:T(8,128)S(1)} %get-tuple-element.183.refs_0_), channel_id=1, source_target_pairs={{0,8},{2,10},{4,12},{6,14},{8,0},{10,2},{12,4},{14,6},{16,24},{18,... | collective-permute-start | bytes 393224 | tf_op jit(solution)/shard_map/ppermute | solution.py:33
  63.9 2.2 %collective-permute-done.24.refs_1_ = f32[256,256]{1,0:T(8,128)S(1)} collective-permute-done((f32[256,256]{1,0:T(8,128)S(1)}, f32[256,256]{1,0:T(8,128)S(1)}, u32[]{:S(2)}, u32[]{:S(2)}) %collective-permute-start.24) | collective-permute-done | bytes 262176 | tf_op jit(solution)/shard_map/ppermute | solution.py:33
  66.1 0.6 combine.28
  66.8 1.8 %collective-permute-start.26 = (f32[256,256]{1,0:T(8,128)S(1)}, f32[256,256]{1,0:T(8,128)S(1)}, u32[]{:S(2)}, u32[]{:S(2)}) collective-permute-start(f32[256,256]{1,0:T(8,128)S(1)} %get-tuple-element.191.refs_0_), channel_id=1, source_target_pairs={{0,16},{2,18},{4,20},{6,22},{8,24},{10,26},{12,28},{14,30},{16,0},... | collective-permute-start | bytes 786440 | tf_op jit(solution)/shard_map/ppermute | solution.py:33
  68.5 10.0 %collective-permute-done.23.refs_1_ = f32[256,256]{1,0:T(8,128)S(1)} collective-permute-done((f32[256,256]{1,0:T(8,128)S(1)}, f32[256,256]{1,0:T(8,128)S(1)}, u32[]{:S(2)}, u32[]{:S(2)}) %collective-permute-start.23) | collective-permute-done | bytes 262176 | tf_op jit(solution)/shard_map/ppermute | solution.py:33
  78.5 1.4 %finish.7 = (f32[512,1024]{1,0:T(8,128)}, f32[8,128]{1,0:T(8,128)S(1)}) custom-call(f32[256,256]{1,0:T(8,128)S(1)} %get-tuple-element.184.refs_0_, f32[256,256]{1,0:T(8,128)S(1)} %collective-permute-done.23.refs_1_, bf16[256,256]{1,0:T(8,128)(2,1)S(1)} %get-tuple-element.160.refs_2_, ...), custom_call_target="tpu_custom_call", output_to_operand_aliasing={{0}: (7, {})} | custom-call | flops 14966639616 | bytes 47970000 | tf_op jit(solution)/shard_map/finish/pallas_call | solution.py:127
  80.5 2.6 %collective-permute-done.26.refs_1_ = f32[256,256]{1,0:T(8,128)S(1)} collective-permute-done((f32[256,256]{1,0:T(8,128)S(1)}, f32[256,256]{1,0:T(8,128)S(1)}, u32[]{:S(2)}, u32[]{:S(2)}) %collective-permute-start.26) | collective-permute-done | bytes 262176 | tf_op jit(solution)/shard_map/ppermute | solution.py:33
  83.1 1.4 %finish.8 = (f32[512,1024]{1,0:T(8,128)}, f32[8,128]{1,0:T(8,128)S(1)}) custom-call(f32[256,256]{1,0:T(8,128)S(1)} %get-tuple-element.191.refs_0_, f32[256,256]{1,0:T(8,128)S(1)} %collective-permute-done.26.refs_1_, bf16[256,256]{1,0:T(8,128)(2,1)S(1)} %get-tuple-element.160.refs_2_, ...), custom_call_target="tpu_custom_call", output_to_operand_aliasing={{0}: (7, {})} | custom-call | flops 14966639616 | bytes 47970000 | tf_op jit(solution)/shard_map/finish/pallas_call | solution.py:127
  84.6 2.7 %collective-permute-done.25.refs_1_ = f32[128,256]{1,0:T(8,128)S(1)} collective-permute-done((f32[128,256]{1,0:T(8,128)S(1)}, f32[128,256]{1,0:T(8,128)S(1)}, u32[]{:S(2)}, u32[]{:S(2)}) %collective-permute-start.25) | collective-permute-done | bytes 131104 | tf_op jit(solution)/shard_map/ppermute | solution.py:33
  87.3 1.2 %finish.9 = (f32[512,1024]{1,0:T(8,128)}, f32[8,128]{1,0:T(8,128)}) custom-call(f32[128,256]{1,0:T(8,128)S(1)} %get-tuple-element.190.refs_0_, f32[128,256]{1,0:T(8,128)S(1)} %collective-permute-done.25.refs_1_, bf16[256,256]{1,0:T(8,128)(2,1)S(1)} %get-tuple-element.160.refs_2_, ...), custom_call_target="tpu_custom_call", output_to_operand_aliasing={{0}: (7, {})} | custom-call | flops 14966639616 | bytes 47970000 | tf_op jit(solution)/shard_map/finish/pallas_call | solution.py:127
  (41 shorter events, 5.7 us)
Async XLA Ops:
  0.0 10.6 %copy-start.1 = (f32[512,128]{1,0:T(8,128)S(1)}, f32[512,128]{1,0:T(8,128)}, u32[]{:S(2)}) copy-start(f32[512,128]{1,0:T(8,128)} %refs_0_.4) | copy-start | bytes 786436
  0.0 10.6 %copy-start = (f32[512,1024]{1,0:T(8,128)S(1)}, f32[512,1024]{1,0:T(8,128)}, u32[]{:S(2)}) copy-start(f32[512,1024]{1,0:T(8,128)} %refs_0_.5) | copy-start | bytes 6291460
  0.0 10.6 %collective-permute-start = (f32[512,128]{1,0:T(8,128)}, f32[512,128]{1,0:T(8,128)S(1)}, u32[]{:S(2)}, u32[]{:S(2)}) collective-permute-start(f32[512,128]{1,0:T(8,128)} %refs_0_.4), channel_id=1, source_target_pairs={{1,0},{0,1},{3,2},{2,3},{5,4},{4,5},{7,6},{6,7},{9,8},{8,9},{11,10... | collective-permute-start | bytes 786440 | tf_op jit(solution)/shard_map/ppermute | solution.py:39
  4.2 11.0 %collective-permute-start.1 = (f32[512,128]{1,0:T(8,128)S(1)}, f32[512,128]{1,0:T(8,128)S(1)}, u32[]{:S(2)}, u32[]{:S(2)}) collective-permute-start(f32[512,128]{1,0:T(8,128)S(1)} %get-tuple-element.111.refs_5_), channel_id=1, source_target_pairs={{1,0},{0,1},{3,2},{2,3},{5,4},{4,5},{7,6},{6,7},{9,8},{8,9},{11,10... | collective-permute-start | bytes 786440 | tf_op jit(solution)/shard_map/ppermute | solution.py:39
  4.4 7.8 %collective-permute-start.2 = (f32[256,128]{1,0:T(8,128)S(1)}, f32[256,128]{1,0:T(8,128)S(1)}, u32[]{:S(2)}, u32[]{:S(2)}) collective-permute-start(f32[256,128]{1,0:T(8,128)S(1)} %get-tuple-element.112.refs_7_), channel_id=1, source_target_pairs={{0,4},{2,6},{4,0},{6,2},{8,12},{10,14},{12,8},{14,10},{16,20},{18,... | collective-permute-start | bytes 393224 | tf_op jit(solution)/shard_map/ppermute | solution.py:33
  6.4 6.7 %collective-permute-start.3 = (f32[256,128]{1,0:T(8,128)S(1)}, f32[256,128]{1,0:T(8,128)S(1)}, u32[]{:S(2)}, u32[]{:S(2)}) collective-permute-start(f32[256,128]{1,0:T(8,128)S(1)} %get-tuple-element.113.refs_9_), channel_id=1, source_target_pairs={{0,8},{2,10},{4,12},{6,14},{8,0},{10,2},{12,4},{14,6},{16,24},{18,... | collective-permute-start | bytes 393224 | tf_op jit(solution)/shard_map/ppermute | solution.py:33
  8.0 8.5 %collective-permute-start.4 = (f32[256,128]{1,0:T(8,128)S(1)}, f32[256,128]{1,0:T(8,128)S(1)}, u32[]{:S(2)}, u32[]{:S(2)}) collective-permute-start(f32[256,128]{1,0:T(8,128)S(1)} %get-tuple-element.117.refs_7_), channel_id=1, source_target_pairs={{0,16},{2,18},{4,20},{6,22},{8,24},{10,26},{12,28},{14,30},{16,0},... | collective-permute-start | bytes 393224 | tf_op jit(solution)/shard_map/ppermute | solution.py:33
  15.9 3.2 %collective-permute-start.6 = (f32[256,256]{1,0:T(8,128)S(1)}, f32[256,256]{1,0:T(8,128)S(1)}, u32[]{:S(2)}, u32[]{:S(2)}) collective-permute-start(f32[256,256]{1,0:T(8,128)S(1)} %get-tuple-element.120.refs_0_), channel_id=1, source_target_pairs={{0,2},{2,0},{4,6},{6,4},{8,10},{10,8},{12,14},{14,12},{16,18},{18,... | collective-permute-start | bytes 786440 | tf_op jit(solution)/shard_map/ppermute | solution.py:33
  16.0 3.2 %collective-permute-start.7 = (f32[128,256]{1,0:T(8,128)S(1)}, f32[128,256]{1,0:T(8,128)S(1)}, u32[]{:S(2)}, u32[]{:S(2)}) collective-permute-start(f32[128,256]{1,0:T(8,128)S(1)} %get-tuple-element.127.refs_0_), channel_id=1, source_target_pairs={{0,2},{2,0},{4,6},{6,4},{8,10},{10,8},{12,14},{14,12},{16,18},{18,... | collective-permute-start | bytes 393224 | tf_op jit(solution)/shard_map/ppermute | solution.py:33
  17.2 4.0 %collective-permute-start.5 = (f32[256,256]{1,0:T(8,128)S(1)}, f32[256,256]{1,0:T(8,128)S(1)}, u32[]{:S(2)}, u32[]{:S(2)}) collective-permute-start(f32[256,256]{1,0:T(8,128)S(1)} %get-tuple-element.119.refs_0_), channel_id=1, source_target_pairs={{0,2},{2,0},{4,6},{6,4},{8,10},{10,8},{12,14},{14,12},{16,18},{18,... | collective-permute-start | bytes 786440 | tf_op jit(solution)/shard_map/ppermute | solution.py:33
  17.4 8.7 %collective-permute-start.10 = (f32[512,128]{1,0:T(8,128)S(1)}, f32[512,128]{1,0:T(8,128)S(1)}, u32[]{:S(2)}, u32[]{:S(2)}) collective-permute-start(f32[512,128]{1,0:T(8,128)S(1)} %get-tuple-element.133.refs_0_), channel_id=1, source_target_pairs={{1,0},{0,1},{3,2},{2,3},{5,4},{4,5},{7,6},{6,7},{9,8},{8,9},{11,10... | collective-permute-start | bytes 786440 | tf_op jit(solution)/shard_map/ppermute | solution.py:39
  19.7 6.5 %collective-permute-start.9 = (f32[128,256]{1,0:T(8,128)S(1)}, f32[128,256]{1,0:T(8,128)S(1)}, u32[]{:S(2)}, u32[]{:S(2)}) collective-permute-start(f32[128,256]{1,0:T(8,128)S(1)} %get-tuple-element.132.refs_0_), channel_id=1, source_target_pairs={{0,4},{2,6},{4,0},{6,2},{8,12},{10,14},{12,8},{14,10},{16,20},{18,... | collective-permute-start | bytes 393224 | tf_op jit(solution)/shard_map/ppermute | solution.py:33
  22.9 5.5 %collective-permute-start.8 = (f32[640,256]{1,0:T(8,128)S(1)}, f32[640,256]{1,0:T(8,128)S(1)}, u32[]{:S(2)}, u32[]{:S(2)}) collective-permute-start(f32[640,256]{1,0:T(8,128)S(1)} %get-tuple-element.131.refs_0_), channel_id=1, source_target_pairs={{0,2},{2,0},{4,6},{6,4},{8,10},{10,8},{12,14},{14,12},{16,18},{18,... | collective-permute-start | bytes 1966088 | tf_op jit(solution)/shard_map/ppermute | solution.py:33
  23.4 8.5 %collective-permute-start.13 = (f32[256,256]{1,0:T(8,128)S(1)}, f32[256,256]{1,0:T(8,128)S(1)}, u32[]{:S(2)}, u32[]{:S(2)}) collective-permute-start(f32[256,256]{1,0:T(8,128)S(1)} %get-tuple-element.143.refs_0_), channel_id=1, source_target_pairs={{0,4},{2,6},{4,0},{6,2},{8,12},{10,14},{12,8},{14,10},{16,20},{18,... | collective-permute-start | bytes 786440 | tf_op jit(solution)/shard_map/ppermute | solution.py:33
  24.0 10.9 %collective-permute-start.12 = (f32[512,128]{1,0:T(8,128)S(1)}, f32[512,128]{1,0:T(8,128)S(1)}, u32[]{:S(2)}, u32[]{:S(2)}) collective-permute-start(f32[512,128]{1,0:T(8,128)S(1)} %get-tuple-element.141.refs_0_), channel_id=1, source_target_pairs={{1,0},{0,1},{3,2},{2,3},{5,4},{4,5},{7,6},{6,7},{9,8},{8,9},{11,10... | collective-permute-start | bytes 786440 | tf_op jit(solution)/shard_map/ppermute | solution.py:39
  26.6 8.5 %collective-permute-start.11 = (f32[128,256]{1,0:T(8,128)S(1)}, f32[128,256]{1,0:T(8,128)S(1)}, u32[]{:S(2)}, u32[]{:S(2)}) collective-permute-start(f32[128,256]{1,0:T(8,128)S(1)} %get-tuple-element.140.refs_0_), channel_id=1, source_target_pairs={{0,8},{2,10},{4,12},{6,14},{8,0},{10,2},{12,4},{14,6},{16,24},{18,... | collective-permute-start | bytes 393224 | tf_op jit(solution)/shard_map/ppermute | solution.py:33
  29.1 10.7 %collective-permute-start.17 = (f32[256,256]{1,0:T(8,128)S(1)}, f32[256,256]{1,0:T(8,128)S(1)}, u32[]{:S(2)}, u32[]{:S(2)}) collective-permute-start(f32[256,256]{1,0:T(8,128)S(1)} %get-tuple-element.155.refs_0_), channel_id=1, source_target_pairs={{0,4},{2,6},{4,0},{6,2},{8,12},{10,14},{12,8},{14,10},{16,20},{18,... | collective-permute-start | bytes 786440 | tf_op jit(solution)/shard_map/ppermute | solution.py:33
  32.6 10.3 %collective-permute-start.16 = (f32[256,256]{1,0:T(8,128)S(1)}, f32[256,256]{1,0:T(8,128)S(1)}, u32[]{:S(2)}, u32[]{:S(2)}) collective-permute-start(f32[256,256]{1,0:T(8,128)S(1)} %get-tuple-element.154.refs_0_), channel_id=1, source_target_pairs={{0,8},{2,10},{4,12},{6,14},{8,0},{10,2},{12,4},{14,6},{16,24},{18,... | collective-permute-start | bytes 786440 | tf_op jit(solution)/shard_map/ppermute | solution.py:33
  35.0 14.1 %collective-permute-start.15 = (f32[512,128]{1,0:T(8,128)S(1)}, f32[512,128]{1,0:T(8,128)S(1)}, u32[]{:S(2)}, u32[]{:S(2)}) collective-permute-start(f32[512,128]{1,0:T(8,128)S(1)} %get-tuple-element.153.refs_0_), channel_id=1, source_target_pairs={{1,0},{0,1},{3,2},{2,3},{5,4},{4,5},{7,6},{6,7},{9,8},{8,9},{11,10... | collective-permute-start | bytes 786440 | tf_op jit(solution)/shard_map/ppermute | solution.py:39
  35.6 15.4 %collective-permute-start.14 = (f32[128,256]{1,0:T(8,128)S(1)}, f32[128,256]{1,0:T(8,128)S(1)}, u32[]{:S(2)}, u32[]{:S(2)}) collective-permute-start(f32[128,256]{1,0:T(8,128)S(1)} %get-tuple-element.152.refs_0_), channel_id=1, source_target_pairs={{0,16},{2,18},{4,20},{6,22},{8,24},{10,26},{12,28},{14,30},{16,0},... | collective-permute-start | bytes 393224 | tf_op jit(solution)/shard_map/ppermute | solution.py:33
  38.9 13.8 %collective-permute-start.21 = (f32[256,256]{1,0:T(8,128)S(1)}, f32[256,256]{1,0:T(8,128)S(1)}, u32[]{:S(2)}, u32[]{:S(2)}) collective-permute-start(f32[256,256]{1,0:T(8,128)S(1)} %get-tuple-element.177.refs_0_), channel_id=1, source_target_pairs={{0,4},{2,6},{4,0},{6,2},{8,12},{10,14},{12,8},{14,10},{16,20},{18,... | collective-permute-start | bytes 786440 | tf_op jit(solution)/shard_map/ppermute | solution.py:33
  40.4 15.7 %collective-permute-start.20 = (f32[256,256]{1,0:T(8,128)S(1)}, f32[256,256]{1,0:T(8,128)S(1)}, u32[]{:S(2)}, u32[]{:S(2)}) collective-permute-start(f32[256,256]{1,0:T(8,128)S(1)} %get-tuple-element.176.refs_0_), channel_id=1, source_target_pairs={{0,8},{2,10},{4,12},{6,14},{8,0},{10,2},{12,4},{14,6},{16,24},{18,... | collective-permute-start | bytes 786440 | tf_op jit(solution)/shard_map/ppermute | solution.py:33
  43.5 15.5 %collective-permute-start.19 = (f32[256,256]{1,0:T(8,128)S(1)}, f32[256,256]{1,0:T(8,128)S(1)}, u32[]{:S(2)}, u32[]{:S(2)}) collective-permute-start(f32[256,256]{1,0:T(8,128)S(1)} %get-tuple-element.175.refs_0_), channel_id=1, source_target_pairs={{0,16},{2,18},{4,20},{6,22},{8,24},{10,26},{12,28},{14,30},{16,0},... | collective-permute-start | bytes 786440 | tf_op jit(solution)/shard_map/ppermute | solution.py:33
  52.6 7.9 %collective-permute-start.18 = (f32[128,256]{1,0:T(8,128)S(1)}, f32[128,256]{1,0:T(8,128)S(1)}, u32[]{:S(2)}, u32[]{:S(2)}) collective-permute-start(f32[128,256]{1,0:T(8,128)S(1)} %get-tuple-element.174.refs_0_), channel_id=1, source_target_pairs={{0,4},{2,6},{4,0},{6,2},{8,12},{10,14},{12,8},{14,10},{16,20},{18,... | collective-permute-start | bytes 393224 | tf_op jit(solution)/shard_map/ppermute | solution.py:33
  53.3 12.8 %collective-permute-start.24 = (f32[256,256]{1,0:T(8,128)S(1)}, f32[256,256]{1,0:T(8,128)S(1)}, u32[]{:S(2)}, u32[]{:S(2)}) collective-permute-start(f32[256,256]{1,0:T(8,128)S(1)} %get-tuple-element.185.refs_0_), channel_id=1, source_target_pairs={{0,8},{2,10},{4,12},{6,14},{8,0},{10,2},{12,4},{14,6},{16,24},{18,... | collective-permute-start | bytes 786440 | tf_op jit(solution)/shard_map/ppermute | solution.py:33
  57.0 21.6 %collective-permute-start.23 = (f32[256,256]{1,0:T(8,128)S(1)}, f32[256,256]{1,0:T(8,128)S(1)}, u32[]{:S(2)}, u32[]{:S(2)}) collective-permute-start(f32[256,256]{1,0:T(8,128)S(1)} %get-tuple-element.184.refs_0_), channel_id=1, source_target_pairs={{0,16},{2,18},{4,20},{6,22},{8,24},{10,26},{12,28},{14,30},{16,0},... | collective-permute-start | bytes 786440 | tf_op jit(solution)/shard_map/ppermute | solution.py:33
  60.9 19.1 %collective-permute-start.22 = (f32[128,256]{1,0:T(8,128)S(1)}, f32[128,256]{1,0:T(8,128)S(1)}, u32[]{:S(2)}, u32[]{:S(2)}) collective-permute-start(f32[128,256]{1,0:T(8,128)S(1)} %get-tuple-element.183.refs_0_), channel_id=1, source_target_pairs={{0,8},{2,10},{4,12},{6,14},{8,0},{10,2},{12,4},{14,6},{16,24},{18,... | collective-permute-start | bytes 393224 | tf_op jit(solution)/shard_map/ppermute | solution.py:33
  66.8 16.4 %collective-permute-start.26 = (f32[256,256]{1,0:T(8,128)S(1)}, f32[256,256]{1,0:T(8,128)S(1)}, u32[]{:S(2)}, u32[]{:S(2)}) collective-permute-start(f32[256,256]{1,0:T(8,128)S(1)} %get-tuple-element.191.refs_0_), channel_id=1, source_target_pairs={{0,16},{2,18},{4,20},{6,22},{8,24},{10,26},{12,28},{14,30},{16,0},... | collective-permute-start | bytes 786440 | tf_op jit(solution)/shard_map/ppermute | solution.py:33
  80.4 6.9 %collective-permute-start.25 = (f32[128,256]{1,0:T(8,128)S(1)}, f32[128,256]{1,0:T(8,128)S(1)}, u32[]{:S(2)}, u32[]{:S(2)}) collective-permute-start(f32[128,256]{1,0:T(8,128)S(1)} %get-tuple-element.190.refs_0_), channel_id=1, source_target_pairs={{0,16},{2,18},{4,20},{6,22},{8,24},{10,26},{12,28},{14,30},{16,0},... | collective-permute-start | bytes 393224 | tf_op jit(solution)/shard_map/ppermute | solution.py:33

commit v3 on v2

--- a/solution.py
+++ b/solution.py
@@ -13,13 +13,15 @@
 VMEM_LIMIT = 32 * 2**20
 MICROSECOND = 3.69e6
 SCALE = 10.0
+
 USUAL = dict(
     pick=1.1,
     inner=1.0,
     later=2.4,
     first=0.6,
     tops=1.0,
-    stack=0.1,
+    hand=0.1,
+    join=0.1,
     node=0.15,
     combine=0.6,
     rest=1.7,
@@ -82,7 +84,9 @@
     def dot(a, b):
         return lax.dot_general(a, b, (over, ((), ())), preferred_element_type=f32)
 
-    return dot(left[0], right[0]) + (dot(left[0], right[1]) + dot(left[1], right[0]))
+    rows = left[0].shape[0]
+    both = dot(jnp.concatenate(left), right[0])
+    return both[:rows] + (dot(left[0], right[1]) + both[rows:])
 
 
 plain = ((1,), (0,))
@@ -154,25 +158,21 @@
 
 
 def pick_body(levels, ins, outs):
-    leaf, reflect, factor, sems = ins[0], ins[1], ins[2], outs[levels]
-    size = leaf.shape[0]
+    reflect, factor, sems = ins[0], ins[1], outs[levels]
     position = lax.axis_index("row")
-    targets = [outs[0].at[pl.ds(size, size)]] + list(outs[1:levels])
-    pltpu.make_async_copy(leaf, outs[0].at[pl.ds(0, size)], sems.at[levels]).start()
     for s in range(levels):
         clear = position // (1 << s) % 2 == 0
 
         @pl.when(clear)
         def _(s=s):
-            pltpu.make_async_copy(factor.at[s], targets[s], sems.at[s]).start()
+            pltpu.make_async_copy(factor.at[s], outs[s], sems.at[s]).start()
 
         @pl.when(jnp.logical_not(clear))
         def _(s=s):
-            pltpu.make_async_copy(reflect.at[s], targets[s], sems.at[s]).start()
+            pltpu.make_async_copy(reflect.at[s], outs[s], sems.at[s]).start()
 
     for s in range(levels):
-        pltpu.make_async_copy(factor.at[s], targets[s], sems.at[s]).wait()
-    pltpu.make_async_copy(leaf, outs[0].at[pl.ds(0, size)], sems.at[levels]).wait()
+        pltpu.make_async_copy(factor.at[s], outs[s], sems.at[s]).wait()
 
 
 def inner_body(n, ins, outs):
@@ -184,6 +184,7 @@
         ref[...] = part
     width = outs[4].shape[1]
     put(outs[4:6], product(turned_parts, parts(trailing[:, :width]), plain))
+    outs[6][...] = ins[n + 1][...]
 
 
 def later_body(start, ins, outs):
@@ -192,13 +193,13 @@
 
 
 def first_body(n, ins, outs):
-    size = outs[0].shape[1]
-    given = ins[5 : 5 + n]
-    put(outs[3:5], triangle(whole([ref[:size] for ref in given])).T)
-    outs[5][...] = whole([ref[size:] for ref in given])
+    put(outs[3:5], triangle(whole([ref[...] for ref in ins[5 : 5 + n]])).T)
     tops_body(0, 0, list(ins[:5]) + list(outs[3:5]), outs[:3])
-    for i, out in enumerate(outs[6:]):
-        stack(out, ins[5 + n + 2 * i : 7 + n + 2 * i])
+
+
+def join_body(n, ins, outs):
+    outs[0][...] = whole([ref[...] for ref in ins[:n]])
+    hand_on(ins[n:], outs[1:])
 
 
 def tops_body(start, inner_start, ins, outs):
@@ -210,8 +211,7 @@
     outs[2][...] = scaled[1]
     taken = product((vec_h[:size], vec_l[:size]), scaled, plain)
     outs[0][...] = (trailing[:size, start : start + width] - taken).T
-    for i, out in enumerate(outs[3:]):
-        stack(out, ins[7 + 2 * i : 9 + 2 * i])
+    hand_on(ins[7:], outs[3:])
 
 
 def rest_body(ins, outs):
@@ -227,31 +227,38 @@
         start += width
 
 
-def stack(out, ins):
-    size = ins[0].shape[0]
-    for i, ref in enumerate(ins):
-        out[i * size : (i + 1) * size] = ref[...]
+def hand_on(ins, outs):
+    ins = list(ins)
+    for out in outs:
+        at = 0
+        while at < out.shape[0]:
+            piece = ins.pop(0)
+            out[at : at + piece.shape[0]] = piece[...]
+            at += piece.shape[0]
 
 
 def node_body(section, n, ins, outs):
     clear = lax.axis_index("row") // (1 << section) % 2 == 0
-    if section:
-        size = ins[0].shape[0] // 2
+    size = outs[0].shape[0]
+    if section == 0:
+        own, partner = ins[0][...], ins[1][...]
+    else:
         own = whole([ref[:size] for ref in ins[:n]])
         partner = whole([ref[size:] for ref in ins[:n]])
-    else:
-        own, partner = ins[0][...], ins[1][...]
     put(outs[:2], jnp.where(clear, partner, own))
     put(outs[2:4], triangle(jnp.where(clear, own, partner)))
-    for ref, value in zip(outs[4:], ins[n:]):
-        ref[...] = value[...]
-
-
-def combine_body(section, last, mine_at, other_at, ins, outs):
-    width = outs[0].shape[1 if last else 0]
-    mine, other = ins[0][mine_at : mine_at + width], ins[1][other_at : other_at + width]
-    node_y = ins[2][...], ins[3][...]
-    node_t = ins[4][...], ins[5][...]
+    hand_on(ins[n if section else 2 :], outs[4:])
+
+
+def combine_body(section, last, spans, ins, outs):
+    pairs, node = ins[: 2 * len(spans)], ins[2 * len(spans) :]
+
+    def rows_of(refs):
+        return jnp.concatenate([ref[at : at + width] for ref, (at, width) in zip(refs, spans)])
+
+    mine, other = rows_of(pairs[::2]), rows_of(pairs[1::2])
+    node_y = node[0][...], node[1][...]
+    node_t = node[2][...], node[3][...]
     clear = lax.axis_index("row") // (1 << section) % 2 == 0
     leader = jnp.where(clear, mine, other)
     follower = jnp.where(clear, other, mine)
@@ -270,23 +277,37 @@
         write(mine - product(parts(coupling), node_y, across))
 
 
-def widths_of(columns):
+def cut(columns, width, ahead=()):
+    widths = []
+    left = columns
+    for each in list(ahead) + [width] * (columns // width):
+        if each <= left:
+            widths.append(each)
+            left -= each
+    return widths + [left] * (left > 0)
+
+
+def spans_of(widths):
+    return [(sum(widths[:i]), width) for i, width in enumerate(widths)]
+
+
+def cuts_of(columns, levels):
     if columns % LANES:
-        return [columns]
-    units = columns // LANES
-    short = min(units, 2 + units % 2)
-    doubles = (units - short) // 2
-    return [LANES] + [2 * LANES] * doubles + [LANES] * (short - 1)
-
-
-def groups_of(widths):
-    chunks = list(range(len(widths)))
-    return [group for group in (chunks[:1], chunks[1:2], chunks[2:]) if group]
-
-
-def order_of(chunks, levels):
-    order = [(s, c) for s in range(levels) for c in range(chunks)]
-    return sorted(order, key=lambda at: (sum(at), at[0]))
+        return [[(0, columns)]] * (levels + 1)
+    double = min(columns, 2 * LANES)
+    coarse = spans_of(cut(columns, double))
+    fine = spans_of(cut(columns, double, (LANES, LANES)))
+    first = spans_of(cut(columns, max(columns - double, LANES), (double,)))
+    return [first] + [fine] * (levels - 2) + [coarse] * (min(levels, 2))
+
+
+def order_of(cuts):
+    order = []
+    for s, given in enumerate(cuts[1:]):
+        for c, (start, _) in enumerate(given):
+            wave = max(i for i, (at, _) in enumerate(cuts[-1]) if at <= start)
+            order.append((s + wave, s, c))
+    return [at[1:] for at in sorted(order)]
 
 
 def per_device(trailing, reflectors, leaf_factor, node_reflect, node_factor):
@@ -294,41 +315,38 @@
     rows, columns = trailing.shape
     size, piece = leaf_factor.shape
     levels = node_factor.shape[0]
-    widths = widths_of(columns)
-    starts = [sum(widths[:c]) for c in range(len(widths))]
-    groups = groups_of(widths)
-    early = sum(widths[c] for group in groups[:2] for c in group)
+    cuts = cuts_of(columns, levels)
+    early = cuts[0][0][1]
     copied = pl.BlockSpec(memory_space=pltpu.VMEM)
     far_away = pl.BlockSpec(memory_space=pl.ANY)
 
     vectors = col_blocks(reflectors)
     n = len(vectors)
-    zeroth, *pieces = line(
+    factor = col_blocks(leaf_factor)
+    pieces = line(
         functools.partial(pick_body, levels),
         "pick",
-        [(in_hbm(x), far_away) for x in (leaf_factor, node_reflect, node_factor)],
-        [held(2 * size, piece)] + [held(size, piece)] * (levels - 1),
-        scratch=[pltpu.SemaphoreType.DMA((levels + 1,))],
-    )
-    pieces = [None] + pieces
-    zeroth = col_blocks(zeroth)
+        [(in_hbm(x), far_away) for x in (node_reflect, node_factor)],
+        [held(size, piece)] * levels,
+        scratch=[pltpu.SemaphoreType.DMA((levels,))],
+    )
     far = [None] + [swapped(pieces[s], "row", s) for s in range(1, levels)]
 
-    def stacked(*sections):
-        given, made = [], []
-        for s in sections:
-            if s < levels:
-                given += [pieces[s], far[s]]
-                made.append(held(2 * size, piece))
-        return given, made
-
-    vec_h, vec_l, vect_h, vect_l, inn_h, inn_l = line(
+    def stacked(sections):
+        given = [x for s in sections for x in (pieces[s], far[s])]
+        return given, [held(2 * size, piece)] * len(sections)
+
+    vec_h, vec_l, vect_h, vect_l, inn_h, inn_l, zeroth = line(
         functools.partial(inner_body, n),
         "inner",
-        [(vectors[0], copied)] + vectors[1:] + [trailing],
-        held_parts(rows, size) + held_parts(size, rows) + held_parts(size, early),
-    )
-    sources = [(inn_h, inn_l)] * 2
+        [(vectors[0], copied)] + vectors[1:] + [trailing, pieces[0]],
+        held_parts(rows, size)
+        + held_parts(size, rows)
+        + held_parts(size, early)
+        + [held(size, piece)],
+    )
+    zeroth = col_blocks(zeroth)
+    sources = [(inn_h, inn_l)]
     if columns > early:
         sources.append(
             line(
@@ -338,52 +356,46 @@
                 held_parts(size, columns - early),
             )
         )
-    given, made = stacked(1, 2)
-    top, high, low, tri_h, tri_l, own, *stacks = line(
+    top, high, low, tri_h, tri_l = line(
         functools.partial(first_body, n),
         "first",
-        list(sources[0]) + [vec_h, vec_l, trailing] + zeroth + given,
-        [held(widths[0], size)]
-        + held_parts(size, widths[0])
-        + held_parts(size, size)
-        + [held(size, size)]
-        + made,
-    )
-    stacks = [None] + stacks
-    other = swapped(top, "row", 0)
-    partner = swapped(own, "row", 0)
-    tops, others, scaled = {0: (top, 0)}, {0: (other, 0)}, [high, low]
+        [inn_h, inn_l, vec_h, vec_l, trailing] + [(factor[0], copied)] + factor[1:],
+        [held(early, size)] + held_parts(size, early) + held_parts(size, size),
+    )
+    tops = [[(0, early, top, swapped(top, "row", 0))]] + [[] for _ in range(levels)]
+    scaled = [high, low]
     nodes = [None] * levels
     out = None
 
-    def tops_of(g):
-        group = groups[g]
-        start, width = starts[group[0]], sum(widths[c] for c in group)
-        given, made = stacked(*range(3, levels)) if g == 1 else ([], [])
-        top, high, low, *more = line(
-            functools.partial(tops_body, start, start if g < 2 else 0),
+    stacks = [None] * levels
+    if columns > early:
+        given, made = stacked(range(1, min(levels, 3)))
+        width = columns - early
+        top, high, low, *stacks[1:3] = line(
+            functools.partial(tops_body, early, 0),
             "tops",
-            list(sources[g]) + [vec_h, vec_l, trailing, tri_h, tri_l] + given,
+            list(sources[1]) + [vec_h, vec_l, trailing, tri_h, tri_l] + given,
             [held(width, size)] + held_parts(size, width) + made,
         )
-        stacks.extend(more)
-        scaled.extend([high, low])
-        other = swapped(top, "row", 0)
-        for c in group:
-            tops[c] = top, starts[c] - start
-            others[c] = other, starts[c] - start
-
-    if len(groups) > 1:
-        tops_of(1)
-    for s in range(len(stacks), levels):
-        given, made = stacked(s)
-        stacks += line(lambda ins, outs: stack(outs[0], ins), "stack", given, made)
+        scaled += [high, low]
+        tops[0].append((early, width, top, swapped(top, "row", 0)))
+    elif levels > 1:
+        stacks[1:3] = line(hand_on, "hand", *stacked(range(1, min(levels, 3))))
+    given, made = stacked(range(3, levels))
+    own, *stacks[3:] = line(
+        functools.partial(join_body, n), "join", zeroth + given, [held(size, size)] + made
+    )
+    partner = swapped(own, "row", 0)
+    (other,) = line(hand_on, "hand", [tops[0][0][3]], [held(early, size)])
+    tops[0][0] = *tops[0][0][:3], other
 
     def node_of(s):
-        inputs = col_blocks(stacks[s]) if s else [own, partner]
+        inputs = [own, partner]
+        if s:
+            inputs = col_blocks(stacks[s])
         held_back = [t for t in range(2, levels) if s == (0 if t == 2 else t - 1)]
         *nodes[s], = line(
-            functools.partial(node_body, s, len(inputs)),
+            functools.partial(node_body, s, n),
             "node",
             inputs + [stacks[t] for t in held_back],
             held_parts(size, size) * 2 + [held(2 * size, piece)] * len(held_back),
@@ -391,20 +403,30 @@
         for t in held_back:
             stacks[t] = nodes[s].pop()
 
-    for s, c in order_of(len(widths), levels):
-        if (s, c) == (1, 0) and len(groups) > 2:
-            tops_of(2)
+    for s, c in order_of(cuts):
         if nodes[s] is None:
+            if 2 < s == levels - 1:
+                at, extent, mine, other = tops[s][0]
+                (other,) = line(hand_on, "hand", [other], [held(*other.shape)])
+                tops[s][0] = at, extent, mine, other
             node_of(s)
-        mine, mine_at = tops[c]
-        other, other_at = others[c]
-        inputs = [mine, other] + nodes[s]
+        start, width = cuts[s + 1][c]
+        inputs, spans = [], []
+        for at, extent, mine, other in tops[s]:
+            low, high = max(at, start), min(at + extent, start + width)
+            if low < high:
+                if low > start:
+                    inputs[1::2] = line(
+                        hand_on, "hand", inputs[1::2], [held(*x.shape) for x in inputs[1::2]]
+                    )
+                inputs += [mine, other]
+                spans.append((low - at, high - low))
+        inputs += nodes[s]
         last = s == levels - 1
-        body = functools.partial(combine_body, s, last, mine_at, other_at)
+        body = functools.partial(combine_body, s, last, spans)
         if not last:
-            (top,) = line(body, "combine", inputs, [held(widths[c], size)])
-            tops[c] = top, 0
-            others[c] = swapped(top, "row", s + 1), 0
+            (top,) = line(body, "combine", inputs, [held(width, size)])
+            tops[s + 1].append((start, width, top, swapped(top, "row", s + 1)))
         else:
             if out is None:
                 (out,) = line(
@@ -418,11 +440,9 @@
                         )
                     ],
                 )
-            block = pl.BlockSpec((size, LANES), lambda i, at=starts[c] // LANES: (0, at))
-            if widths[c] != LANES:
-                block = pl.BlockSpec(
-                    (pl.Element(size), pl.Element(widths[c])), lambda i, at=starts[c]: (0, at)
-                )
+            block = pl.BlockSpec(
+                (pl.Element(size), pl.Element(width)), lambda i, start=start: (0, start)
+            )
             (out,) = line(
                 body,
                 "finish",

time: 88.6 us -> 85.5 us (0.965)
  waiting for transfers between devices: 26.3 us -> 24 us
  Pallas kernels: 22.7 us -> 20.8 us
  starting transfers between devices: 39.1 us -> 40.2 us
    ppermute x5 -> x6, starting transfers between devices: 5.28 us -> 9.08 us  [turned(): lax.ppermute(value, axis, [((to + step) % size, to) for to in range(size)])]
    ppermute x5 -> x6, waiting for transfers between devices: 3.79 us -> 0.76 us  [turned(): lax.ppermute(value, axis, [((to + step) % size, to) for to in range(size)])]
    ppermute x22 -> x20, starting transfers between devices: 33.8 us -> 31.1 us  [swapped(): return lax.ppermute(value, axis, pairs)]
    pallas_call x31 -> x32, Pallas kernels: 22.7 us -> 20.8 us  [__call__(): pl.pallas_call(kernel, grid=grid, out_shape=out_shape, in_specs=in_specs,...]
    ppermute x22 -> x20, waiting for transfers between devices: 22.6 us -> 23.3 us  [swapped(): return lax.ppermute(value, axis, pairs)]
  transfers between devices with their start and end apart: 27 -> 26, of which waited for: 10 -> 8; matrix products, arithmetic and copies ran while one was open for 0% -> 0% of each run, Pallas kernels for 24% -> 23%
where the time goes in v3:
time: 85.5 us; the launch traced here: 85.3 us
  starting transfers between devices  40.2 us (47%)
  waiting for transfers between devices  24 us (28%)
  Pallas kernels  20.8 us (24%)
    ppermute x20, starting transfers between devices, swapped(): return lax.ppermute(value, axis, pairs)  31.1 us
    ppermute x20, waiting for transfers between devices, swapped(): return lax.ppermute(value, axis, pairs)  23.3 us
    pallas_call x32, Pallas kernels, __call__(): pl.pallas_call(kernel, grid=grid, out_shape=out_shape, in_specs=in_specs,...  20.8 us
    ppermute x6, starting transfers between devices, turned(): lax.ppermute(value, axis, [((to + step) % size, to) for to in range(size)])  9.08 us
  transfers between devices with their start and end apart: 26, of which 8 were waited for; matrix products, arithmetic and copies ran while one was open for 0% of the time, Pallas kernels for 23%

profile of v3, /device:TPU:0, one launch (start us, length us, event | category | flops | bytes accessed | tf_op | source)
XLA Modules:
  0.0 85.3 jit_solution(15486433621858746759)
XLA Ops:
  0.0 3.0 %collective-permute-start = (f32[512,128]{1,0:T(8,128)}, f32[512,128]{1,0:T(8,128)S(1)}, u32[]{:S(2)}, u32[]{:S(2)}) collective-permute-start(f32[512,128]{1,0:T(8,128)} %refs_0_.4), channel_id=1, source_target_pairs={{1,0},{0,1},{3,2},{2,3},{5,4},{4,5},{7,6},{6,7},{9,8},{8,9},{11,10... | collective-permute-start | bytes 786440 | tf_op jit(solution)/shard_map/ppermute | solution.py:41
  3.0 1.1 %pick.1 = (f32[256,128]{1,0:T(8,128)S(1)}, f32[256,128]{1,0:T(8,128)S(1)}, f32[256,128]{1,0:T(8,128)S(1)}, f32[256,128]{1,0:T(8,128)S(1)}, f32[8,128]{1,0:T(8,128)S(1)}) custom-call(f32[4,256,128]{2,1,0:T(8,128)} %refs_0_.3, f32[4,256,128]{2,1,0:T(8,128)} %refs_1_.1), custom_call_target="tpu_custom_call" | custom-call | flops 12664080384 | bytes 40590000 | tf_op jit(solution)/shard_map/pick/pallas_call | solution.py:131
  4.2 2.0 %collective-permute-start.2 = (f32[256,128]{1,0:T(8,128)S(1)}, f32[256,128]{1,0:T(8,128)S(1)}, u32[]{:S(2)}, u32[]{:S(2)}) collective-permute-start(f32[256,128]{1,0:T(8,128)S(1)} %get-tuple-element.115.refs_7_), channel_id=1, source_target_pairs={{0,4},{2,6},{4,0},{6,2},{8,12},{10,14},{12,8},{14,10},{16,20},{18,... | collective-permute-start | bytes 393224 | tf_op jit(solution)/shard_map/ppermute | solution.py:35
  6.2 1.6 %collective-permute-start.3 = (f32[256,128]{1,0:T(8,128)S(1)}, f32[256,128]{1,0:T(8,128)S(1)}, u32[]{:S(2)}, u32[]{:S(2)}) collective-permute-start(f32[256,128]{1,0:T(8,128)S(1)} %get-tuple-element.116.refs_9_), channel_id=1, source_target_pairs={{0,8},{2,10},{4,12},{6,14},{8,0},{10,2},{12,4},{14,6},{16,24},{18,... | collective-permute-start | bytes 393224 | tf_op jit(solution)/shard_map/ppermute | solution.py:35
  7.7 2.6 %collective-permute-start.6 = (f32[256,128]{1,0:T(8,128)S(1)}, f32[256,128]{1,0:T(8,128)S(1)}, u32[]{:S(2)}, u32[]{:S(2)}) collective-permute-start(f32[256,128]{1,0:T(8,128)S(1)} %get-tuple-element.120.refs_2_), channel_id=1, source_target_pairs={{0,16},{2,18},{4,20},{6,22},{8,24},{10,26},{12,28},{14,30},{16,0},... | collective-permute-start | bytes 393224 | tf_op jit(solution)/shard_map/ppermute | solution.py:35
  10.9 2.1 %collective-permute-start.5 = (f32[256,128]{1,0:T(8,128)S(1)}, f32[256,128]{1,0:T(8,128)S(1)}, u32[]{:S(2)}, u32[]{:S(2)}) collective-permute-start(f32[256,128]{1,0:T(8,128)S(1)} %get-tuple-element.119.refs_0_), channel_id=1, source_target_pairs={{1,0},{0,1},{3,2},{2,3},{5,4},{4,5},{7,6},{6,7},{9,8},{8,9},{11,10... | collective-permute-start | bytes 393224 | tf_op jit(solution)/shard_map/ppermute | solution.py:41
  13.0 0.9 %later.1 = (bf16[256,768]{1,0:T(8,128)(2,1)S(1)}, bf16[256,768]{1,0:T(8,128)(2,1)S(1)}, f32[8,128]{1,0:T(8,128)S(1)}) custom-call(bf16[256,512]{1,0:T(8,128)(2,1)S(1)} %get-tuple-element.103.refs_0_, bf16[256,512]{1,0:T(8,128)(2,1)S(1)} %get-tuple-element.104.refs_1_, f32[512,1024]{1,0:T(8,128)S(1)} %copy-done, f32[8,128]{1,0:T(8,128)S(1)} %get-tuple-element.105.refs_3_), custom_call_target="tpu_custom_call" | custom-call | flops 27630718976 | bytes 88560000 | tf_op jit(solution)/shard_map/later/pallas_call | solution.py:131
  13.9 0.8 first.1
  14.8 1.1 %tops.1 = (f32[768,256]{1,0:T(8,128)S(1)}, bf16[256,768]{1,0:T(8,128)(2,1)S(1)}, bf16[256,768]{1,0:T(8,128)(2,1)S(1)}, f32[512,128]{1,0:T(8,128)S(1)}, f32[512,128]{1,0:T(8,128)S(1)}, /*index=5*/f32[8,128]{1,0:T(8,128)S(1)}) custom-call(bf16[256,768]{1,0:T(8,128)(2,1)S(1)} %get-tuple-element.106.refs_0_, bf16[256,768]{1,0:T(8,128)(2,1)S(1)} %get-tuple-element.107.refs_1_, ...), custom_call_target="tpu_custom_call" | custom-call | flops 11512800256 | bytes 36900000 | tf_op jit(solution)/shard_map/tops/pallas_call | solution.py:131
  16.6 1.9 %collective-permute-start.10 = (f32[512,128]{1,0:T(8,128)S(1)}, f32[512,128]{1,0:T(8,128)S(1)}, u32[]{:S(2)}, u32[]{:S(2)}) collective-permute-start(f32[512,128]{1,0:T(8,128)S(1)} %get-tuple-element.134.refs_0_), channel_id=1, source_target_pairs={{1,0},{0,1},{3,2},{2,3},{5,4},{4,5},{7,6},{6,7},{9,8},{8,9},{11,10... | collective-permute-start | bytes 786440 | tf_op jit(solution)/shard_map/ppermute | solution.py:41
  19.2 1.6 %collective-permute-start.9 = (f32[128,256]{1,0:T(8,128)S(1)}, f32[128,256]{1,0:T(8,128)S(1)}, u32[]{:S(2)}, u32[]{:S(2)}) collective-permute-start(f32[128,256]{1,0:T(8,128)S(1)} %get-tuple-element.133.refs_0_), channel_id=1, source_target_pairs={{0,4},{2,6},{4,0},{6,2},{8,12},{10,14},{12,8},{14,10},{16,20},{18,... | collective-permute-start | bytes 393224 | tf_op jit(solution)/shard_map/ppermute | solution.py:35
  21.2 0.6 collective-permute-start.14
  21.8 1.0 %collective-permute-start.12 = (f32[512,128]{1,0:T(8,128)S(1)}, f32[512,128]{1,0:T(8,128)S(1)}, u32[]{:S(2)}, u32[]{:S(2)}) collective-permute-start(f32[512,128]{1,0:T(8,128)S(1)} %get-tuple-element.144.refs_0_), channel_id=1, source_target_pairs={{1,0},{0,1},{3,2},{2,3},{5,4},{4,5},{7,6},{6,7},{9,8},{8,9},{11,10... | collective-permute-start | bytes 786440 | tf_op jit(solution)/shard_map/ppermute | solution.py:41
  22.9 0.6 combine.16
  23.5 1.6 %collective-permute-start.13 = (f32[256,256]{1,0:T(8,128)S(1)}, f32[256,256]{1,0:T(8,128)S(1)}, u32[]{:S(2)}, u32[]{:S(2)}) collective-permute-start(f32[256,256]{1,0:T(8,128)S(1)} %get-tuple-element.146.refs_0_), channel_id=1, source_target_pairs={{0,4},{2,6},{4,0},{6,2},{8,12},{10,14},{12,8},{14,10},{16,20},{18,... | collective-permute-start | bytes 786440 | tf_op jit(solution)/shard_map/ppermute | solution.py:35
  25.1 0.7 collective-permute-done.10.refs_1_
  26.4 2.1 %collective-permute-start.11 = (f32[128,256]{1,0:T(8,128)S(1)}, f32[128,256]{1,0:T(8,128)S(1)}, u32[]{:S(2)}, u32[]{:S(2)}) collective-permute-start(f32[128,256]{1,0:T(8,128)S(1)} %get-tuple-element.143.refs_0_), channel_id=1, source_target_pairs={{0,8},{2,10},{4,12},{6,14},{8,0},{10,2},{12,4},{14,6},{16,24},{18,... | collective-permute-start | bytes 393224 | tf_op jit(solution)/shard_map/ppermute | solution.py:35
  28.9 1.5 %collective-permute-start.15 = (f32[128,256]{1,0:T(8,128)S(1)}, f32[128,256]{1,0:T(8,128)S(1)}, u32[]{:S(2)}, u32[]{:S(2)}) collective-permute-start(f32[128,256]{1,0:T(8,128)S(1)} %get-tuple-element.154.refs_2_), channel_id=1, source_target_pairs={{0,8},{2,10},{4,12},{6,14},{8,0},{10,2},{12,4},{14,6},{16,24},{18,... | collective-permute-start | bytes 393224 | tf_op jit(solution)/shard_map/ppermute | solution.py:35
  30.5 0.6 combine.19
  31.1 1.9 %collective-permute-start.19 = (f32[256,256]{1,0:T(8,128)S(1)}, f32[256,256]{1,0:T(8,128)S(1)}, u32[]{:S(2)}, u32[]{:S(2)}) collective-permute-start(f32[256,256]{1,0:T(8,128)S(1)} %get-tuple-element.164.refs_0_), channel_id=1, source_target_pairs={{0,4},{2,6},{4,0},{6,2},{8,12},{10,14},{12,8},{14,10},{16,20},{18,... | collective-permute-start | bytes 786440 | tf_op jit(solution)/shard_map/ppermute | solution.py:35
  33.0 1.0 %collective-permute-done.13.refs_1_ = f32[256,256]{1,0:T(8,128)S(1)} collective-permute-done((f32[256,256]{1,0:T(8,128)S(1)}, f32[256,256]{1,0:T(8,128)S(1)}, u32[]{:S(2)}, u32[]{:S(2)}) %collective-permute-start.13) | collective-permute-done | bytes 262176 | tf_op jit(solution)/shard_map/ppermute | solution.py:35
  34.0 0.6 combine.20
  34.6 1.6 %collective-permute-start.18 = (f32[256,256]{1,0:T(8,128)S(1)}, f32[256,256]{1,0:T(8,128)S(1)}, u32[]{:S(2)}, u32[]{:S(2)}) collective-permute-start(f32[256,256]{1,0:T(8,128)S(1)} %get-tuple-element.163.refs_0_), channel_id=1, source_target_pairs={{0,8},{2,10},{4,12},{6,14},{8,0},{10,2},{12,4},{14,6},{16,24},{18,... | collective-permute-start | bytes 786440 | tf_op jit(solution)/shard_map/ppermute | solution.py:35
  36.5 0.6 combine.21
  37.1 2.7 %collective-permute-start.17 = (f32[256,256]{1,0:T(8,128)S(1)}, f32[256,256]{1,0:T(8,128)S(1)}, u32[]{:S(2)}, u32[]{:S(2)}) collective-permute-start(f32[256,256]{1,0:T(8,128)S(1)} %get-tuple-element.162.refs_0_), channel_id=1, source_target_pairs={{0,16},{2,18},{4,20},{6,22},{8,24},{10,26},{12,28},{14,30},{16,0},... | collective-permute-start | bytes 786440 | tf_op jit(solution)/shard_map/ppermute | solution.py:35
  39.8 1.0 %collective-permute-start.20 = (f32[512,128]{1,0:T(8,128)S(1)}, f32[512,128]{1,0:T(8,128)S(1)}, u32[]{:S(2)}, u32[]{:S(2)}) collective-permute-start(f32[512,128]{1,0:T(8,128)S(1)} %get-tuple-element.169.refs_0_), channel_id=1, source_target_pairs={{1,0},{0,1},{3,2},{2,3},{5,4},{4,5},{7,6},{6,7},{9,8},{8,9},{11,10... | collective-permute-start | bytes 786440 | tf_op jit(solution)/shard_map/ppermute | solution.py:41
  40.8 0.6 combine.22
  41.4 1.9 %collective-permute-start.16 = (f32[256,256]{1,0:T(8,128)S(1)}, f32[256,256]{1,0:T(8,128)S(1)}, u32[]{:S(2)}, u32[]{:S(2)}) collective-permute-start(f32[256,256]{1,0:T(8,128)S(1)} %get-tuple-element.161.refs_0_), channel_id=1, source_target_pairs={{0,4},{2,6},{4,0},{6,2},{8,12},{10,14},{12,8},{14,10},{16,20},{18,... | collective-permute-start | bytes 786440 | tf_op jit(solution)/shard_map/ppermute | solution.py:35
  43.3 0.6 combine.23
  44.0 0.6 collective-permute-start.23
  44.6 1.9 %collective-permute-done.18.refs_1_ = f32[256,256]{1,0:T(8,128)S(1)} collective-permute-done((f32[256,256]{1,0:T(8,128)S(1)}, f32[256,256]{1,0:T(8,128)S(1)}, u32[]{:S(2)}, u32[]{:S(2)}) %collective-permute-start.18) | collective-permute-done | bytes 262176 | tf_op jit(solution)/shard_map/ppermute | solution.py:35
  46.4 0.6 combine.24
  47.1 2.9 %collective-permute-start.22 = (f32[256,256]{1,0:T(8,128)S(1)}, f32[256,256]{1,0:T(8,128)S(1)}, u32[]{:S(2)}, u32[]{:S(2)}) collective-permute-start(f32[256,256]{1,0:T(8,128)S(1)} %get-tuple-element.184.refs_0_), channel_id=1, source_target_pairs={{0,16},{2,18},{4,20},{6,22},{8,24},{10,26},{12,28},{14,30},{16,0},... | collective-permute-start | bytes 786440 | tf_op jit(solution)/shard_map/ppermute | solution.py:35
  50.6 1.5 %rest.1 = (f32[512,1024]{1,0:T(8,128)}, f32[8,128]{1,0:T(8,128)S(1)}) custom-call(f32[512,1024]{1,0:T(8,128)S(1)} %copy-done, bf16[512,256]{1,0:T(8,128)(2,1)S(1)} %get-tuple-element.108.refs_2_.refs_1_, bf16[512,256]{1,0:T(8,128)(2,1)S(1)} %get-tuple-element.109.refs_3_.refs_2_, bf16[256,256]{1,0:T(8,128)(2,1)S(1)} %get-tuple-element.175.refs_3_, ...), custom_call_target="tpu_custom_call" | custom-call | flops 19571759104 | bytes 62730000 | tf_op jit(solution)/shard_map/rest/pallas_call | solution.py:131
  52.2 1.5 %finish.4 = (f32[512,1024]{1,0:T(8,128)}, f32[8,128]{1,0:T(8,128)S(1)}) custom-call(f32[256,256]{1,0:T(8,128)S(1)} %get-tuple-element.162.refs_0_, f32[256,256]{1,0:T(8,128)S(1)} %get-tuple-element.168.refs_1_, bf16[256,256]{1,0:T(8,128)(2,1)S(1)} %get-tuple-element.171.refs_2_, ...), custom_call_target="tpu_custom_call", output_to_operand_aliasing={{0}: (7, {})} | custom-call | flops 14966639616 | bytes 47970000 | tf_op jit(solution)/shard_map/finish/pallas_call | solution.py:131
  53.6 0.8 combine.25
  54.4 2.8 %collective-permute-start.21 = (f32[256,256]{1,0:T(8,128)S(1)}, f32[256,256]{1,0:T(8,128)S(1)}, u32[]{:S(2)}, u32[]{:S(2)}) collective-permute-start(f32[256,256]{1,0:T(8,128)S(1)} %get-tuple-element.183.refs_0_), channel_id=1, source_target_pairs={{0,8},{2,10},{4,12},{6,14},{8,0},{10,2},{12,4},{14,6},{16,24},{18,... | collective-permute-start | bytes 786440 | tf_op jit(solution)/shard_map/ppermute | solution.py:35
  57.3 1.7 %collective-permute-done.23.refs_1_ = f32[256,256]{1,0:T(8,128)S(1)} collective-permute-done((f32[256,256]{1,0:T(8,128)S(1)}, f32[256,256]{1,0:T(8,128)S(1)}, u32[]{:S(2)}, u32[]{:S(2)}) %collective-permute-start.23) | collective-permute-done | bytes 262176 | tf_op jit(solution)/shard_map/ppermute | solution.py:35
  59.0 0.6 combine.26
  59.6 1.8 %collective-permute-start.25 = (f32[256,256]{1,0:T(8,128)S(1)}, f32[256,256]{1,0:T(8,128)S(1)}, u32[]{:S(2)}, u32[]{:S(2)}) collective-permute-start(f32[256,256]{1,0:T(8,128)S(1)} %get-tuple-element.191.refs_0_), channel_id=1, source_target_pairs={{0,16},{2,18},{4,20},{6,22},{8,24},{10,26},{12,28},{14,30},{16,0},... | collective-permute-start | bytes 786440 | tf_op jit(solution)/shard_map/ppermute | solution.py:35
  61.4 1.5 %finish.5 = (f32[512,1024]{1,0:T(8,128)}, f32[8,128]{1,0:T(8,128)S(1)}) custom-call(f32[256,256]{1,0:T(8,128)S(1)} %get-tuple-element.184.refs_0_, f32[256,256]{1,0:T(8,128)S(1)} %collective-permute-done.22.refs_1_, bf16[256,256]{1,0:T(8,128)(2,1)S(1)} %get-tuple-element.171.refs_2_, ...), custom_call_target="tpu_custom_call", output_to_operand_aliasing={{0}: (7, {})} | custom-call | flops 14966639616 | bytes 47970000 | tf_op jit(solution)/shard_map/finish/pallas_call | solution.py:131
  62.9 5.5 %collective-permute-done.21.refs_1_ = f32[256,256]{1,0:T(8,128)S(1)} collective-permute-done((f32[256,256]{1,0:T(8,128)S(1)}, f32[256,256]{1,0:T(8,128)S(1)}, u32[]{:S(2)}, u32[]{:S(2)}) %collective-permute-start.21) | collective-permute-done | bytes 262176 | tf_op jit(solution)/shard_map/ppermute | solution.py:35
  68.3 0.6 combine.27
  68.9 0.7 collective-permute-start.24
  69.7 9.5 %collective-permute-done.25.refs_1_ = f32[256,256]{1,0:T(8,128)S(1)} collective-permute-done((f32[256,256]{1,0:T(8,128)S(1)}, f32[256,256]{1,0:T(8,128)S(1)}, u32[]{:S(2)}, u32[]{:S(2)}) %collective-permute-start.25) | collective-permute-done | bytes 262176 | tf_op jit(solution)/shard_map/ppermute | solution.py:35
  79.2 1.5 %finish.6 = (f32[512,1024]{1,0:T(8,128)}, f32[8,128]{1,0:T(8,128)S(1)}) custom-call(f32[256,256]{1,0:T(8,128)S(1)} %get-tuple-element.191.refs_0_, f32[256,256]{1,0:T(8,128)S(1)} %collective-permute-done.25.refs_1_, bf16[256,256]{1,0:T(8,128)(2,1)S(1)} %get-tuple-element.171.refs_2_, ...), custom_call_target="tpu_custom_call", output_to_operand_aliasing={{0}: (7, {})} | custom-call | flops 14966639616 | bytes 47970000 | tf_op jit(solution)/shard_map/finish/pallas_call | solution.py:131
  80.7 3.2 %collective-permute-done.24.refs_1_ = f32[256,256]{1,0:T(8,128)S(1)} collective-permute-done((f32[256,256]{1,0:T(8,128)S(1)}, f32[256,256]{1,0:T(8,128)S(1)}, u32[]{:S(2)}, u32[]{:S(2)}) %collective-permute-start.24) | collective-permute-done | bytes 262176 | tf_op jit(solution)/shard_map/ppermute | solution.py:35
  83.9 1.5 %finish.7 = (f32[512,1024]{1,0:T(8,128)}, f32[8,128]{1,0:T(8,128)}) custom-call(f32[256,256]{1,0:T(8,128)S(1)} %get-tuple-element.190.refs_0_, f32[256,256]{1,0:T(8,128)S(1)} %collective-permute-done.24.refs_1_, bf16[256,256]{1,0:T(8,128)(2,1)S(1)} %get-tuple-element.171.refs_2_, ...), custom_call_target="tpu_custom_call", output_to_operand_aliasing={{0}: (7, {})} | custom-call | flops 14966639616 | bytes 47970000 | tf_op jit(solution)/shard_map/finish/pallas_call | solution.py:131
  (42 shorter events, 4.4 us)
Async XLA Ops:
  0.0 10.4 %copy-start.1 = (f32[512,128]{1,0:T(8,128)S(1)}, f32[512,128]{1,0:T(8,128)}, u32[]{:S(2)}) copy-start(f32[512,128]{1,0:T(8,128)} %refs_0_.4) | copy-start | bytes 786436
  0.0 10.4 %copy-start = (f32[512,1024]{1,0:T(8,128)S(1)}, f32[512,1024]{1,0:T(8,128)}, u32[]{:S(2)}) copy-start(f32[512,1024]{1,0:T(8,128)} %refs_0_.5) | copy-start | bytes 6291460
  0.0 10.4 %collective-permute-start = (f32[512,128]{1,0:T(8,128)}, f32[512,128]{1,0:T(8,128)S(1)}, u32[]{:S(2)}, u32[]{:S(2)}) collective-permute-start(f32[512,128]{1,0:T(8,128)} %refs_0_.4), channel_id=1, source_target_pairs={{1,0},{0,1},{3,2},{2,3},{5,4},{4,5},{7,6},{6,7},{9,8},{8,9},{11,10... | collective-permute-start | bytes 786440 | tf_op jit(solution)/shard_map/ppermute | solution.py:41
  3.0 10.9 %collective-permute-start.1 = (f32[256,128]{1,0:T(8,128)}, f32[256,128]{1,0:T(8,128)S(1)}, u32[]{:S(2)}, u32[]{:S(2)}) collective-permute-start(f32[256,128]{1,0:T(8,128)} %refs_5_.1), channel_id=1, source_target_pairs={{1,0},{0,1},{3,2},{2,3},{5,4},{4,5},{7,6},{6,7},{9,8},{8,9},{11,10... | collective-permute-start | bytes 393224 | tf_op jit(solution)/shard_map/ppermute | solution.py:41
  4.2 10.6 %collective-permute-start.2 = (f32[256,128]{1,0:T(8,128)S(1)}, f32[256,128]{1,0:T(8,128)S(1)}, u32[]{:S(2)}, u32[]{:S(2)}) collective-permute-start(f32[256,128]{1,0:T(8,128)S(1)} %get-tuple-element.115.refs_7_), channel_id=1, source_target_pairs={{0,4},{2,6},{4,0},{6,2},{8,12},{10,14},{12,8},{14,10},{16,20},{18,... | collective-permute-start | bytes 393224 | tf_op jit(solution)/shard_map/ppermute | solution.py:35
  6.2 8.6 %collective-permute-start.3 = (f32[256,128]{1,0:T(8,128)S(1)}, f32[256,128]{1,0:T(8,128)S(1)}, u32[]{:S(2)}, u32[]{:S(2)}) collective-permute-start(f32[256,128]{1,0:T(8,128)S(1)} %get-tuple-element.116.refs_9_), channel_id=1, source_target_pairs={{0,8},{2,10},{4,12},{6,14},{8,0},{10,2},{12,4},{14,6},{16,24},{18,... | collective-permute-start | bytes 393224 | tf_op jit(solution)/shard_map/ppermute | solution.py:35
  7.7 8.2 %collective-permute-start.6 = (f32[256,128]{1,0:T(8,128)S(1)}, f32[256,128]{1,0:T(8,128)S(1)}, u32[]{:S(2)}, u32[]{:S(2)}) collective-permute-start(f32[256,128]{1,0:T(8,128)S(1)} %get-tuple-element.120.refs_2_), channel_id=1, source_target_pairs={{0,16},{2,18},{4,20},{6,22},{8,24},{10,26},{12,28},{14,30},{16,0},... | collective-permute-start | bytes 393224 | tf_op jit(solution)/shard_map/ppermute | solution.py:35
  10.9 5.0 %collective-permute-start.5 = (f32[256,128]{1,0:T(8,128)S(1)}, f32[256,128]{1,0:T(8,128)S(1)}, u32[]{:S(2)}, u32[]{:S(2)}) collective-permute-start(f32[256,128]{1,0:T(8,128)S(1)} %get-tuple-element.119.refs_0_), channel_id=1, source_target_pairs={{1,0},{0,1},{3,2},{2,3},{5,4},{4,5},{7,6},{6,7},{9,8},{8,9},{11,10... | collective-permute-start | bytes 393224 | tf_op jit(solution)/shard_map/ppermute | solution.py:41
  13.0 0.9 %copy-start.2 = (f32[256,128]{1,0:T(8,128)S(1)}, f32[256,128]{1,0:T(8,128)}, u32[]{:S(2)}) copy-start(f32[256,128]{1,0:T(8,128)} %refs_5_.1) | copy-start | bytes 393220
  14.7 3.9 %collective-permute-start.8 = (f32[256,256]{1,0:T(8,128)S(1)}, f32[256,256]{1,0:T(8,128)S(1)}, u32[]{:S(2)}, u32[]{:S(2)}) collective-permute-start(f32[256,256]{1,0:T(8,128)S(1)} %get-tuple-element.124.refs_0_), channel_id=1, source_target_pairs={{0,2},{2,0},{4,6},{6,4},{8,10},{10,8},{12,14},{14,12},{16,18},{18,... | collective-permute-start | bytes 786440 | tf_op jit(solution)/shard_map/ppermute | solution.py:35
  16.0 2.6 %collective-permute-start.7 = (f32[256,256]{1,0:T(8,128)S(1)}, f32[256,256]{1,0:T(8,128)S(1)}, u32[]{:S(2)}, u32[]{:S(2)}) collective-permute-start(f32[256,256]{1,0:T(8,128)S(1)} %get-tuple-element.122.refs_0_), channel_id=1, source_target_pairs={{0,2},{2,0},{4,6},{6,4},{8,10},{10,8},{12,14},{14,12},{16,18},{18,... | collective-permute-start | bytes 786440 | tf_op jit(solution)/shard_map/ppermute | solution.py:35
  16.6 6.3 %collective-permute-start.4 = (f32[768,256]{1,0:T(8,128)S(1)}, f32[768,256]{1,0:T(8,128)S(1)}, u32[]{:S(2)}, u32[]{:S(2)}) collective-permute-start(f32[768,256]{1,0:T(8,128)S(1)} %get-tuple-element.118.refs_0_), channel_id=1, source_target_pairs={{0,2},{2,0},{4,6},{6,4},{8,10},{10,8},{12,14},{14,12},{16,18},{18,... | collective-permute-start | bytes 2359304 | tf_op jit(solution)/shard_map/ppermute | solution.py:35
  16.6 9.1 %collective-permute-start.10 = (f32[512,128]{1,0:T(8,128)S(1)}, f32[512,128]{1,0:T(8,128)S(1)}, u32[]{:S(2)}, u32[]{:S(2)}) collective-permute-start(f32[512,128]{1,0:T(8,128)S(1)} %get-tuple-element.134.refs_0_), channel_id=1, source_target_pairs={{1,0},{0,1},{3,2},{2,3},{5,4},{4,5},{7,6},{6,7},{9,8},{8,9},{11,10... | collective-permute-start | bytes 786440 | tf_op jit(solution)/shard_map/ppermute | solution.py:41
  19.2 6.7 %collective-permute-start.9 = (f32[128,256]{1,0:T(8,128)S(1)}, f32[128,256]{1,0:T(8,128)S(1)}, u32[]{:S(2)}, u32[]{:S(2)}) collective-permute-start(f32[128,256]{1,0:T(8,128)S(1)} %get-tuple-element.133.refs_0_), channel_id=1, source_target_pairs={{0,4},{2,6},{4,0},{6,2},{8,12},{10,14},{12,8},{14,10},{16,20},{18,... | collective-permute-start | bytes 393224 | tf_op jit(solution)/shard_map/ppermute | solution.py:35
  21.2 7.2 %collective-permute-start.14 = (f32[128,256]{1,0:T(8,128)S(1)}, f32[128,256]{1,0:T(8,128)S(1)}, u32[]{:S(2)}, u32[]{:S(2)}) collective-permute-start(f32[128,256]{1,0:T(8,128)S(1)} %get-tuple-element.147.refs_0_), channel_id=1, source_target_pairs={{0,4},{2,6},{4,0},{6,2},{8,12},{10,14},{12,8},{14,10},{16,20},{18,... | collective-permute-start | bytes 393224 | tf_op jit(solution)/shard_map/ppermute | solution.py:35
  21.8 14.4 %collective-permute-start.12 = (f32[512,128]{1,0:T(8,128)S(1)}, f32[512,128]{1,0:T(8,128)S(1)}, u32[]{:S(2)}, u32[]{:S(2)}) collective-permute-start(f32[512,128]{1,0:T(8,128)S(1)} %get-tuple-element.144.refs_0_), channel_id=1, source_target_pairs={{1,0},{0,1},{3,2},{2,3},{5,4},{4,5},{7,6},{6,7},{9,8},{8,9},{11,10... | collective-permute-start | bytes 786440 | tf_op jit(solution)/shard_map/ppermute | solution.py:41
  23.5 10.5 %collective-permute-start.13 = (f32[256,256]{1,0:T(8,128)S(1)}, f32[256,256]{1,0:T(8,128)S(1)}, u32[]{:S(2)}, u32[]{:S(2)}) collective-permute-start(f32[256,256]{1,0:T(8,128)S(1)} %get-tuple-element.146.refs_0_), channel_id=1, source_target_pairs={{0,4},{2,6},{4,0},{6,2},{8,12},{10,14},{12,8},{14,10},{16,20},{18,... | collective-permute-start | bytes 786440 | tf_op jit(solution)/shard_map/ppermute | solution.py:35
  26.4 10.1 %collective-permute-start.11 = (f32[128,256]{1,0:T(8,128)S(1)}, f32[128,256]{1,0:T(8,128)S(1)}, u32[]{:S(2)}, u32[]{:S(2)}) collective-permute-start(f32[128,256]{1,0:T(8,128)S(1)} %get-tuple-element.143.refs_0_), channel_id=1, source_target_pairs={{0,8},{2,10},{4,12},{6,14},{8,0},{10,2},{12,4},{14,6},{16,24},{18,... | collective-permute-start | bytes 393224 | tf_op jit(solution)/shard_map/ppermute | solution.py:35
  28.9 7.5 %collective-permute-start.15 = (f32[128,256]{1,0:T(8,128)S(1)}, f32[128,256]{1,0:T(8,128)S(1)}, u32[]{:S(2)}, u32[]{:S(2)}) collective-permute-start(f32[128,256]{1,0:T(8,128)S(1)} %get-tuple-element.154.refs_2_), channel_id=1, source_target_pairs={{0,8},{2,10},{4,12},{6,14},{8,0},{10,2},{12,4},{14,6},{16,24},{18,... | collective-permute-start | bytes 393224 | tf_op jit(solution)/shard_map/ppermute | solution.py:35
  31.1 12.3 %collective-permute-start.19 = (f32[256,256]{1,0:T(8,128)S(1)}, f32[256,256]{1,0:T(8,128)S(1)}, u32[]{:S(2)}, u32[]{:S(2)}) collective-permute-start(f32[256,256]{1,0:T(8,128)S(1)} %get-tuple-element.164.refs_0_), channel_id=1, source_target_pairs={{0,4},{2,6},{4,0},{6,2},{8,12},{10,14},{12,8},{14,10},{16,20},{18,... | collective-permute-start | bytes 786440 | tf_op jit(solution)/shard_map/ppermute | solution.py:35
  34.6 11.8 %collective-permute-start.18 = (f32[256,256]{1,0:T(8,128)S(1)}, f32[256,256]{1,0:T(8,128)S(1)}, u32[]{:S(2)}, u32[]{:S(2)}) collective-permute-start(f32[256,256]{1,0:T(8,128)S(1)} %get-tuple-element.163.refs_0_), channel_id=1, source_target_pairs={{0,8},{2,10},{4,12},{6,14},{8,0},{10,2},{12,4},{14,6},{16,24},{18,... | collective-permute-start | bytes 786440 | tf_op jit(solution)/shard_map/ppermute | solution.py:35
  37.1 13.3 %collective-permute-start.17 = (f32[256,256]{1,0:T(8,128)S(1)}, f32[256,256]{1,0:T(8,128)S(1)}, u32[]{:S(2)}, u32[]{:S(2)}) collective-permute-start(f32[256,256]{1,0:T(8,128)S(1)} %get-tuple-element.162.refs_0_), channel_id=1, source_target_pairs={{0,16},{2,18},{4,20},{6,22},{8,24},{10,26},{12,28},{14,30},{16,0},... | collective-permute-start | bytes 786440 | tf_op jit(solution)/shard_map/ppermute | solution.py:35
  39.8 10.7 %collective-permute-start.20 = (f32[512,128]{1,0:T(8,128)S(1)}, f32[512,128]{1,0:T(8,128)S(1)}, u32[]{:S(2)}, u32[]{:S(2)}) collective-permute-start(f32[512,128]{1,0:T(8,128)S(1)} %get-tuple-element.169.refs_0_), channel_id=1, source_target_pairs={{1,0},{0,1},{3,2},{2,3},{5,4},{4,5},{7,6},{6,7},{9,8},{8,9},{11,10... | collective-permute-start | bytes 786440 | tf_op jit(solution)/shard_map/ppermute | solution.py:41
  41.4 12.2 %collective-permute-start.16 = (f32[256,256]{1,0:T(8,128)S(1)}, f32[256,256]{1,0:T(8,128)S(1)}, u32[]{:S(2)}, u32[]{:S(2)}) collective-permute-start(f32[256,256]{1,0:T(8,128)S(1)} %get-tuple-element.161.refs_0_), channel_id=1, source_target_pairs={{0,4},{2,6},{4,0},{6,2},{8,12},{10,14},{12,8},{14,10},{16,20},{18,... | collective-permute-start | bytes 786440 | tf_op jit(solution)/shard_map/ppermute | solution.py:35
  44.0 15.0 %collective-permute-start.23 = (f32[256,256]{1,0:T(8,128)S(1)}, f32[256,256]{1,0:T(8,128)S(1)}, u32[]{:S(2)}, u32[]{:S(2)}) collective-permute-start(f32[256,256]{1,0:T(8,128)S(1)} %get-tuple-element.185.refs_0_), channel_id=1, source_target_pairs={{0,8},{2,10},{4,12},{6,14},{8,0},{10,2},{12,4},{14,6},{16,24},{18,... | collective-permute-start | bytes 786440 | tf_op jit(solution)/shard_map/ppermute | solution.py:35
  47.1 14.3 %collective-permute-start.22 = (f32[256,256]{1,0:T(8,128)S(1)}, f32[256,256]{1,0:T(8,128)S(1)}, u32[]{:S(2)}, u32[]{:S(2)}) collective-permute-start(f32[256,256]{1,0:T(8,128)S(1)} %get-tuple-element.184.refs_0_), channel_id=1, source_target_pairs={{0,16},{2,18},{4,20},{6,22},{8,24},{10,26},{12,28},{14,30},{16,0},... | collective-permute-start | bytes 786440 | tf_op jit(solution)/shard_map/ppermute | solution.py:35
  54.4 13.9 %collective-permute-start.21 = (f32[256,256]{1,0:T(8,128)S(1)}, f32[256,256]{1,0:T(8,128)S(1)}, u32[]{:S(2)}, u32[]{:S(2)}) collective-permute-start(f32[256,256]{1,0:T(8,128)S(1)} %get-tuple-element.183.refs_0_), channel_id=1, source_target_pairs={{0,8},{2,10},{4,12},{6,14},{8,0},{10,2},{12,4},{14,6},{16,24},{18,... | collective-permute-start | bytes 786440 | tf_op jit(solution)/shard_map/ppermute | solution.py:35
  59.6 19.6 %collective-permute-start.25 = (f32[256,256]{1,0:T(8,128)S(1)}, f32[256,256]{1,0:T(8,128)S(1)}, u32[]{:S(2)}, u32[]{:S(2)}) collective-permute-start(f32[256,256]{1,0:T(8,128)S(1)} %get-tuple-element.191.refs_0_), channel_id=1, source_target_pairs={{0,16},{2,18},{4,20},{6,22},{8,24},{10,26},{12,28},{14,30},{16,0},... | collective-permute-start | bytes 786440 | tf_op jit(solution)/shard_map/ppermute | solution.py:35
  68.9 14.9 %collective-permute-start.24 = (f32[256,256]{1,0:T(8,128)S(1)}, f32[256,256]{1,0:T(8,128)S(1)}, u32[]{:S(2)}, u32[]{:S(2)}) collective-permute-start(f32[256,256]{1,0:T(8,128)S(1)} %get-tuple-element.190.refs_0_), channel_id=1, source_target_pairs={{0,16},{2,18},{4,20},{6,22},{8,24},{10,26},{12,28},{14,30},{16,0},... | collective-permute-start | bytes 786440 | tf_op jit(solution)/shard_map/ppermute | solution.py:35

commit v4 on v3

--- a/solution.py
+++ b/solution.py
@@ -11,21 +11,18 @@
 bf16 = jnp.bfloat16
 LANES = 128
 VMEM_LIMIT = 32 * 2**20
-MICROSECOND = 3.69e6
-SCALE = 10.0
-
 USUAL = dict(
-    pick=1.1,
-    inner=1.0,
-    later=2.4,
-    first=0.6,
-    tops=1.0,
-    hand=0.1,
-    join=0.1,
-    node=0.15,
-    combine=0.6,
-    rest=1.7,
-    finish=1.3,
+    pick=11.0,
+    inner=10.0,
+    later=24.0,
+    first=6.0,
+    tops=10.0,
+    hand=1.0,
+    join=1.0,
+    node=1.5,
+    combine=6.0,
+    rest=17.0,
+    finish=13.0,
 )
 
 
@@ -138,7 +135,7 @@
             input_output_aliases=aliases,
             compiler_params=pltpu.CompilerParams(vmem_limit_bytes=VMEM_LIMIT),
             cost_estimate=pl.CostEstimate(
-                flops=int(SCALE * 312 * MICROSECOND * USUAL[name]), bytes_accessed=int(SCALE * MICROSECOND * USUAL[name]), transcendentals=0
+                flops=int(USUAL[name] * 1.15e9), bytes_accessed=0, transcendentals=0
             ),
             name=name,
         )(*operands)
@@ -245,36 +242,35 @@
     else:
         own = whole([ref[:size] for ref in ins[:n]])
         partner = whole([ref[size:] for ref in ins[:n]])
-    put(outs[:2], jnp.where(clear, partner, own))
-    put(outs[2:4], triangle(jnp.where(clear, own, partner)))
+    lower = parts(jnp.where(clear, partner, own))
+    upper = triangle(jnp.where(clear, own, partner))
+
+    @pl.when(clear)
+    def _():
+        put(outs[:2], upper)
+        put(outs[2:4], product(lower, parts(upper), plain))
+
+    @pl.when(jnp.logical_not(clear))
+    def _():
+        across_both = product(parts(upper), lower, across)
+        put(outs[:2], product(lower, parts(across_both), plain))
+        put(outs[2:4], across_both)
+
     hand_on(ins[n if section else 2 :], outs[4:])
 
 
-def combine_body(section, last, spans, ins, outs):
+def combine_body(last, spans, ins, outs):
     pairs, node = ins[: 2 * len(spans)], ins[2 * len(spans) :]
 
     def rows_of(refs):
         return jnp.concatenate([ref[at : at + width] for ref, (at, width) in zip(refs, spans)])
 
     mine, other = rows_of(pairs[::2]), rows_of(pairs[1::2])
-    node_y = node[0][...], node[1][...]
-    node_t = node[2][...], node[3][...]
-    clear = lax.axis_index("row") // (1 << section) % 2 == 0
-    leader = jnp.where(clear, mine, other)
-    follower = jnp.where(clear, other, mine)
-    summed = leader + product(parts(follower), node_y, plain)
-    coupling = product(parts(summed), node_t, plain)
-
-    def write(value):
-        outs[0][...] = value.T if last else value
-
-    @pl.when(clear)
-    def _():
-        write(mine - coupling)
-
-    @pl.when(jnp.logical_not(clear))
-    def _():
-        write(mine - product(parts(coupling), node_y, across))
+    by_mine = node[0][...], node[1][...]
+    by_other = node[2][...], node[3][...]
+    change = product(parts(mine), by_mine, plain) + product(parts(other), by_other, plain)
+    result = mine - change
+    outs[0][...] = result.T if last else result
 
 
 def cut(columns, width, ahead=()):
@@ -423,7 +419,7 @@
                 spans.append((low - at, high - low))
         inputs += nodes[s]
         last = s == levels - 1
-        body = functools.partial(combine_body, s, last, spans)
+        body = functools.partial(combine_body, last, spans)
         if not last:
             (top,) = line(body, "combine", inputs, [held(width, size)])
             tops[s + 1].append((start, width, top, swapped(top, "row", s + 1)))
@@ -436,7 +432,9 @@
                     [
                         (
                             jax.ShapeDtypeStruct((rows, columns), f32),
-                            pl.BlockSpec((rows - size, columns), lambda i: (1, 0)),
+                            pl.BlockSpec(
+                                (pl.Element(rows - size), pl.Element(columns)), lambda i: (size, 0)
+                            ),
                         )
                     ],
                 )

time: 85.5 us -> 85.4 us (level)
  waiting for transfers between devices: 24 us -> 29.1 us
  Pallas kernels: 20.8 us -> 17.5 us
  starting transfers between devices: 40.2 us -> 38.3 us
    ppermute x20, waiting for transfers between devices: 23.3 us -> 28 us  [swapped(): return lax.ppermute(value, axis, pairs)]
    pallas_call x32, Pallas kernels: 20.8 us -> 17.5 us  [__call__(): pl.pallas_call(kernel, grid=grid, out_shape=out_shape, in_specs=in_specs,...]
    ppermute x20, starting transfers between devices: 31.1 us -> 29.4 us  [swapped(): return lax.ppermute(value, axis, pairs)]
  transfers between devices with their start and end apart: 26 -> 26, of which waited for: 8 -> 9; matrix products, arithmetic and copies ran while one was open for 0% -> 0% of each run, Pallas kernels for 23% -> 19%
where the time goes in v4:
time: 85.4 us; the launch traced here: 85.3 us
  starting transfers between devices  38.3 us (45%)
  waiting for transfers between devices  29.1 us (34%)
  Pallas kernels  17.5 us (20%)
    ppermute x20, starting transfers between devices, swapped(): return lax.ppermute(value, axis, pairs)  29.4 us
    ppermute x20, waiting for transfers between devices, swapped(): return lax.ppermute(value, axis, pairs)  28 us
    pallas_call x32, Pallas kernels, __call__(): pl.pallas_call(kernel, grid=grid, out_shape=out_shape, in_specs=in_specs,...  17.5 us
    ppermute x6, starting transfers between devices, turned(): lax.ppermute(value, axis, [((to + step) % size, to) for to in range(size)])  8.95 us
  transfers between devices with their start and end apart: 26, of which 9 were waited for; matrix products, arithmetic and copies ran while one was open for 0% of the time, Pallas kernels for 19%

profile of v4, /device:TPU:0, one launch (start us, length us, event | category | flops | bytes accessed | tf_op | source)
XLA Modules:
  0.0 85.3 jit_solution(8833254833901672986)
XLA Ops:
  0.0 3.0 %collective-permute-start = (f32[512,128]{1,0:T(8,128)}, f32[512,128]{1,0:T(8,128)S(1)}, u32[]{:S(2)}, u32[]{:S(2)}) collective-permute-start(f32[512,128]{1,0:T(8,128)} %refs_0_.4), channel_id=1, source_target_pairs={{1,0},{0,1},{3,2},{2,3},{5,4},{4,5},{7,6},{6,7},{9,8},{8,9},{11,10... | collective-permute-start | bytes 786440 | tf_op jit(solution)/shard_map/ppermute | solution.py:38
  3.0 1.1 %pick.1 = (f32[256,128]{1,0:T(8,128)S(1)}, f32[256,128]{1,0:T(8,128)S(1)}, f32[256,128]{1,0:T(8,128)S(1)}, f32[256,128]{1,0:T(8,128)S(1)}, f32[8,128]{1,0:T(8,128)S(1)}) custom-call(f32[4,256,128]{2,1,0:T(8,128)} %refs_0_.3, f32[4,256,128]{2,1,0:T(8,128)} %refs_1_.1), custom_call_target="tpu_custom_call" | custom-call | flops 12650000384 | tf_op jit(solution)/shard_map/pick/pallas_call | solution.py:128
  4.2 2.0 %collective-permute-start.2 = (f32[256,128]{1,0:T(8,128)S(1)}, f32[256,128]{1,0:T(8,128)S(1)}, u32[]{:S(2)}, u32[]{:S(2)}) collective-permute-start(f32[256,128]{1,0:T(8,128)S(1)} %get-tuple-element.115.refs_7_), channel_id=1, source_target_pairs={{0,4},{2,6},{4,0},{6,2},{8,12},{10,14},{12,8},{14,10},{16,20},{18,... | collective-permute-start | bytes 393224 | tf_op jit(solution)/shard_map/ppermute | solution.py:32
  6.2 1.6 %collective-permute-start.3 = (f32[256,128]{1,0:T(8,128)S(1)}, f32[256,128]{1,0:T(8,128)S(1)}, u32[]{:S(2)}, u32[]{:S(2)}) collective-permute-start(f32[256,128]{1,0:T(8,128)S(1)} %get-tuple-element.116.refs_9_), channel_id=1, source_target_pairs={{0,8},{2,10},{4,12},{6,14},{8,0},{10,2},{12,4},{14,6},{16,24},{18,... | collective-permute-start | bytes 393224 | tf_op jit(solution)/shard_map/ppermute | solution.py:32
  7.7 2.6 %collective-permute-start.6 = (f32[256,128]{1,0:T(8,128)S(1)}, f32[256,128]{1,0:T(8,128)S(1)}, u32[]{:S(2)}, u32[]{:S(2)}) collective-permute-start(f32[256,128]{1,0:T(8,128)S(1)} %get-tuple-element.120.refs_2_), channel_id=1, source_target_pairs={{0,16},{2,18},{4,20},{6,22},{8,24},{10,26},{12,28},{14,30},{16,0},... | collective-permute-start | bytes 393224 | tf_op jit(solution)/shard_map/ppermute | solution.py:32
  10.4 0.5 inner.1
  10.9 2.1 %collective-permute-start.5 = (f32[256,128]{1,0:T(8,128)S(1)}, f32[256,128]{1,0:T(8,128)S(1)}, u32[]{:S(2)}, u32[]{:S(2)}) collective-permute-start(f32[256,128]{1,0:T(8,128)S(1)} %get-tuple-element.119.refs_0_), channel_id=1, source_target_pairs={{1,0},{0,1},{3,2},{2,3},{5,4},{4,5},{7,6},{6,7},{9,8},{8,9},{11,10... | collective-permute-start | bytes 393224 | tf_op jit(solution)/shard_map/ppermute | solution.py:38
  13.0 0.9 %later.1 = (bf16[256,768]{1,0:T(8,128)(2,1)S(1)}, bf16[256,768]{1,0:T(8,128)(2,1)S(1)}, f32[8,128]{1,0:T(8,128)S(1)}) custom-call(bf16[256,512]{1,0:T(8,128)(2,1)S(1)} %get-tuple-element.103.refs_0_, bf16[256,512]{1,0:T(8,128)(2,1)S(1)} %get-tuple-element.104.refs_1_, f32[512,1024]{1,0:T(8,128)S(1)} %copy-done, f32[8,128]{1,0:T(8,128)S(1)} %get-tuple-element.105.refs_3_), custom_call_target="tpu_custom_call" | custom-call | flops 27599998976 | tf_op jit(solution)/shard_map/later/pallas_call | solution.py:128
  13.9 0.8 first.1
  14.8 1.1 %tops.1 = (f32[768,256]{1,0:T(8,128)S(1)}, bf16[256,768]{1,0:T(8,128)(2,1)S(1)}, bf16[256,768]{1,0:T(8,128)(2,1)S(1)}, f32[512,128]{1,0:T(8,128)S(1)}, f32[512,128]{1,0:T(8,128)S(1)}, /*index=5*/f32[8,128]{1,0:T(8,128)S(1)}) custom-call(bf16[256,768]{1,0:T(8,128)(2,1)S(1)} %get-tuple-element.106.refs_0_, bf16[256,768]{1,0:T(8,128)(2,1)S(1)} %get-tuple-element.107.refs_1_, ...), custom_call_target="tpu_custom_call" | custom-call | flops 11500000256 | tf_op jit(solution)/shard_map/tops/pallas_call | solution.py:128
  16.0 0.5 collective-permute-start.7
  16.6 1.9 %collective-permute-start.10 = (f32[512,128]{1,0:T(8,128)S(1)}, f32[512,128]{1,0:T(8,128)S(1)}, u32[]{:S(2)}, u32[]{:S(2)}) collective-permute-start(f32[512,128]{1,0:T(8,128)S(1)} %get-tuple-element.134.refs_0_), channel_id=1, source_target_pairs={{1,0},{0,1},{3,2},{2,3},{5,4},{4,5},{7,6},{6,7},{9,8},{8,9},{11,10... | collective-permute-start | bytes 786440 | tf_op jit(solution)/shard_map/ppermute | solution.py:38
  18.6 0.4 node.4
  19.3 1.6 %collective-permute-start.9 = (f32[128,256]{1,0:T(8,128)S(1)}, f32[128,256]{1,0:T(8,128)S(1)}, u32[]{:S(2)}, u32[]{:S(2)}) collective-permute-start(f32[128,256]{1,0:T(8,128)S(1)} %get-tuple-element.133.refs_0_), channel_id=1, source_target_pairs={{0,4},{2,6},{4,0},{6,2},{8,12},{10,14},{12,8},{14,10},{16,20},{18,... | collective-permute-start | bytes 393224 | tf_op jit(solution)/shard_map/ppermute | solution.py:32
  21.2 0.6 collective-permute-start.14
  21.8 1.0 %collective-permute-start.12 = (f32[512,128]{1,0:T(8,128)S(1)}, f32[512,128]{1,0:T(8,128)S(1)}, u32[]{:S(2)}, u32[]{:S(2)}) collective-permute-start(f32[512,128]{1,0:T(8,128)S(1)} %get-tuple-element.144.refs_0_), channel_id=1, source_target_pairs={{1,0},{0,1},{3,2},{2,3},{5,4},{4,5},{7,6},{6,7},{9,8},{8,9},{11,10... | collective-permute-start | bytes 786440 | tf_op jit(solution)/shard_map/ppermute | solution.py:38
  23.1 1.6 %collective-permute-start.13 = (f32[256,256]{1,0:T(8,128)S(1)}, f32[256,256]{1,0:T(8,128)S(1)}, u32[]{:S(2)}, u32[]{:S(2)}) collective-permute-start(f32[256,256]{1,0:T(8,128)S(1)} %get-tuple-element.146.refs_0_), channel_id=1, source_target_pairs={{0,4},{2,6},{4,0},{6,2},{8,12},{10,14},{12,8},{14,10},{16,20},{18,... | collective-permute-start | bytes 786440 | tf_op jit(solution)/shard_map/ppermute | solution.py:32
  24.7 1.0 %collective-permute-done.10.refs_1_ = f32[512,128]{1,0:T(8,128)S(1)} collective-permute-done((f32[512,128]{1,0:T(8,128)S(1)}, f32[512,128]{1,0:T(8,128)S(1)}, u32[]{:S(2)}, u32[]{:S(2)}) %collective-permute-start.10) | collective-permute-done | bytes 262176 | tf_op jit(solution)/shard_map/ppermute | solution.py:38
  25.8 0.4 node.5
  26.5 2.1 %collective-permute-start.11 = (f32[128,256]{1,0:T(8,128)S(1)}, f32[128,256]{1,0:T(8,128)S(1)}, u32[]{:S(2)}, u32[]{:S(2)}) collective-permute-start(f32[128,256]{1,0:T(8,128)S(1)} %get-tuple-element.143.refs_0_), channel_id=1, source_target_pairs={{0,8},{2,10},{4,12},{6,14},{8,0},{10,2},{12,4},{14,6},{16,24},{18,... | collective-permute-start | bytes 393224 | tf_op jit(solution)/shard_map/ppermute | solution.py:32
  28.9 1.6 %collective-permute-start.15 = (f32[128,256]{1,0:T(8,128)S(1)}, f32[128,256]{1,0:T(8,128)S(1)}, u32[]{:S(2)}, u32[]{:S(2)}) collective-permute-start(f32[128,256]{1,0:T(8,128)S(1)} %get-tuple-element.154.refs_2_), channel_id=1, source_target_pairs={{0,8},{2,10},{4,12},{6,14},{8,0},{10,2},{12,4},{14,6},{16,24},{18,... | collective-permute-start | bytes 393224 | tf_op jit(solution)/shard_map/ppermute | solution.py:32
  30.5 0.4 combine.19
  30.8 1.6 %collective-permute-start.19 = (f32[256,256]{1,0:T(8,128)S(1)}, f32[256,256]{1,0:T(8,128)S(1)}, u32[]{:S(2)}, u32[]{:S(2)}) collective-permute-start(f32[256,256]{1,0:T(8,128)S(1)} %get-tuple-element.164.refs_0_), channel_id=1, source_target_pairs={{0,4},{2,6},{4,0},{6,2},{8,12},{10,14},{12,8},{14,10},{16,20},{18,... | collective-permute-start | bytes 786440 | tf_op jit(solution)/shard_map/ppermute | solution.py:32
  32.4 1.8 %collective-permute-done.13.refs_1_ = f32[256,256]{1,0:T(8,128)S(1)} collective-permute-done((f32[256,256]{1,0:T(8,128)S(1)}, f32[256,256]{1,0:T(8,128)S(1)}, u32[]{:S(2)}, u32[]{:S(2)}) %collective-permute-start.13) | collective-permute-done | bytes 262176 | tf_op jit(solution)/shard_map/ppermute | solution.py:32
  34.2 0.4 combine.20
  34.5 1.6 %collective-permute-start.18 = (f32[256,256]{1,0:T(8,128)S(1)}, f32[256,256]{1,0:T(8,128)S(1)}, u32[]{:S(2)}, u32[]{:S(2)}) collective-permute-start(f32[256,256]{1,0:T(8,128)S(1)} %get-tuple-element.163.refs_0_), channel_id=1, source_target_pairs={{0,8},{2,10},{4,12},{6,14},{8,0},{10,2},{12,4},{14,6},{16,24},{18,... | collective-permute-start | bytes 786440 | tf_op jit(solution)/shard_map/ppermute | solution.py:32
  36.2 0.5 node.6
  37.1 2.6 %collective-permute-start.17 = (f32[256,256]{1,0:T(8,128)S(1)}, f32[256,256]{1,0:T(8,128)S(1)}, u32[]{:S(2)}, u32[]{:S(2)}) collective-permute-start(f32[256,256]{1,0:T(8,128)S(1)} %get-tuple-element.162.refs_0_), channel_id=1, source_target_pairs={{0,16},{2,18},{4,20},{6,22},{8,24},{10,26},{12,28},{14,30},{16,0},... | collective-permute-start | bytes 786440 | tf_op jit(solution)/shard_map/ppermute | solution.py:32
  39.7 0.9 %collective-permute-start.20 = (f32[512,128]{1,0:T(8,128)S(1)}, f32[512,128]{1,0:T(8,128)S(1)}, u32[]{:S(2)}, u32[]{:S(2)}) collective-permute-start(f32[512,128]{1,0:T(8,128)S(1)} %get-tuple-element.169.refs_0_), channel_id=1, source_target_pairs={{1,0},{0,1},{3,2},{2,3},{5,4},{4,5},{7,6},{6,7},{9,8},{8,9},{11,10... | collective-permute-start | bytes 786440 | tf_op jit(solution)/shard_map/ppermute | solution.py:38
  41.0 1.6 %collective-permute-start.16 = (f32[256,256]{1,0:T(8,128)S(1)}, f32[256,256]{1,0:T(8,128)S(1)}, u32[]{:S(2)}, u32[]{:S(2)}) collective-permute-start(f32[256,256]{1,0:T(8,128)S(1)} %get-tuple-element.161.refs_0_), channel_id=1, source_target_pairs={{0,4},{2,6},{4,0},{6,2},{8,12},{10,14},{12,8},{14,10},{16,20},{18,... | collective-permute-start | bytes 786440 | tf_op jit(solution)/shard_map/ppermute | solution.py:32
  43.0 1.0 %collective-permute-start.23 = (f32[256,256]{1,0:T(8,128)S(1)}, f32[256,256]{1,0:T(8,128)S(1)}, u32[]{:S(2)}, u32[]{:S(2)}) collective-permute-start(f32[256,256]{1,0:T(8,128)S(1)} %get-tuple-element.185.refs_0_), channel_id=1, source_target_pairs={{0,8},{2,10},{4,12},{6,14},{8,0},{10,2},{12,4},{14,6},{16,24},{18,... | collective-permute-start | bytes 786440 | tf_op jit(solution)/shard_map/ppermute | solution.py:32
  43.9 3.1 %collective-permute-done.18.refs_1_ = f32[256,256]{1,0:T(8,128)S(1)} collective-permute-done((f32[256,256]{1,0:T(8,128)S(1)}, f32[256,256]{1,0:T(8,128)S(1)}, u32[]{:S(2)}, u32[]{:S(2)}) %collective-permute-start.18) | collective-permute-done | bytes 262176 | tf_op jit(solution)/shard_map/ppermute | solution.py:32
  47.1 0.4 combine.24
  47.4 2.2 %collective-permute-start.22 = (f32[256,256]{1,0:T(8,128)S(1)}, f32[256,256]{1,0:T(8,128)S(1)}, u32[]{:S(2)}, u32[]{:S(2)}) collective-permute-start(f32[256,256]{1,0:T(8,128)S(1)} %get-tuple-element.184.refs_0_), channel_id=1, source_target_pairs={{0,16},{2,18},{4,20},{6,22},{8,24},{10,26},{12,28},{14,30},{16,0},... | collective-permute-start | bytes 786440 | tf_op jit(solution)/shard_map/ppermute | solution.py:32
  49.6 1.6 %collective-permute-done.17.refs_0_ = f32[256,256]{1,0:T(8,128)S(1)} collective-permute-done((f32[256,256]{1,0:T(8,128)S(1)}, f32[256,256]{1,0:T(8,128)S(1)}, u32[]{:S(2)}, u32[]{:S(2)}) %collective-permute-start.17) | collective-permute-done | bytes 262176 | tf_op jit(solution)/shard_map/ppermute | solution.py:32
  51.2 0.6 node.7
  51.9 1.5 %rest.1 = (f32[512,1024]{1,0:T(8,128)}, f32[8,128]{1,0:T(8,128)S(1)}) custom-call(f32[512,1024]{1,0:T(8,128)S(1)} %copy-done, bf16[512,256]{1,0:T(8,128)(2,1)S(1)} %get-tuple-element.108.refs_2_.refs_1_, bf16[512,256]{1,0:T(8,128)(2,1)S(1)} %get-tuple-element.109.refs_3_.refs_2_, bf16[256,256]{1,0:T(8,128)(2,1)S(1)} %get-tuple-element.175.refs_3_, ...), custom_call_target="tpu_custom_call" | custom-call | flops 19549999104 | tf_op jit(solution)/shard_map/rest/pallas_call | solution.py:128
  53.4 1.2 %finish.4 = (f32[512,1024]{1,0:T(8,128)}, f32[8,128]{1,0:T(8,128)S(1)}) custom-call(f32[256,256]{1,0:T(8,128)S(1)} %get-tuple-element.162.refs_0_, f32[256,256]{1,0:T(8,128)S(1)} %get-tuple-element.168.refs_1_, bf16[256,256]{1,0:T(8,128)(2,1)S(1)} %get-tuple-element.171.refs_2_, ...), custom_call_target="tpu_custom_call", output_to_operand_aliasing={{0}: (7, {})} | custom-call | flops 14949999616 | tf_op jit(solution)/shard_map/finish/pallas_call | solution.py:128
  55.0 1.5 %collective-permute-start.21 = (f32[256,256]{1,0:T(8,128)S(1)}, f32[256,256]{1,0:T(8,128)S(1)}, u32[]{:S(2)}, u32[]{:S(2)}) collective-permute-start(f32[256,256]{1,0:T(8,128)S(1)} %get-tuple-element.183.refs_0_), channel_id=1, source_target_pairs={{0,8},{2,10},{4,12},{6,14},{8,0},{10,2},{12,4},{14,6},{16,24},{18,... | collective-permute-start | bytes 786440 | tf_op jit(solution)/shard_map/ppermute | solution.py:32
  56.4 1.8 %collective-permute-done.23.refs_1_ = f32[256,256]{1,0:T(8,128)S(1)} collective-permute-done((f32[256,256]{1,0:T(8,128)S(1)}, f32[256,256]{1,0:T(8,128)S(1)}, u32[]{:S(2)}, u32[]{:S(2)}) %collective-permute-start.23) | collective-permute-done | bytes 262176 | tf_op jit(solution)/shard_map/ppermute | solution.py:32
  58.6 2.5 %collective-permute-start.25 = (f32[256,256]{1,0:T(8,128)S(1)}, f32[256,256]{1,0:T(8,128)S(1)}, u32[]{:S(2)}, u32[]{:S(2)}) collective-permute-start(f32[256,256]{1,0:T(8,128)S(1)} %get-tuple-element.191.refs_0_), channel_id=1, source_target_pairs={{0,16},{2,18},{4,20},{6,22},{8,24},{10,26},{12,28},{14,30},{16,0},... | collective-permute-start | bytes 786440 | tf_op jit(solution)/shard_map/ppermute | solution.py:32
  61.4 1.2 %finish.5 = (f32[512,1024]{1,0:T(8,128)}, f32[8,128]{1,0:T(8,128)S(1)}) custom-call(f32[256,256]{1,0:T(8,128)S(1)} %get-tuple-element.184.refs_0_, f32[256,256]{1,0:T(8,128)S(1)} %collective-permute-done.22.refs_1_, bf16[256,256]{1,0:T(8,128)(2,1)S(1)} %get-tuple-element.171.refs_2_, ...), custom_call_target="tpu_custom_call", output_to_operand_aliasing={{0}: (7, {})} | custom-call | flops 14949999616 | tf_op jit(solution)/shard_map/finish/pallas_call | solution.py:128
  62.6 5.9 %collective-permute-done.21.refs_1_ = f32[256,256]{1,0:T(8,128)S(1)} collective-permute-done((f32[256,256]{1,0:T(8,128)S(1)}, f32[256,256]{1,0:T(8,128)S(1)}, u32[]{:S(2)}, u32[]{:S(2)}) %collective-permute-start.21) | collective-permute-done | bytes 262176 | tf_op jit(solution)/shard_map/ppermute | solution.py:32
  68.8 0.6 collective-permute-start.24
  69.4 10.2 %collective-permute-done.25.refs_1_ = f32[256,256]{1,0:T(8,128)S(1)} collective-permute-done((f32[256,256]{1,0:T(8,128)S(1)}, f32[256,256]{1,0:T(8,128)S(1)}, u32[]{:S(2)}, u32[]{:S(2)}) %collective-permute-start.25) | collective-permute-done | bytes 262176 | tf_op jit(solution)/shard_map/ppermute | solution.py:32
  79.6 1.2 %finish.6 = (f32[512,1024]{1,0:T(8,128)}, f32[8,128]{1,0:T(8,128)S(1)}) custom-call(f32[256,256]{1,0:T(8,128)S(1)} %get-tuple-element.191.refs_0_, f32[256,256]{1,0:T(8,128)S(1)} %collective-permute-done.25.refs_1_, bf16[256,256]{1,0:T(8,128)(2,1)S(1)} %get-tuple-element.171.refs_2_, ...), custom_call_target="tpu_custom_call", output_to_operand_aliasing={{0}: (7, {})} | custom-call | flops 14949999616 | tf_op jit(solution)/shard_map/finish/pallas_call | solution.py:128
  80.8 3.3 %collective-permute-done.24.refs_1_ = f32[256,256]{1,0:T(8,128)S(1)} collective-permute-done((f32[256,256]{1,0:T(8,128)S(1)}, f32[256,256]{1,0:T(8,128)S(1)}, u32[]{:S(2)}, u32[]{:S(2)}) %collective-permute-start.24) | collective-permute-done | bytes 262176 | tf_op jit(solution)/shard_map/ppermute | solution.py:32
  84.1 1.2 %finish.7 = (f32[512,1024]{1,0:T(8,128)}, f32[8,128]{1,0:T(8,128)}) custom-call(f32[256,256]{1,0:T(8,128)S(1)} %get-tuple-element.190.refs_0_, f32[256,256]{1,0:T(8,128)S(1)} %collective-permute-done.24.refs_1_, bf16[256,256]{1,0:T(8,128)(2,1)S(1)} %get-tuple-element.171.refs_2_, ...), custom_call_target="tpu_custom_call", output_to_operand_aliasing={{0}: (7, {})} | custom-call | flops 14949999616 | tf_op jit(solution)/shard_map/finish/pallas_call | solution.py:128
  (42 shorter events, 4.4 us)
Async XLA Ops:
  0.0 10.4 %copy-start.1 = (f32[512,128]{1,0:T(8,128)S(1)}, f32[512,128]{1,0:T(8,128)}, u32[]{:S(2)}) copy-start(f32[512,128]{1,0:T(8,128)} %refs_0_.4) | copy-start | bytes 786436
  0.0 10.4 %copy-start = (f32[512,1024]{1,0:T(8,128)S(1)}, f32[512,1024]{1,0:T(8,128)}, u32[]{:S(2)}) copy-start(f32[512,1024]{1,0:T(8,128)} %refs_0_.5) | copy-start | bytes 6291460
  0.0 10.4 %collective-permute-start = (f32[512,128]{1,0:T(8,128)}, f32[512,128]{1,0:T(8,128)S(1)}, u32[]{:S(2)}, u32[]{:S(2)}) collective-permute-start(f32[512,128]{1,0:T(8,128)} %refs_0_.4), channel_id=1, source_target_pairs={{1,0},{0,1},{3,2},{2,3},{5,4},{4,5},{7,6},{6,7},{9,8},{8,9},{11,10... | collective-permute-start | bytes 786440 | tf_op jit(solution)/shard_map/ppermute | solution.py:38
  3.0 10.9 %collective-permute-start.1 = (f32[256,128]{1,0:T(8,128)}, f32[256,128]{1,0:T(8,128)S(1)}, u32[]{:S(2)}, u32[]{:S(2)}) collective-permute-start(f32[256,128]{1,0:T(8,128)} %refs_5_.1), channel_id=1, source_target_pairs={{1,0},{0,1},{3,2},{2,3},{5,4},{4,5},{7,6},{6,7},{9,8},{8,9},{11,10... | collective-permute-start | bytes 393224 | tf_op jit(solution)/shard_map/ppermute | solution.py:38
  4.2 10.6 %collective-permute-start.2 = (f32[256,128]{1,0:T(8,128)S(1)}, f32[256,128]{1,0:T(8,128)S(1)}, u32[]{:S(2)}, u32[]{:S(2)}) collective-permute-start(f32[256,128]{1,0:T(8,128)S(1)} %get-tuple-element.115.refs_7_), channel_id=1, source_target_pairs={{0,4},{2,6},{4,0},{6,2},{8,12},{10,14},{12,8},{14,10},{16,20},{18,... | collective-permute-start | bytes 393224 | tf_op jit(solution)/shard_map/ppermute | solution.py:32
  6.2 8.6 %collective-permute-start.3 = (f32[256,128]{1,0:T(8,128)S(1)}, f32[256,128]{1,0:T(8,128)S(1)}, u32[]{:S(2)}, u32[]{:S(2)}) collective-permute-start(f32[256,128]{1,0:T(8,128)S(1)} %get-tuple-element.116.refs_9_), channel_id=1, source_target_pairs={{0,8},{2,10},{4,12},{6,14},{8,0},{10,2},{12,4},{14,6},{16,24},{18,... | collective-permute-start | bytes 393224 | tf_op jit(solution)/shard_map/ppermute | solution.py:32
  7.7 8.2 %collective-permute-start.6 = (f32[256,128]{1,0:T(8,128)S(1)}, f32[256,128]{1,0:T(8,128)S(1)}, u32[]{:S(2)}, u32[]{:S(2)}) collective-permute-start(f32[256,128]{1,0:T(8,128)S(1)} %get-tuple-element.120.refs_2_), channel_id=1, source_target_pairs={{0,16},{2,18},{4,20},{6,22},{8,24},{10,26},{12,28},{14,30},{16,0},... | collective-permute-start | bytes 393224 | tf_op jit(solution)/shard_map/ppermute | solution.py:32
  10.9 5.0 %collective-permute-start.5 = (f32[256,128]{1,0:T(8,128)S(1)}, f32[256,128]{1,0:T(8,128)S(1)}, u32[]{:S(2)}, u32[]{:S(2)}) collective-permute-start(f32[256,128]{1,0:T(8,128)S(1)} %get-tuple-element.119.refs_0_), channel_id=1, source_target_pairs={{1,0},{0,1},{3,2},{2,3},{5,4},{4,5},{7,6},{6,7},{9,8},{8,9},{11,10... | collective-permute-start | bytes 393224 | tf_op jit(solution)/shard_map/ppermute | solution.py:38
  13.0 0.9 %copy-start.2 = (f32[256,128]{1,0:T(8,128)S(1)}, f32[256,128]{1,0:T(8,128)}, u32[]{:S(2)}) copy-start(f32[256,128]{1,0:T(8,128)} %refs_5_.1) | copy-start | bytes 393220
  14.7 3.9 %collective-permute-start.8 = (f32[256,256]{1,0:T(8,128)S(1)}, f32[256,256]{1,0:T(8,128)S(1)}, u32[]{:S(2)}, u32[]{:S(2)}) collective-permute-start(f32[256,256]{1,0:T(8,128)S(1)} %get-tuple-element.124.refs_0_), channel_id=1, source_target_pairs={{0,2},{2,0},{4,6},{6,4},{8,10},{10,8},{12,14},{14,12},{16,18},{18,... | collective-permute-start | bytes 786440 | tf_op jit(solution)/shard_map/ppermute | solution.py:32
  16.0 2.6 %collective-permute-start.7 = (f32[256,256]{1,0:T(8,128)S(1)}, f32[256,256]{1,0:T(8,128)S(1)}, u32[]{:S(2)}, u32[]{:S(2)}) collective-permute-start(f32[256,256]{1,0:T(8,128)S(1)} %get-tuple-element.122.refs_0_), channel_id=1, source_target_pairs={{0,2},{2,0},{4,6},{6,4},{8,10},{10,8},{12,14},{14,12},{16,18},{18,... | collective-permute-start | bytes 786440 | tf_op jit(solution)/shard_map/ppermute | solution.py:32
  16.6 6.2 %collective-permute-start.4 = (f32[768,256]{1,0:T(8,128)S(1)}, f32[768,256]{1,0:T(8,128)S(1)}, u32[]{:S(2)}, u32[]{:S(2)}) collective-permute-start(f32[768,256]{1,0:T(8,128)S(1)} %get-tuple-element.118.refs_0_), channel_id=1, source_target_pairs={{0,2},{2,0},{4,6},{6,4},{8,10},{10,8},{12,14},{14,12},{16,18},{18,... | collective-permute-start | bytes 2359304 | tf_op jit(solution)/shard_map/ppermute | solution.py:32
  16.6 9.1 %collective-permute-start.10 = (f32[512,128]{1,0:T(8,128)S(1)}, f32[512,128]{1,0:T(8,128)S(1)}, u32[]{:S(2)}, u32[]{:S(2)}) collective-permute-start(f32[512,128]{1,0:T(8,128)S(1)} %get-tuple-element.134.refs_0_), channel_id=1, source_target_pairs={{1,0},{0,1},{3,2},{2,3},{5,4},{4,5},{7,6},{6,7},{9,8},{8,9},{11,10... | collective-permute-start | bytes 786440 | tf_op jit(solution)/shard_map/ppermute | solution.py:38
  19.3 6.9 %collective-permute-start.9 = (f32[128,256]{1,0:T(8,128)S(1)}, f32[128,256]{1,0:T(8,128)S(1)}, u32[]{:S(2)}, u32[]{:S(2)}) collective-permute-start(f32[128,256]{1,0:T(8,128)S(1)} %get-tuple-element.133.refs_0_), channel_id=1, source_target_pairs={{0,4},{2,6},{4,0},{6,2},{8,12},{10,14},{12,8},{14,10},{16,20},{18,... | collective-permute-start | bytes 393224 | tf_op jit(solution)/shard_map/ppermute | solution.py:32
  21.2 7.4 %collective-permute-start.14 = (f32[128,256]{1,0:T(8,128)S(1)}, f32[128,256]{1,0:T(8,128)S(1)}, u32[]{:S(2)}, u32[]{:S(2)}) collective-permute-start(f32[128,256]{1,0:T(8,128)S(1)} %get-tuple-element.147.refs_0_), channel_id=1, source_target_pairs={{0,4},{2,6},{4,0},{6,2},{8,12},{10,14},{12,8},{14,10},{16,20},{18,... | collective-permute-start | bytes 393224 | tf_op jit(solution)/shard_map/ppermute | solution.py:32
  21.8 14.4 %collective-permute-start.12 = (f32[512,128]{1,0:T(8,128)S(1)}, f32[512,128]{1,0:T(8,128)S(1)}, u32[]{:S(2)}, u32[]{:S(2)}) collective-permute-start(f32[512,128]{1,0:T(8,128)S(1)} %get-tuple-element.144.refs_0_), channel_id=1, source_target_pairs={{1,0},{0,1},{3,2},{2,3},{5,4},{4,5},{7,6},{6,7},{9,8},{8,9},{11,10... | collective-permute-start | bytes 786440 | tf_op jit(solution)/shard_map/ppermute | solution.py:38
  23.1 11.0 %collective-permute-start.13 = (f32[256,256]{1,0:T(8,128)S(1)}, f32[256,256]{1,0:T(8,128)S(1)}, u32[]{:S(2)}, u32[]{:S(2)}) collective-permute-start(f32[256,256]{1,0:T(8,128)S(1)} %get-tuple-element.146.refs_0_), channel_id=1, source_target_pairs={{0,4},{2,6},{4,0},{6,2},{8,12},{10,14},{12,8},{14,10},{16,20},{18,... | collective-permute-start | bytes 786440 | tf_op jit(solution)/shard_map/ppermute | solution.py:32
  26.5 10.2 %collective-permute-start.11 = (f32[128,256]{1,0:T(8,128)S(1)}, f32[128,256]{1,0:T(8,128)S(1)}, u32[]{:S(2)}, u32[]{:S(2)}) collective-permute-start(f32[128,256]{1,0:T(8,128)S(1)} %get-tuple-element.143.refs_0_), channel_id=1, source_target_pairs={{0,8},{2,10},{4,12},{6,14},{8,0},{10,2},{12,4},{14,6},{16,24},{18,... | collective-permute-start | bytes 393224 | tf_op jit(solution)/shard_map/ppermute | solution.py:32
  28.9 7.8 %collective-permute-start.15 = (f32[128,256]{1,0:T(8,128)S(1)}, f32[128,256]{1,0:T(8,128)S(1)}, u32[]{:S(2)}, u32[]{:S(2)}) collective-permute-start(f32[128,256]{1,0:T(8,128)S(1)} %get-tuple-element.154.refs_2_), channel_id=1, source_target_pairs={{0,8},{2,10},{4,12},{6,14},{8,0},{10,2},{12,4},{14,6},{16,24},{18,... | collective-permute-start | bytes 393224 | tf_op jit(solution)/shard_map/ppermute | solution.py:32
  30.8 11.8 %collective-permute-start.19 = (f32[256,256]{1,0:T(8,128)S(1)}, f32[256,256]{1,0:T(8,128)S(1)}, u32[]{:S(2)}, u32[]{:S(2)}) collective-permute-start(f32[256,256]{1,0:T(8,128)S(1)} %get-tuple-element.164.refs_0_), channel_id=1, source_target_pairs={{0,4},{2,6},{4,0},{6,2},{8,12},{10,14},{12,8},{14,10},{16,20},{18,... | collective-permute-start | bytes 786440 | tf_op jit(solution)/shard_map/ppermute | solution.py:32
  34.5 12.5 %collective-permute-start.18 = (f32[256,256]{1,0:T(8,128)S(1)}, f32[256,256]{1,0:T(8,128)S(1)}, u32[]{:S(2)}, u32[]{:S(2)}) collective-permute-start(f32[256,256]{1,0:T(8,128)S(1)} %get-tuple-element.163.refs_0_), channel_id=1, source_target_pairs={{0,8},{2,10},{4,12},{6,14},{8,0},{10,2},{12,4},{14,6},{16,24},{18,... | collective-permute-start | bytes 786440 | tf_op jit(solution)/shard_map/ppermute | solution.py:32
  37.1 14.1 %collective-permute-start.17 = (f32[256,256]{1,0:T(8,128)S(1)}, f32[256,256]{1,0:T(8,128)S(1)}, u32[]{:S(2)}, u32[]{:S(2)}) collective-permute-start(f32[256,256]{1,0:T(8,128)S(1)} %get-tuple-element.162.refs_0_), channel_id=1, source_target_pairs={{0,16},{2,18},{4,20},{6,22},{8,24},{10,26},{12,28},{14,30},{16,0},... | collective-permute-start | bytes 786440 | tf_op jit(solution)/shard_map/ppermute | solution.py:32
  39.7 11.5 %collective-permute-start.20 = (f32[512,128]{1,0:T(8,128)S(1)}, f32[512,128]{1,0:T(8,128)S(1)}, u32[]{:S(2)}, u32[]{:S(2)}) collective-permute-start(f32[512,128]{1,0:T(8,128)S(1)} %get-tuple-element.169.refs_0_), channel_id=1, source_target_pairs={{1,0},{0,1},{3,2},{2,3},{5,4},{4,5},{7,6},{6,7},{9,8},{8,9},{11,10... | collective-permute-start | bytes 786440 | tf_op jit(solution)/shard_map/ppermute | solution.py:38
  41.0 13.5 %collective-permute-start.16 = (f32[256,256]{1,0:T(8,128)S(1)}, f32[256,256]{1,0:T(8,128)S(1)}, u32[]{:S(2)}, u32[]{:S(2)}) collective-permute-start(f32[256,256]{1,0:T(8,128)S(1)} %get-tuple-element.161.refs_0_), channel_id=1, source_target_pairs={{0,4},{2,6},{4,0},{6,2},{8,12},{10,14},{12,8},{14,10},{16,20},{18,... | collective-permute-start | bytes 786440 | tf_op jit(solution)/shard_map/ppermute | solution.py:32
  43.0 15.2 %collective-permute-start.23 = (f32[256,256]{1,0:T(8,128)S(1)}, f32[256,256]{1,0:T(8,128)S(1)}, u32[]{:S(2)}, u32[]{:S(2)}) collective-permute-start(f32[256,256]{1,0:T(8,128)S(1)} %get-tuple-element.185.refs_0_), channel_id=1, source_target_pairs={{0,8},{2,10},{4,12},{6,14},{8,0},{10,2},{12,4},{14,6},{16,24},{18,... | collective-permute-start | bytes 786440 | tf_op jit(solution)/shard_map/ppermute | solution.py:32
  47.4 14.0 %collective-permute-start.22 = (f32[256,256]{1,0:T(8,128)S(1)}, f32[256,256]{1,0:T(8,128)S(1)}, u32[]{:S(2)}, u32[]{:S(2)}) collective-permute-start(f32[256,256]{1,0:T(8,128)S(1)} %get-tuple-element.184.refs_0_), channel_id=1, source_target_pairs={{0,16},{2,18},{4,20},{6,22},{8,24},{10,26},{12,28},{14,30},{16,0},... | collective-permute-start | bytes 786440 | tf_op jit(solution)/shard_map/ppermute | solution.py:32
  55.0 13.5 %collective-permute-start.21 = (f32[256,256]{1,0:T(8,128)S(1)}, f32[256,256]{1,0:T(8,128)S(1)}, u32[]{:S(2)}, u32[]{:S(2)}) collective-permute-start(f32[256,256]{1,0:T(8,128)S(1)} %get-tuple-element.183.refs_0_), channel_id=1, source_target_pairs={{0,8},{2,10},{4,12},{6,14},{8,0},{10,2},{12,4},{14,6},{16,24},{18,... | collective-permute-start | bytes 786440 | tf_op jit(solution)/shard_map/ppermute | solution.py:32
  58.6 21.0 %collective-permute-start.25 = (f32[256,256]{1,0:T(8,128)S(1)}, f32[256,256]{1,0:T(8,128)S(1)}, u32[]{:S(2)}, u32[]{:S(2)}) collective-permute-start(f32[256,256]{1,0:T(8,128)S(1)} %get-tuple-element.191.refs_0_), channel_id=1, source_target_pairs={{0,16},{2,18},{4,20},{6,22},{8,24},{10,26},{12,28},{14,30},{16,0},... | collective-permute-start | bytes 786440 | tf_op jit(solution)/shard_map/ppermute | solution.py:32
  68.8 15.3 %collective-permute-start.24 = (f32[256,256]{1,0:T(8,128)S(1)}, f32[256,256]{1,0:T(8,128)S(1)}, u32[]{:S(2)}, u32[]{:S(2)}) collective-permute-start(f32[256,256]{1,0:T(8,128)S(1)} %get-tuple-element.190.refs_0_), channel_id=1, source_target_pairs={{0,16},{2,18},{4,20},{6,22},{8,24},{10,26},{12,28},{14,30},{16,0},... | collective-permute-start | bytes 786440 | tf_op jit(solution)/shard_map/ppermute | solution.py:32

commit v5 on v4

--- a/solution.py
+++ b/solution.py
@@ -389,7 +389,7 @@
         inputs = [own, partner]
         if s:
             inputs = col_blocks(stacks[s])
-        held_back = [t for t in range(2, levels) if s == (0 if t == 2 else t - 1)]
+        held_back = [t for t in range(3, levels) if s == t - 1]
         *nodes[s], = line(
             functools.partial(node_body, s, n),
             "node",
@@ -423,6 +423,8 @@
         if not last:
             (top,) = line(body, "combine", inputs, [held(width, size)])
             tops[s + 1].append((start, width, top, swapped(top, "row", s + 1)))
+            if levels > 2 and (s, c) == (0, min(2, len(cuts[1]) - 1)):
+                (stacks[2],) = line(hand_on, "hand", [stacks[2]], [held(2 * size, piece)])
         else:
             if out is None:
                 (out,) = line(

time: 85.4 us -> 85.4 us (level)
    pallas_call x32 -> x33, Pallas kernels: 17.5 us -> 17.5 us  [__call__(): pl.pallas_call(kernel, grid=grid, out_shape=out_shape, in_specs=in_specs,...]
  transfers between devices with their start and end apart: 26 -> 26, of which waited for: 9 -> 10; matrix products, arithmetic and copies ran while one was open for 0% -> 0% of each run, Pallas kernels for 19% -> 19%
where the time goes in v5:
time: 85.4 us; the launch traced here: 85.2 us
  starting transfers between devices  38 us (44%)
  waiting for transfers between devices  29.4 us (34%)
  Pallas kernels  17.5 us (20%)
    ppermute x20, starting transfers between devices, swapped(): return lax.ppermute(value, axis, pairs)  29 us
    ppermute x20, waiting for transfers between devices, swapped(): return lax.ppermute(value, axis, pairs)  28.8 us
    pallas_call x33, Pallas kernels, __call__(): pl.pallas_call(kernel, grid=grid, out_shape=out_shape, in_specs=in_specs,...  17.5 us
    ppermute x6, starting transfers between devices, turned(): lax.ppermute(value, axis, [((to + step) % size, to) for to in range(size)])  9.03 us
  transfers between devices with their start and end apart: 26, of which 10 were waited for; matrix products, arithmetic and copies ran while one was open for 0% of the time, Pallas kernels for 19%

profile of v5, /device:TPU:0, one launch (start us, length us, event | category | flops | bytes accessed | tf_op | source)
XLA Modules:
  0.0 85.2 jit_solution(533342536659165893)
XLA Ops:
  0.0 3.0 %collective-permute-start = (f32[512,128]{1,0:T(8,128)}, f32[512,128]{1,0:T(8,128)S(1)}, u32[]{:S(2)}, u32[]{:S(2)}) collective-permute-start(f32[512,128]{1,0:T(8,128)} %refs_0_.4), channel_id=1, source_target_pairs={{1,0},{0,1},{3,2},{2,3},{5,4},{4,5},{7,6},{6,7},{9,8},{8,9},{11,10... | collective-permute-start | bytes 786440 | tf_op jit(solution)/shard_map/ppermute | solution.py:38
  3.0 1.1 %pick.1 = (f32[256,128]{1,0:T(8,128)S(1)}, f32[256,128]{1,0:T(8,128)S(1)}, f32[256,128]{1,0:T(8,128)S(1)}, f32[256,128]{1,0:T(8,128)S(1)}, f32[8,128]{1,0:T(8,128)S(1)}) custom-call(f32[4,256,128]{2,1,0:T(8,128)} %refs_0_.3, f32[4,256,128]{2,1,0:T(8,128)} %refs_1_.1), custom_call_target="tpu_custom_call" | custom-call | flops 12650000384 | tf_op jit(solution)/shard_map/pick/pallas_call | solution.py:128
  4.2 2.0 %collective-permute-start.2 = (f32[256,128]{1,0:T(8,128)S(1)}, f32[256,128]{1,0:T(8,128)S(1)}, u32[]{:S(2)}, u32[]{:S(2)}) collective-permute-start(f32[256,128]{1,0:T(8,128)S(1)} %get-tuple-element.116.refs_7_), channel_id=1, source_target_pairs={{0,4},{2,6},{4,0},{6,2},{8,12},{10,14},{12,8},{14,10},{16,20},{18,... | collective-permute-start | bytes 393224 | tf_op jit(solution)/shard_map/ppermute | solution.py:32
  6.2 1.6 %collective-permute-start.3 = (f32[256,128]{1,0:T(8,128)S(1)}, f32[256,128]{1,0:T(8,128)S(1)}, u32[]{:S(2)}, u32[]{:S(2)}) collective-permute-start(f32[256,128]{1,0:T(8,128)S(1)} %get-tuple-element.117.refs_9_), channel_id=1, source_target_pairs={{0,8},{2,10},{4,12},{6,14},{8,0},{10,2},{12,4},{14,6},{16,24},{18,... | collective-permute-start | bytes 393224 | tf_op jit(solution)/shard_map/ppermute | solution.py:32
  7.7 2.6 %collective-permute-start.6 = (f32[256,128]{1,0:T(8,128)S(1)}, f32[256,128]{1,0:T(8,128)S(1)}, u32[]{:S(2)}, u32[]{:S(2)}) collective-permute-start(f32[256,128]{1,0:T(8,128)S(1)} %get-tuple-element.121.refs_2_), channel_id=1, source_target_pairs={{0,16},{2,18},{4,20},{6,22},{8,24},{10,26},{12,28},{14,30},{16,0},... | collective-permute-start | bytes 393224 | tf_op jit(solution)/shard_map/ppermute | solution.py:32
  10.4 0.5 inner.1
  10.9 2.1 %collective-permute-start.5 = (f32[256,128]{1,0:T(8,128)S(1)}, f32[256,128]{1,0:T(8,128)S(1)}, u32[]{:S(2)}, u32[]{:S(2)}) collective-permute-start(f32[256,128]{1,0:T(8,128)S(1)} %get-tuple-element.120.refs_0_), channel_id=1, source_target_pairs={{1,0},{0,1},{3,2},{2,3},{5,4},{4,5},{7,6},{6,7},{9,8},{8,9},{11,10... | collective-permute-start | bytes 393224 | tf_op jit(solution)/shard_map/ppermute | solution.py:38
  13.0 0.9 %later.1 = (bf16[256,768]{1,0:T(8,128)(2,1)S(1)}, bf16[256,768]{1,0:T(8,128)(2,1)S(1)}, f32[8,128]{1,0:T(8,128)S(1)}) custom-call(bf16[256,512]{1,0:T(8,128)(2,1)S(1)} %get-tuple-element.104.refs_0_, bf16[256,512]{1,0:T(8,128)(2,1)S(1)} %get-tuple-element.105.refs_1_, f32[512,1024]{1,0:T(8,128)S(1)} %copy-done, f32[8,128]{1,0:T(8,128)S(1)} %get-tuple-element.106.refs_3_), custom_call_target="tpu_custom_call" | custom-call | flops 27599998976 | tf_op jit(solution)/shard_map/later/pallas_call | solution.py:128
  13.9 0.8 first.1
  14.8 1.2 %tops.1 = (f32[768,256]{1,0:T(8,128)S(1)}, bf16[256,768]{1,0:T(8,128)(2,1)S(1)}, bf16[256,768]{1,0:T(8,128)(2,1)S(1)}, f32[512,128]{1,0:T(8,128)S(1)}, f32[512,128]{1,0:T(8,128)S(1)}, /*index=5*/f32[8,128]{1,0:T(8,128)S(1)}) custom-call(bf16[256,768]{1,0:T(8,128)(2,1)S(1)} %get-tuple-element.107.refs_0_, bf16[256,768]{1,0:T(8,128)(2,1)S(1)} %get-tuple-element.108.refs_1_, ...), custom_call_target="tpu_custom_call" | custom-call | flops 11500000256 | tf_op jit(solution)/shard_map/tops/pallas_call | solution.py:128
  16.0 0.5 collective-permute-start.7
  16.7 1.9 %collective-permute-start.10 = (f32[512,128]{1,0:T(8,128)S(1)}, f32[512,128]{1,0:T(8,128)S(1)}, u32[]{:S(2)}, u32[]{:S(2)}) collective-permute-start(f32[512,128]{1,0:T(8,128)S(1)} %get-tuple-element.134.refs_0_), channel_id=1, source_target_pairs={{1,0},{0,1},{3,2},{2,3},{5,4},{4,5},{7,6},{6,7},{9,8},{8,9},{11,10... | collective-permute-start | bytes 786440 | tf_op jit(solution)/shard_map/ppermute | solution.py:38
  18.6 0.4 node.4
  19.3 1.6 %collective-permute-start.9 = (f32[128,256]{1,0:T(8,128)S(1)}, f32[128,256]{1,0:T(8,128)S(1)}, u32[]{:S(2)}, u32[]{:S(2)}) collective-permute-start(f32[128,256]{1,0:T(8,128)S(1)} %get-tuple-element.133.refs_0_), channel_id=1, source_target_pairs={{0,4},{2,6},{4,0},{6,2},{8,12},{10,14},{12,8},{14,10},{16,20},{18,... | collective-permute-start | bytes 393224 | tf_op jit(solution)/shard_map/ppermute | solution.py:32
  21.1 0.6 collective-permute-start.14
  22.1 1.6 %collective-permute-start.13 = (f32[256,256]{1,0:T(8,128)S(1)}, f32[256,256]{1,0:T(8,128)S(1)}, u32[]{:S(2)}, u32[]{:S(2)}) collective-permute-start(f32[256,256]{1,0:T(8,128)S(1)} %get-tuple-element.148.refs_0_), channel_id=1, source_target_pairs={{0,4},{2,6},{4,0},{6,2},{8,12},{10,14},{12,8},{14,10},{16,20},{18,... | collective-permute-start | bytes 786440 | tf_op jit(solution)/shard_map/ppermute | solution.py:32
  23.7 1.1 %collective-permute-start.12 = (f32[512,128]{1,0:T(8,128)S(1)}, f32[512,128]{1,0:T(8,128)S(1)}, u32[]{:S(2)}, u32[]{:S(2)}) collective-permute-start(f32[512,128]{1,0:T(8,128)S(1)} %get-tuple-element.146.refs_0_), channel_id=1, source_target_pairs={{1,0},{0,1},{3,2},{2,3},{5,4},{4,5},{7,6},{6,7},{9,8},{8,9},{11,10... | collective-permute-start | bytes 786440 | tf_op jit(solution)/shard_map/ppermute | solution.py:38
  24.8 0.5 collective-permute-done.10.refs_1_
  25.3 0.4 node.5
  26.1 1.7 %collective-permute-start.11 = (f32[128,256]{1,0:T(8,128)S(1)}, f32[128,256]{1,0:T(8,128)S(1)}, u32[]{:S(2)}, u32[]{:S(2)}) collective-permute-start(f32[128,256]{1,0:T(8,128)S(1)} %get-tuple-element.145.refs_0_), channel_id=1, source_target_pairs={{0,8},{2,10},{4,12},{6,14},{8,0},{10,2},{12,4},{14,6},{16,24},{18,... | collective-permute-start | bytes 393224 | tf_op jit(solution)/shard_map/ppermute | solution.py:32
  27.7 0.8 collective-permute-done.14.refs_1_
  28.8 1.6 %collective-permute-start.15 = (f32[128,256]{1,0:T(8,128)S(1)}, f32[128,256]{1,0:T(8,128)S(1)}, u32[]{:S(2)}, u32[]{:S(2)}) collective-permute-start(f32[128,256]{1,0:T(8,128)S(1)} %get-tuple-element.156.refs_2_), channel_id=1, source_target_pairs={{0,8},{2,10},{4,12},{6,14},{8,0},{10,2},{12,4},{14,6},{16,24},{18,... | collective-permute-start | bytes 393224 | tf_op jit(solution)/shard_map/ppermute | solution.py:32
  30.8 1.6 %collective-permute-start.19 = (f32[256,256]{1,0:T(8,128)S(1)}, f32[256,256]{1,0:T(8,128)S(1)}, u32[]{:S(2)}, u32[]{:S(2)}) collective-permute-start(f32[256,256]{1,0:T(8,128)S(1)} %get-tuple-element.166.refs_0_), channel_id=1, source_target_pairs={{0,4},{2,6},{4,0},{6,2},{8,12},{10,14},{12,8},{14,10},{16,20},{18,... | collective-permute-start | bytes 786440 | tf_op jit(solution)/shard_map/ppermute | solution.py:32
  32.4 1.8 %collective-permute-done.13.refs_1_ = f32[256,256]{1,0:T(8,128)S(1)} collective-permute-done((f32[256,256]{1,0:T(8,128)S(1)}, f32[256,256]{1,0:T(8,128)S(1)}, u32[]{:S(2)}, u32[]{:S(2)}) %collective-permute-start.13) | collective-permute-done | bytes 262176 | tf_op jit(solution)/shard_map/ppermute | solution.py:32
  34.5 1.6 %collective-permute-start.18 = (f32[256,256]{1,0:T(8,128)S(1)}, f32[256,256]{1,0:T(8,128)S(1)}, u32[]{:S(2)}, u32[]{:S(2)}) collective-permute-start(f32[256,256]{1,0:T(8,128)S(1)} %get-tuple-element.165.refs_0_), channel_id=1, source_target_pairs={{0,8},{2,10},{4,12},{6,14},{8,0},{10,2},{12,4},{14,6},{16,24},{18,... | collective-permute-start | bytes 786440 | tf_op jit(solution)/shard_map/ppermute | solution.py:32
  36.2 0.5 node.6
  37.0 2.7 %collective-permute-start.17 = (f32[256,256]{1,0:T(8,128)S(1)}, f32[256,256]{1,0:T(8,128)S(1)}, u32[]{:S(2)}, u32[]{:S(2)}) collective-permute-start(f32[256,256]{1,0:T(8,128)S(1)} %get-tuple-element.164.refs_0_), channel_id=1, source_target_pairs={{0,16},{2,18},{4,20},{6,22},{8,24},{10,26},{12,28},{14,30},{16,0},... | collective-permute-start | bytes 786440 | tf_op jit(solution)/shard_map/ppermute | solution.py:32
  39.7 0.9 %collective-permute-start.20 = (f32[512,128]{1,0:T(8,128)S(1)}, f32[512,128]{1,0:T(8,128)S(1)}, u32[]{:S(2)}, u32[]{:S(2)}) collective-permute-start(f32[512,128]{1,0:T(8,128)S(1)} %get-tuple-element.171.refs_0_), channel_id=1, source_target_pairs={{1,0},{0,1},{3,2},{2,3},{5,4},{4,5},{7,6},{6,7},{9,8},{8,9},{11,10... | collective-permute-start | bytes 786440 | tf_op jit(solution)/shard_map/ppermute | solution.py:38
  41.0 1.6 %collective-permute-start.16 = (f32[256,256]{1,0:T(8,128)S(1)}, f32[256,256]{1,0:T(8,128)S(1)}, u32[]{:S(2)}, u32[]{:S(2)}) collective-permute-start(f32[256,256]{1,0:T(8,128)S(1)} %get-tuple-element.163.refs_0_), channel_id=1, source_target_pairs={{0,4},{2,6},{4,0},{6,2},{8,12},{10,14},{12,8},{14,10},{16,20},{18,... | collective-permute-start | bytes 786440 | tf_op jit(solution)/shard_map/ppermute | solution.py:32
  42.6 0.4 combine.23
  43.0 1.0 %collective-permute-start.23 = (f32[256,256]{1,0:T(8,128)S(1)}, f32[256,256]{1,0:T(8,128)S(1)}, u32[]{:S(2)}, u32[]{:S(2)}) collective-permute-start(f32[256,256]{1,0:T(8,128)S(1)} %get-tuple-element.187.refs_0_), channel_id=1, source_target_pairs={{0,8},{2,10},{4,12},{6,14},{8,0},{10,2},{12,4},{14,6},{16,24},{18,... | collective-permute-start | bytes 786440 | tf_op jit(solution)/shard_map/ppermute | solution.py:32
  43.9 3.1 %collective-permute-done.18.refs_1_ = f32[256,256]{1,0:T(8,128)S(1)} collective-permute-done((f32[256,256]{1,0:T(8,128)S(1)}, f32[256,256]{1,0:T(8,128)S(1)}, u32[]{:S(2)}, u32[]{:S(2)}) %collective-permute-start.18) | collective-permute-done | bytes 262176 | tf_op jit(solution)/shard_map/ppermute | solution.py:32
  47.0 0.4 combine.24
  47.4 2.1 %collective-permute-start.22 = (f32[256,256]{1,0:T(8,128)S(1)}, f32[256,256]{1,0:T(8,128)S(1)}, u32[]{:S(2)}, u32[]{:S(2)}) collective-permute-start(f32[256,256]{1,0:T(8,128)S(1)} %get-tuple-element.186.refs_0_), channel_id=1, source_target_pairs={{0,16},{2,18},{4,20},{6,22},{8,24},{10,26},{12,28},{14,30},{16,0},... | collective-permute-start | bytes 786440 | tf_op jit(solution)/shard_map/ppermute | solution.py:32
  49.6 1.6 %collective-permute-done.17.refs_0_ = f32[256,256]{1,0:T(8,128)S(1)} collective-permute-done((f32[256,256]{1,0:T(8,128)S(1)}, f32[256,256]{1,0:T(8,128)S(1)}, u32[]{:S(2)}, u32[]{:S(2)}) %collective-permute-start.17) | collective-permute-done | bytes 262176 | tf_op jit(solution)/shard_map/ppermute | solution.py:32
  51.2 0.6 node.7
  51.8 1.5 %rest.1 = (f32[512,1024]{1,0:T(8,128)}, f32[8,128]{1,0:T(8,128)S(1)}) custom-call(f32[512,1024]{1,0:T(8,128)S(1)} %copy-done, bf16[512,256]{1,0:T(8,128)(2,1)S(1)} %get-tuple-element.109.refs_2_.refs_1_, bf16[512,256]{1,0:T(8,128)(2,1)S(1)} %get-tuple-element.110.refs_3_.refs_2_, bf16[256,256]{1,0:T(8,128)(2,1)S(1)} %get-tuple-element.177.refs_3_, ...), custom_call_target="tpu_custom_call" | custom-call | flops 19549999104 | tf_op jit(solution)/shard_map/rest/pallas_call | solution.py:128
  53.3 1.1 %finish.4 = (f32[512,1024]{1,0:T(8,128)}, f32[8,128]{1,0:T(8,128)S(1)}) custom-call(f32[256,256]{1,0:T(8,128)S(1)} %get-tuple-element.164.refs_0_, f32[256,256]{1,0:T(8,128)S(1)} %get-tuple-element.170.refs_1_, bf16[256,256]{1,0:T(8,128)(2,1)S(1)} %get-tuple-element.173.refs_2_, ...), custom_call_target="tpu_custom_call", output_to_operand_aliasing={{0}: (7, {})} | custom-call | flops 14949999616 | tf_op jit(solution)/shard_map/finish/pallas_call | solution.py:128
  54.9 1.5 %collective-permute-start.21 = (f32[256,256]{1,0:T(8,128)S(1)}, f32[256,256]{1,0:T(8,128)S(1)}, u32[]{:S(2)}, u32[]{:S(2)}) collective-permute-start(f32[256,256]{1,0:T(8,128)S(1)} %get-tuple-element.185.refs_0_), channel_id=1, source_target_pairs={{0,8},{2,10},{4,12},{6,14},{8,0},{10,2},{12,4},{14,6},{16,24},{18,... | collective-permute-start | bytes 786440 | tf_op jit(solution)/shard_map/ppermute | solution.py:32
  56.4 1.8 %collective-permute-done.23.refs_1_ = f32[256,256]{1,0:T(8,128)S(1)} collective-permute-done((f32[256,256]{1,0:T(8,128)S(1)}, f32[256,256]{1,0:T(8,128)S(1)}, u32[]{:S(2)}, u32[]{:S(2)}) %collective-permute-start.23) | collective-permute-done | bytes 262176 | tf_op jit(solution)/shard_map/ppermute | solution.py:32
  58.6 2.5 %collective-permute-start.25 = (f32[256,256]{1,0:T(8,128)S(1)}, f32[256,256]{1,0:T(8,128)S(1)}, u32[]{:S(2)}, u32[]{:S(2)}) collective-permute-start(f32[256,256]{1,0:T(8,128)S(1)} %get-tuple-element.193.refs_0_), channel_id=1, source_target_pairs={{0,16},{2,18},{4,20},{6,22},{8,24},{10,26},{12,28},{14,30},{16,0},... | collective-permute-start | bytes 786440 | tf_op jit(solution)/shard_map/ppermute | solution.py:32
  61.3 1.1 %finish.5 = (f32[512,1024]{1,0:T(8,128)}, f32[8,128]{1,0:T(8,128)S(1)}) custom-call(f32[256,256]{1,0:T(8,128)S(1)} %get-tuple-element.186.refs_0_, f32[256,256]{1,0:T(8,128)S(1)} %collective-permute-done.22.refs_1_, bf16[256,256]{1,0:T(8,128)(2,1)S(1)} %get-tuple-element.173.refs_2_, ...), custom_call_target="tpu_custom_call", output_to_operand_aliasing={{0}: (7, {})} | custom-call | flops 14949999616 | tf_op jit(solution)/shard_map/finish/pallas_call | solution.py:128
  62.5 5.9 %collective-permute-done.21.refs_1_ = f32[256,256]{1,0:T(8,128)S(1)} collective-permute-done((f32[256,256]{1,0:T(8,128)S(1)}, f32[256,256]{1,0:T(8,128)S(1)}, u32[]{:S(2)}, u32[]{:S(2)}) %collective-permute-start.21) | collective-permute-done | bytes 262176 | tf_op jit(solution)/shard_map/ppermute | solution.py:32
  68.8 0.6 collective-permute-start.24
  69.4 10.2 %collective-permute-done.25.refs_1_ = f32[256,256]{1,0:T(8,128)S(1)} collective-permute-done((f32[256,256]{1,0:T(8,128)S(1)}, f32[256,256]{1,0:T(8,128)S(1)}, u32[]{:S(2)}, u32[]{:S(2)}) %collective-permute-start.25) | collective-permute-done | bytes 262176 | tf_op jit(solution)/shard_map/ppermute | solution.py:32
  79.6 1.1 %finish.6 = (f32[512,1024]{1,0:T(8,128)}, f32[8,128]{1,0:T(8,128)S(1)}) custom-call(f32[256,256]{1,0:T(8,128)S(1)} %get-tuple-element.193.refs_0_, f32[256,256]{1,0:T(8,128)S(1)} %collective-permute-done.25.refs_1_, bf16[256,256]{1,0:T(8,128)(2,1)S(1)} %get-tuple-element.173.refs_2_, ...), custom_call_target="tpu_custom_call", output_to_operand_aliasing={{0}: (7, {})} | custom-call | flops 14949999616 | tf_op jit(solution)/shard_map/finish/pallas_call | solution.py:128
  80.7 3.4 %collective-permute-done.24.refs_1_ = f32[256,256]{1,0:T(8,128)S(1)} collective-permute-done((f32[256,256]{1,0:T(8,128)S(1)}, f32[256,256]{1,0:T(8,128)S(1)}, u32[]{:S(2)}, u32[]{:S(2)}) %collective-permute-start.24) | collective-permute-done | bytes 262176 | tf_op jit(solution)/shard_map/ppermute | solution.py:32
  84.1 1.2 %finish.7 = (f32[512,1024]{1,0:T(8,128)}, f32[8,128]{1,0:T(8,128)}) custom-call(f32[256,256]{1,0:T(8,128)S(1)} %get-tuple-element.192.refs_0_, f32[256,256]{1,0:T(8,128)S(1)} %collective-permute-done.24.refs_1_, bf16[256,256]{1,0:T(8,128)(2,1)S(1)} %get-tuple-element.173.refs_2_, ...), custom_call_target="tpu_custom_call", output_to_operand_aliasing={{0}: (7, {})} | custom-call | flops 14949999616 | tf_op jit(solution)/shard_map/finish/pallas_call | solution.py:128
  (43 shorter events, 4.7 us)
Async XLA Ops:
  0.0 10.4 %copy-start.1 = (f32[512,128]{1,0:T(8,128)S(1)}, f32[512,128]{1,0:T(8,128)}, u32[]{:S(2)}) copy-start(f32[512,128]{1,0:T(8,128)} %refs_0_.4) | copy-start | bytes 786436
  0.0 10.4 %copy-start = (f32[512,1024]{1,0:T(8,128)S(1)}, f32[512,1024]{1,0:T(8,128)}, u32[]{:S(2)}) copy-start(f32[512,1024]{1,0:T(8,128)} %refs_0_.5) | copy-start | bytes 6291460
  0.0 10.4 %collective-permute-start = (f32[512,128]{1,0:T(8,128)}, f32[512,128]{1,0:T(8,128)S(1)}, u32[]{:S(2)}, u32[]{:S(2)}) collective-permute-start(f32[512,128]{1,0:T(8,128)} %refs_0_.4), channel_id=1, source_target_pairs={{1,0},{0,1},{3,2},{2,3},{5,4},{4,5},{7,6},{6,7},{9,8},{8,9},{11,10... | collective-permute-start | bytes 786440 | tf_op jit(solution)/shard_map/ppermute | solution.py:38
  3.0 10.9 %collective-permute-start.1 = (f32[256,128]{1,0:T(8,128)}, f32[256,128]{1,0:T(8,128)S(1)}, u32[]{:S(2)}, u32[]{:S(2)}) collective-permute-start(f32[256,128]{1,0:T(8,128)} %refs_5_.1), channel_id=1, source_target_pairs={{1,0},{0,1},{3,2},{2,3},{5,4},{4,5},{7,6},{6,7},{9,8},{8,9},{11,10... | collective-permute-start | bytes 393224 | tf_op jit(solution)/shard_map/ppermute | solution.py:38
  4.2 10.6 %collective-permute-start.2 = (f32[256,128]{1,0:T(8,128)S(1)}, f32[256,128]{1,0:T(8,128)S(1)}, u32[]{:S(2)}, u32[]{:S(2)}) collective-permute-start(f32[256,128]{1,0:T(8,128)S(1)} %get-tuple-element.116.refs_7_), channel_id=1, source_target_pairs={{0,4},{2,6},{4,0},{6,2},{8,12},{10,14},{12,8},{14,10},{16,20},{18,... | collective-permute-start | bytes 393224 | tf_op jit(solution)/shard_map/ppermute | solution.py:32
  6.2 8.6 %collective-permute-start.3 = (f32[256,128]{1,0:T(8,128)S(1)}, f32[256,128]{1,0:T(8,128)S(1)}, u32[]{:S(2)}, u32[]{:S(2)}) collective-permute-start(f32[256,128]{1,0:T(8,128)S(1)} %get-tuple-element.117.refs_9_), channel_id=1, source_target_pairs={{0,8},{2,10},{4,12},{6,14},{8,0},{10,2},{12,4},{14,6},{16,24},{18,... | collective-permute-start | bytes 393224 | tf_op jit(solution)/shard_map/ppermute | solution.py:32
  7.7 8.2 %collective-permute-start.6 = (f32[256,128]{1,0:T(8,128)S(1)}, f32[256,128]{1,0:T(8,128)S(1)}, u32[]{:S(2)}, u32[]{:S(2)}) collective-permute-start(f32[256,128]{1,0:T(8,128)S(1)} %get-tuple-element.121.refs_2_), channel_id=1, source_target_pairs={{0,16},{2,18},{4,20},{6,22},{8,24},{10,26},{12,28},{14,30},{16,0},... | collective-permute-start | bytes 393224 | tf_op jit(solution)/shard_map/ppermute | solution.py:32
  10.9 5.0 %collective-permute-start.5 = (f32[256,128]{1,0:T(8,128)S(1)}, f32[256,128]{1,0:T(8,128)S(1)}, u32[]{:S(2)}, u32[]{:S(2)}) collective-permute-start(f32[256,128]{1,0:T(8,128)S(1)} %get-tuple-element.120.refs_0_), channel_id=1, source_target_pairs={{1,0},{0,1},{3,2},{2,3},{5,4},{4,5},{7,6},{6,7},{9,8},{8,9},{11,10... | collective-permute-start | bytes 393224 | tf_op jit(solution)/shard_map/ppermute | solution.py:38
  13.0 0.9 %copy-start.2 = (f32[256,128]{1,0:T(8,128)S(1)}, f32[256,128]{1,0:T(8,128)}, u32[]{:S(2)}) copy-start(f32[256,128]{1,0:T(8,128)} %refs_5_.1) | copy-start | bytes 393220
  14.7 3.9 %collective-permute-start.8 = (f32[256,256]{1,0:T(8,128)S(1)}, f32[256,256]{1,0:T(8,128)S(1)}, u32[]{:S(2)}, u32[]{:S(2)}) collective-permute-start(f32[256,256]{1,0:T(8,128)S(1)} %get-tuple-element.124.refs_0_), channel_id=1, source_target_pairs={{0,2},{2,0},{4,6},{6,4},{8,10},{10,8},{12,14},{14,12},{16,18},{18,... | collective-permute-start | bytes 786440 | tf_op jit(solution)/shard_map/ppermute | solution.py:32
  16.0 2.6 %collective-permute-start.7 = (f32[256,256]{1,0:T(8,128)S(1)}, f32[256,256]{1,0:T(8,128)S(1)}, u32[]{:S(2)}, u32[]{:S(2)}) collective-permute-start(f32[256,256]{1,0:T(8,128)S(1)} %get-tuple-element.123.refs_0_), channel_id=1, source_target_pairs={{0,2},{2,0},{4,6},{6,4},{8,10},{10,8},{12,14},{14,12},{16,18},{18,... | collective-permute-start | bytes 786440 | tf_op jit(solution)/shard_map/ppermute | solution.py:32
  16.6 5.2 %collective-permute-start.4 = (f32[768,256]{1,0:T(8,128)S(1)}, f32[768,256]{1,0:T(8,128)S(1)}, u32[]{:S(2)}, u32[]{:S(2)}) collective-permute-start(f32[768,256]{1,0:T(8,128)S(1)} %get-tuple-element.119.refs_0_), channel_id=1, source_target_pairs={{0,2},{2,0},{4,6},{6,4},{8,10},{10,8},{12,14},{14,12},{16,18},{18,... | collective-permute-start | bytes 2359304 | tf_op jit(solution)/shard_map/ppermute | solution.py:32
  16.7 8.7 %collective-permute-start.10 = (f32[512,128]{1,0:T(8,128)S(1)}, f32[512,128]{1,0:T(8,128)S(1)}, u32[]{:S(2)}, u32[]{:S(2)}) collective-permute-start(f32[512,128]{1,0:T(8,128)S(1)} %get-tuple-element.134.refs_0_), channel_id=1, source_target_pairs={{1,0},{0,1},{3,2},{2,3},{5,4},{4,5},{7,6},{6,7},{9,8},{8,9},{11,10... | collective-permute-start | bytes 786440 | tf_op jit(solution)/shard_map/ppermute | solution.py:38
  19.3 6.5 %collective-permute-start.9 = (f32[128,256]{1,0:T(8,128)S(1)}, f32[128,256]{1,0:T(8,128)S(1)}, u32[]{:S(2)}, u32[]{:S(2)}) collective-permute-start(f32[128,256]{1,0:T(8,128)S(1)} %get-tuple-element.133.refs_0_), channel_id=1, source_target_pairs={{0,4},{2,6},{4,0},{6,2},{8,12},{10,14},{12,8},{14,10},{16,20},{18,... | collective-permute-start | bytes 393224 | tf_op jit(solution)/shard_map/ppermute | solution.py:32
  21.1 7.4 %collective-permute-start.14 = (f32[128,256]{1,0:T(8,128)S(1)}, f32[128,256]{1,0:T(8,128)S(1)}, u32[]{:S(2)}, u32[]{:S(2)}) collective-permute-start(f32[128,256]{1,0:T(8,128)S(1)} %get-tuple-element.149.refs_0_), channel_id=1, source_target_pairs={{0,4},{2,6},{4,0},{6,2},{8,12},{10,14},{12,8},{14,10},{16,20},{18,... | collective-permute-start | bytes 393224 | tf_op jit(solution)/shard_map/ppermute | solution.py:32
  22.1 12.0 %collective-permute-start.13 = (f32[256,256]{1,0:T(8,128)S(1)}, f32[256,256]{1,0:T(8,128)S(1)}, u32[]{:S(2)}, u32[]{:S(2)}) collective-permute-start(f32[256,256]{1,0:T(8,128)S(1)} %get-tuple-element.148.refs_0_), channel_id=1, source_target_pairs={{0,4},{2,6},{4,0},{6,2},{8,12},{10,14},{12,8},{14,10},{16,20},{18,... | collective-permute-start | bytes 786440 | tf_op jit(solution)/shard_map/ppermute | solution.py:32
  23.7 12.5 %collective-permute-start.12 = (f32[512,128]{1,0:T(8,128)S(1)}, f32[512,128]{1,0:T(8,128)S(1)}, u32[]{:S(2)}, u32[]{:S(2)}) collective-permute-start(f32[512,128]{1,0:T(8,128)S(1)} %get-tuple-element.146.refs_0_), channel_id=1, source_target_pairs={{1,0},{0,1},{3,2},{2,3},{5,4},{4,5},{7,6},{6,7},{9,8},{8,9},{11,10... | collective-permute-start | bytes 786440 | tf_op jit(solution)/shard_map/ppermute | solution.py:38
  26.1 10.6 %collective-permute-start.11 = (f32[128,256]{1,0:T(8,128)S(1)}, f32[128,256]{1,0:T(8,128)S(1)}, u32[]{:S(2)}, u32[]{:S(2)}) collective-permute-start(f32[128,256]{1,0:T(8,128)S(1)} %get-tuple-element.145.refs_0_), channel_id=1, source_target_pairs={{0,8},{2,10},{4,12},{6,14},{8,0},{10,2},{12,4},{14,6},{16,24},{18,... | collective-permute-start | bytes 393224 | tf_op jit(solution)/shard_map/ppermute | solution.py:32
  28.8 7.9 %collective-permute-start.15 = (f32[128,256]{1,0:T(8,128)S(1)}, f32[128,256]{1,0:T(8,128)S(1)}, u32[]{:S(2)}, u32[]{:S(2)}) collective-permute-start(f32[128,256]{1,0:T(8,128)S(1)} %get-tuple-element.156.refs_2_), channel_id=1, source_target_pairs={{0,8},{2,10},{4,12},{6,14},{8,0},{10,2},{12,4},{14,6},{16,24},{18,... | collective-permute-start | bytes 393224 | tf_op jit(solution)/shard_map/ppermute | solution.py:32
  30.8 11.8 %collective-permute-start.19 = (f32[256,256]{1,0:T(8,128)S(1)}, f32[256,256]{1,0:T(8,128)S(1)}, u32[]{:S(2)}, u32[]{:S(2)}) collective-permute-start(f32[256,256]{1,0:T(8,128)S(1)} %get-tuple-element.166.refs_0_), channel_id=1, source_target_pairs={{0,4},{2,6},{4,0},{6,2},{8,12},{10,14},{12,8},{14,10},{16,20},{18,... | collective-permute-start | bytes 786440 | tf_op jit(solution)/shard_map/ppermute | solution.py:32
  34.5 12.5 %collective-permute-start.18 = (f32[256,256]{1,0:T(8,128)S(1)}, f32[256,256]{1,0:T(8,128)S(1)}, u32[]{:S(2)}, u32[]{:S(2)}) collective-permute-start(f32[256,256]{1,0:T(8,128)S(1)} %get-tuple-element.165.refs_0_), channel_id=1, source_target_pairs={{0,8},{2,10},{4,12},{6,14},{8,0},{10,2},{12,4},{14,6},{16,24},{18,... | collective-permute-start | bytes 786440 | tf_op jit(solution)/shard_map/ppermute | solution.py:32
  37.0 14.1 %collective-permute-start.17 = (f32[256,256]{1,0:T(8,128)S(1)}, f32[256,256]{1,0:T(8,128)S(1)}, u32[]{:S(2)}, u32[]{:S(2)}) collective-permute-start(f32[256,256]{1,0:T(8,128)S(1)} %get-tuple-element.164.refs_0_), channel_id=1, source_target_pairs={{0,16},{2,18},{4,20},{6,22},{8,24},{10,26},{12,28},{14,30},{16,0},... | collective-permute-start | bytes 786440 | tf_op jit(solution)/shard_map/ppermute | solution.py:32
  39.7 11.4 %collective-permute-start.20 = (f32[512,128]{1,0:T(8,128)S(1)}, f32[512,128]{1,0:T(8,128)S(1)}, u32[]{:S(2)}, u32[]{:S(2)}) collective-permute-start(f32[512,128]{1,0:T(8,128)S(1)} %get-tuple-element.171.refs_0_), channel_id=1, source_target_pairs={{1,0},{0,1},{3,2},{2,3},{5,4},{4,5},{7,6},{6,7},{9,8},{8,9},{11,10... | collective-permute-start | bytes 786440 | tf_op jit(solution)/shard_map/ppermute | solution.py:38
  41.0 13.5 %collective-permute-start.16 = (f32[256,256]{1,0:T(8,128)S(1)}, f32[256,256]{1,0:T(8,128)S(1)}, u32[]{:S(2)}, u32[]{:S(2)}) collective-permute-start(f32[256,256]{1,0:T(8,128)S(1)} %get-tuple-element.163.refs_0_), channel_id=1, source_target_pairs={{0,4},{2,6},{4,0},{6,2},{8,12},{10,14},{12,8},{14,10},{16,20},{18,... | collective-permute-start | bytes 786440 | tf_op jit(solution)/shard_map/ppermute | solution.py:32
  43.0 15.2 %collective-permute-start.23 = (f32[256,256]{1,0:T(8,128)S(1)}, f32[256,256]{1,0:T(8,128)S(1)}, u32[]{:S(2)}, u32[]{:S(2)}) collective-permute-start(f32[256,256]{1,0:T(8,128)S(1)} %get-tuple-element.187.refs_0_), channel_id=1, source_target_pairs={{0,8},{2,10},{4,12},{6,14},{8,0},{10,2},{12,4},{14,6},{16,24},{18,... | collective-permute-start | bytes 786440 | tf_op jit(solution)/shard_map/ppermute | solution.py:32
  47.4 13.9 %collective-permute-start.22 = (f32[256,256]{1,0:T(8,128)S(1)}, f32[256,256]{1,0:T(8,128)S(1)}, u32[]{:S(2)}, u32[]{:S(2)}) collective-permute-start(f32[256,256]{1,0:T(8,128)S(1)} %get-tuple-element.186.refs_0_), channel_id=1, source_target_pairs={{0,16},{2,18},{4,20},{6,22},{8,24},{10,26},{12,28},{14,30},{16,0},... | collective-permute-start | bytes 786440 | tf_op jit(solution)/shard_map/ppermute | solution.py:32
  54.9 13.5 %collective-permute-start.21 = (f32[256,256]{1,0:T(8,128)S(1)}, f32[256,256]{1,0:T(8,128)S(1)}, u32[]{:S(2)}, u32[]{:S(2)}) collective-permute-start(f32[256,256]{1,0:T(8,128)S(1)} %get-tuple-element.185.refs_0_), channel_id=1, source_target_pairs={{0,8},{2,10},{4,12},{6,14},{8,0},{10,2},{12,4},{14,6},{16,24},{18,... | collective-permute-start | bytes 786440 | tf_op jit(solution)/shard_map/ppermute | solution.py:32
  58.6 21.0 %collective-permute-start.25 = (f32[256,256]{1,0:T(8,128)S(1)}, f32[256,256]{1,0:T(8,128)S(1)}, u32[]{:S(2)}, u32[]{:S(2)}) collective-permute-start(f32[256,256]{1,0:T(8,128)S(1)} %get-tuple-element.193.refs_0_), channel_id=1, source_target_pairs={{0,16},{2,18},{4,20},{6,22},{8,24},{10,26},{12,28},{14,30},{16,0},... | collective-permute-start | bytes 786440 | tf_op jit(solution)/shard_map/ppermute | solution.py:32
  68.8 15.3 %collective-permute-start.24 = (f32[256,256]{1,0:T(8,128)S(1)}, f32[256,256]{1,0:T(8,128)S(1)}, u32[]{:S(2)}, u32[]{:S(2)}) collective-permute-start(f32[256,256]{1,0:T(8,128)S(1)} %get-tuple-element.192.refs_0_), channel_id=1, source_target_pairs={{0,16},{2,18},{4,20},{6,22},{8,24},{10,26},{12,28},{14,30},{16,0},... | collective-permute-start | bytes 786440 | tf_op jit(solution)/shard_map/ppermute | solution.py:32

commit v6 on v5

--- a/solution.py
+++ b/solution.py
@@ -423,7 +423,7 @@
         if not last:
             (top,) = line(body, "combine", inputs, [held(width, size)])
             tops[s + 1].append((start, width, top, swapped(top, "row", s + 1)))
-            if levels > 2 and (s, c) == (0, min(2, len(cuts[1]) - 1)):
+            if levels > 2 and (s, c) == (1, 0):
                 (stacks[2],) = line(hand_on, "hand", [stacks[2]], [held(2 * size, piece)])
         else:
             if out is None:

time: 85.4 us -> 85.4 us (level)
    ppermute x6, waiting for transfers between devices: 0.6 us -> 1.68 us  [turned(): lax.ppermute(value, axis, [((to + step) % size, to) for to in range(size)])]
    ppermute x20, waiting for transfers between devices: 28.8 us -> 27.8 us  [swapped(): return lax.ppermute(value, axis, pairs)]
  transfers between devices with their start and end apart: 26 -> 26, of which waited for: 10 -> 9; matrix products, arithmetic and copies ran while one was open for 0% -> 0% of each run, Pallas kernels for 19% -> 19%
where the time goes in v6:
time: 85.4 us; the launch traced here: 85.2 us
  starting transfers between devices  37.9 us (44%)
  waiting for transfers between devices  29.5 us (35%)
  Pallas kernels  17.5 us (20%)
    ppermute x20, starting transfers between devices, swapped(): return lax.ppermute(value, axis, pairs)  28.3 us
    ppermute x20, waiting for transfers between devices, swapped(): return lax.ppermute(value, axis, pairs)  27.8 us
    pallas_call x33, Pallas kernels, __call__(): pl.pallas_call(kernel, grid=grid, out_shape=out_shape, in_specs=in_specs,...  17.5 us
    ppermute x6, starting transfers between devices, turned(): lax.ppermute(value, axis, [((to + step) % size, to) for to in range(size)])  9.61 us
  transfers between devices with their start and end apart: 26, of which 9 were waited for; matrix products, arithmetic and copies ran while one was open for 0% of the time, Pallas kernels for 19%

profile of v6, /device:TPU:0, one launch (start us, length us, event | category | flops | bytes accessed | tf_op | source)
XLA Modules:
  0.0 85.2 jit_solution(17901552976880501399)
XLA Ops:
  0.0 3.0 %collective-permute-start = (f32[512,128]{1,0:T(8,128)}, f32[512,128]{1,0:T(8,128)S(1)}, u32[]{:S(2)}, u32[]{:S(2)}) collective-permute-start(f32[512,128]{1,0:T(8,128)} %refs_0_.4), channel_id=1, source_target_pairs={{1,0},{0,1},{3,2},{2,3},{5,4},{4,5},{7,6},{6,7},{9,8},{8,9},{11,10... | collective-permute-start | bytes 786440 | tf_op jit(solution)/shard_map/ppermute | solution.py:38
  3.0 1.1 %pick.1 = (f32[256,128]{1,0:T(8,128)S(1)}, f32[256,128]{1,0:T(8,128)S(1)}, f32[256,128]{1,0:T(8,128)S(1)}, f32[256,128]{1,0:T(8,128)S(1)}, f32[8,128]{1,0:T(8,128)S(1)}) custom-call(f32[4,256,128]{2,1,0:T(8,128)} %refs_0_.3, f32[4,256,128]{2,1,0:T(8,128)} %refs_1_.1), custom_call_target="tpu_custom_call" | custom-call | flops 12650000384 | tf_op jit(solution)/shard_map/pick/pallas_call | solution.py:128
  4.2 2.0 %collective-permute-start.2 = (f32[256,128]{1,0:T(8,128)S(1)}, f32[256,128]{1,0:T(8,128)S(1)}, u32[]{:S(2)}, u32[]{:S(2)}) collective-permute-start(f32[256,128]{1,0:T(8,128)S(1)} %get-tuple-element.116.refs_7_), channel_id=1, source_target_pairs={{0,4},{2,6},{4,0},{6,2},{8,12},{10,14},{12,8},{14,10},{16,20},{18,... | collective-permute-start | bytes 393224 | tf_op jit(solution)/shard_map/ppermute | solution.py:32
  6.2 1.6 %collective-permute-start.3 = (f32[256,128]{1,0:T(8,128)S(1)}, f32[256,128]{1,0:T(8,128)S(1)}, u32[]{:S(2)}, u32[]{:S(2)}) collective-permute-start(f32[256,128]{1,0:T(8,128)S(1)} %get-tuple-element.117.refs_9_), channel_id=1, source_target_pairs={{0,8},{2,10},{4,12},{6,14},{8,0},{10,2},{12,4},{14,6},{16,24},{18,... | collective-permute-start | bytes 393224 | tf_op jit(solution)/shard_map/ppermute | solution.py:32
  7.7 2.6 %collective-permute-start.6 = (f32[256,128]{1,0:T(8,128)S(1)}, f32[256,128]{1,0:T(8,128)S(1)}, u32[]{:S(2)}, u32[]{:S(2)}) collective-permute-start(f32[256,128]{1,0:T(8,128)S(1)} %get-tuple-element.121.refs_2_), channel_id=1, source_target_pairs={{0,16},{2,18},{4,20},{6,22},{8,24},{10,26},{12,28},{14,30},{16,0},... | collective-permute-start | bytes 393224 | tf_op jit(solution)/shard_map/ppermute | solution.py:32
  10.4 0.5 inner.1
  10.9 2.1 %collective-permute-start.5 = (f32[256,128]{1,0:T(8,128)S(1)}, f32[256,128]{1,0:T(8,128)S(1)}, u32[]{:S(2)}, u32[]{:S(2)}) collective-permute-start(f32[256,128]{1,0:T(8,128)S(1)} %get-tuple-element.120.refs_0_), channel_id=1, source_target_pairs={{1,0},{0,1},{3,2},{2,3},{5,4},{4,5},{7,6},{6,7},{9,8},{8,9},{11,10... | collective-permute-start | bytes 393224 | tf_op jit(solution)/shard_map/ppermute | solution.py:38
  13.0 0.9 %later.1 = (bf16[256,768]{1,0:T(8,128)(2,1)S(1)}, bf16[256,768]{1,0:T(8,128)(2,1)S(1)}, f32[8,128]{1,0:T(8,128)S(1)}) custom-call(bf16[256,512]{1,0:T(8,128)(2,1)S(1)} %get-tuple-element.104.refs_0_, bf16[256,512]{1,0:T(8,128)(2,1)S(1)} %get-tuple-element.105.refs_1_, f32[512,1024]{1,0:T(8,128)S(1)} %copy-done, f32[8,128]{1,0:T(8,128)S(1)} %get-tuple-element.106.refs_3_), custom_call_target="tpu_custom_call" | custom-call | flops 27599998976 | tf_op jit(solution)/shard_map/later/pallas_call | solution.py:128
  13.9 0.8 first.1
  14.8 1.2 %tops.1 = (f32[768,256]{1,0:T(8,128)S(1)}, bf16[256,768]{1,0:T(8,128)(2,1)S(1)}, bf16[256,768]{1,0:T(8,128)(2,1)S(1)}, f32[512,128]{1,0:T(8,128)S(1)}, f32[512,128]{1,0:T(8,128)S(1)}, /*index=5*/f32[8,128]{1,0:T(8,128)S(1)}) custom-call(bf16[256,768]{1,0:T(8,128)(2,1)S(1)} %get-tuple-element.107.refs_0_, bf16[256,768]{1,0:T(8,128)(2,1)S(1)} %get-tuple-element.108.refs_1_, ...), custom_call_target="tpu_custom_call" | custom-call | flops 11500000256 | tf_op jit(solution)/shard_map/tops/pallas_call | solution.py:128
  16.0 0.5 collective-permute-start.7
  16.7 1.9 %collective-permute-start.10 = (f32[512,128]{1,0:T(8,128)S(1)}, f32[512,128]{1,0:T(8,128)S(1)}, u32[]{:S(2)}, u32[]{:S(2)}) collective-permute-start(f32[512,128]{1,0:T(8,128)S(1)} %get-tuple-element.134.refs_0_), channel_id=1, source_target_pairs={{1,0},{0,1},{3,2},{2,3},{5,4},{4,5},{7,6},{6,7},{9,8},{8,9},{11,10... | collective-permute-start | bytes 786440 | tf_op jit(solution)/shard_map/ppermute | solution.py:38
  18.6 0.4 node.4
  19.3 1.6 %collective-permute-start.9 = (f32[128,256]{1,0:T(8,128)S(1)}, f32[128,256]{1,0:T(8,128)S(1)}, u32[]{:S(2)}, u32[]{:S(2)}) collective-permute-start(f32[128,256]{1,0:T(8,128)S(1)} %get-tuple-element.133.refs_0_), channel_id=1, source_target_pairs={{0,4},{2,6},{4,0},{6,2},{8,12},{10,14},{12,8},{14,10},{16,20},{18,... | collective-permute-start | bytes 393224 | tf_op jit(solution)/shard_map/ppermute | solution.py:32
  21.1 0.6 collective-permute-start.14
  21.7 0.4 combine.16
  22.1 1.6 %collective-permute-start.13 = (f32[256,256]{1,0:T(8,128)S(1)}, f32[256,256]{1,0:T(8,128)S(1)}, u32[]{:S(2)}, u32[]{:S(2)}) collective-permute-start(f32[256,256]{1,0:T(8,128)S(1)} %get-tuple-element.148.refs_0_), channel_id=1, source_target_pairs={{0,4},{2,6},{4,0},{6,2},{8,12},{10,14},{12,8},{14,10},{16,20},{18,... | collective-permute-start | bytes 786440 | tf_op jit(solution)/shard_map/ppermute | solution.py:32
  23.7 1.6 %collective-permute-done.10.refs_1_ = f32[512,128]{1,0:T(8,128)S(1)} collective-permute-done((f32[512,128]{1,0:T(8,128)S(1)}, f32[512,128]{1,0:T(8,128)S(1)}, u32[]{:S(2)}, u32[]{:S(2)}) %collective-permute-start.10) | collective-permute-done | bytes 262176 | tf_op jit(solution)/shard_map/ppermute | solution.py:38
  25.3 0.4 node.5
  26.1 1.6 %collective-permute-start.12 = (f32[512,128]{1,0:T(8,128)S(1)}, f32[512,128]{1,0:T(8,128)S(1)}, u32[]{:S(2)}, u32[]{:S(2)}) collective-permute-start(f32[512,128]{1,0:T(8,128)S(1)} %get-tuple-element.146.refs_0_), channel_id=1, source_target_pairs={{1,0},{0,1},{3,2},{2,3},{5,4},{4,5},{7,6},{6,7},{9,8},{8,9},{11,10... | collective-permute-start | bytes 786440 | tf_op jit(solution)/shard_map/ppermute | solution.py:38
  27.7 1.6 %collective-permute-start.11 = (f32[128,256]{1,0:T(8,128)S(1)}, f32[128,256]{1,0:T(8,128)S(1)}, u32[]{:S(2)}, u32[]{:S(2)}) collective-permute-start(f32[128,256]{1,0:T(8,128)S(1)} %get-tuple-element.143.refs_0_), channel_id=1, source_target_pairs={{0,8},{2,10},{4,12},{6,14},{8,0},{10,2},{12,4},{14,6},{16,24},{18,... | collective-permute-start | bytes 393224 | tf_op jit(solution)/shard_map/ppermute | solution.py:32
  29.6 0.9 %collective-permute-start.15 = (f32[128,256]{1,0:T(8,128)S(1)}, f32[128,256]{1,0:T(8,128)S(1)}, u32[]{:S(2)}, u32[]{:S(2)}) collective-permute-start(f32[128,256]{1,0:T(8,128)S(1)} %get-tuple-element.156.refs_2_), channel_id=1, source_target_pairs={{0,8},{2,10},{4,12},{6,14},{8,0},{10,2},{12,4},{14,6},{16,24},{18,... | collective-permute-start | bytes 393224 | tf_op jit(solution)/shard_map/ppermute | solution.py:32
  30.8 1.6 %collective-permute-start.19 = (f32[256,256]{1,0:T(8,128)S(1)}, f32[256,256]{1,0:T(8,128)S(1)}, u32[]{:S(2)}, u32[]{:S(2)}) collective-permute-start(f32[256,256]{1,0:T(8,128)S(1)} %get-tuple-element.166.refs_0_), channel_id=1, source_target_pairs={{0,4},{2,6},{4,0},{6,2},{8,12},{10,14},{12,8},{14,10},{16,20},{18,... | collective-permute-start | bytes 786440 | tf_op jit(solution)/shard_map/ppermute | solution.py:32
  32.5 1.7 %collective-permute-done.13.refs_1_ = f32[256,256]{1,0:T(8,128)S(1)} collective-permute-done((f32[256,256]{1,0:T(8,128)S(1)}, f32[256,256]{1,0:T(8,128)S(1)}, u32[]{:S(2)}, u32[]{:S(2)}) %collective-permute-start.13) | collective-permute-done | bytes 262176 | tf_op jit(solution)/shard_map/ppermute | solution.py:32
  34.5 1.6 %collective-permute-start.18 = (f32[256,256]{1,0:T(8,128)S(1)}, f32[256,256]{1,0:T(8,128)S(1)}, u32[]{:S(2)}, u32[]{:S(2)}) collective-permute-start(f32[256,256]{1,0:T(8,128)S(1)} %get-tuple-element.165.refs_0_), channel_id=1, source_target_pairs={{0,8},{2,10},{4,12},{6,14},{8,0},{10,2},{12,4},{14,6},{16,24},{18,... | collective-permute-start | bytes 786440 | tf_op jit(solution)/shard_map/ppermute | solution.py:32
  36.2 0.5 node.6
  37.0 2.7 %collective-permute-start.17 = (f32[256,256]{1,0:T(8,128)S(1)}, f32[256,256]{1,0:T(8,128)S(1)}, u32[]{:S(2)}, u32[]{:S(2)}) collective-permute-start(f32[256,256]{1,0:T(8,128)S(1)} %get-tuple-element.164.refs_0_), channel_id=1, source_target_pairs={{0,16},{2,18},{4,20},{6,22},{8,24},{10,26},{12,28},{14,30},{16,0},... | collective-permute-start | bytes 786440 | tf_op jit(solution)/shard_map/ppermute | solution.py:32
  39.7 0.9 %collective-permute-start.20 = (f32[512,128]{1,0:T(8,128)S(1)}, f32[512,128]{1,0:T(8,128)S(1)}, u32[]{:S(2)}, u32[]{:S(2)}) collective-permute-start(f32[512,128]{1,0:T(8,128)S(1)} %get-tuple-element.171.refs_0_), channel_id=1, source_target_pairs={{1,0},{0,1},{3,2},{2,3},{5,4},{4,5},{7,6},{6,7},{9,8},{8,9},{11,10... | collective-permute-start | bytes 786440 | tf_op jit(solution)/shard_map/ppermute | solution.py:38
  41.0 1.6 %collective-permute-start.16 = (f32[256,256]{1,0:T(8,128)S(1)}, f32[256,256]{1,0:T(8,128)S(1)}, u32[]{:S(2)}, u32[]{:S(2)}) collective-permute-start(f32[256,256]{1,0:T(8,128)S(1)} %get-tuple-element.163.refs_0_), channel_id=1, source_target_pairs={{0,4},{2,6},{4,0},{6,2},{8,12},{10,14},{12,8},{14,10},{16,20},{18,... | collective-permute-start | bytes 786440 | tf_op jit(solution)/shard_map/ppermute | solution.py:32
  42.6 0.4 combine.23
  43.0 0.9 %collective-permute-start.23 = (f32[256,256]{1,0:T(8,128)S(1)}, f32[256,256]{1,0:T(8,128)S(1)}, u32[]{:S(2)}, u32[]{:S(2)}) collective-permute-start(f32[256,256]{1,0:T(8,128)S(1)} %get-tuple-element.187.refs_0_), channel_id=1, source_target_pairs={{0,8},{2,10},{4,12},{6,14},{8,0},{10,2},{12,4},{14,6},{16,24},{18,... | collective-permute-start | bytes 786440 | tf_op jit(solution)/shard_map/ppermute | solution.py:32
  43.9 3.1 %collective-permute-done.18.refs_1_ = f32[256,256]{1,0:T(8,128)S(1)} collective-permute-done((f32[256,256]{1,0:T(8,128)S(1)}, f32[256,256]{1,0:T(8,128)S(1)}, u32[]{:S(2)}, u32[]{:S(2)}) %collective-permute-start.18) | collective-permute-done | bytes 262176 | tf_op jit(solution)/shard_map/ppermute | solution.py:32
  47.0 0.4 combine.24
  47.4 2.2 %collective-permute-start.22 = (f32[256,256]{1,0:T(8,128)S(1)}, f32[256,256]{1,0:T(8,128)S(1)}, u32[]{:S(2)}, u32[]{:S(2)}) collective-permute-start(f32[256,256]{1,0:T(8,128)S(1)} %get-tuple-element.186.refs_0_), channel_id=1, source_target_pairs={{0,16},{2,18},{4,20},{6,22},{8,24},{10,26},{12,28},{14,30},{16,0},... | collective-permute-start | bytes 786440 | tf_op jit(solution)/shard_map/ppermute | solution.py:32
  49.6 1.5 %collective-permute-done.17.refs_0_ = f32[256,256]{1,0:T(8,128)S(1)} collective-permute-done((f32[256,256]{1,0:T(8,128)S(1)}, f32[256,256]{1,0:T(8,128)S(1)}, u32[]{:S(2)}, u32[]{:S(2)}) %collective-permute-start.17) | collective-permute-done | bytes 262176 | tf_op jit(solution)/shard_map/ppermute | solution.py:32
  51.2 0.6 node.7
  51.8 1.5 %rest.1 = (f32[512,1024]{1,0:T(8,128)}, f32[8,128]{1,0:T(8,128)S(1)}) custom-call(f32[512,1024]{1,0:T(8,128)S(1)} %copy-done, bf16[512,256]{1,0:T(8,128)(2,1)S(1)} %get-tuple-element.109.refs_2_.refs_1_, bf16[512,256]{1,0:T(8,128)(2,1)S(1)} %get-tuple-element.110.refs_3_.refs_2_, bf16[256,256]{1,0:T(8,128)(2,1)S(1)} %get-tuple-element.177.refs_3_, ...), custom_call_target="tpu_custom_call" | custom-call | flops 19549999104 | tf_op jit(solution)/shard_map/rest/pallas_call | solution.py:128
  53.4 1.2 %finish.4 = (f32[512,1024]{1,0:T(8,128)}, f32[8,128]{1,0:T(8,128)S(1)}) custom-call(f32[256,256]{1,0:T(8,128)S(1)} %get-tuple-element.164.refs_0_, f32[256,256]{1,0:T(8,128)S(1)} %get-tuple-element.170.refs_1_, bf16[256,256]{1,0:T(8,128)(2,1)S(1)} %get-tuple-element.173.refs_2_, ...), custom_call_target="tpu_custom_call", output_to_operand_aliasing={{0}: (7, {})} | custom-call | flops 14949999616 | tf_op jit(solution)/shard_map/finish/pallas_call | solution.py:128
  54.9 1.5 %collective-permute-start.21 = (f32[256,256]{1,0:T(8,128)S(1)}, f32[256,256]{1,0:T(8,128)S(1)}, u32[]{:S(2)}, u32[]{:S(2)}) collective-permute-start(f32[256,256]{1,0:T(8,128)S(1)} %get-tuple-element.185.refs_0_), channel_id=1, source_target_pairs={{0,8},{2,10},{4,12},{6,14},{8,0},{10,2},{12,4},{14,6},{16,24},{18,... | collective-permute-start | bytes 786440 | tf_op jit(solution)/shard_map/ppermute | solution.py:32
  56.4 1.8 %collective-permute-done.23.refs_1_ = f32[256,256]{1,0:T(8,128)S(1)} collective-permute-done((f32[256,256]{1,0:T(8,128)S(1)}, f32[256,256]{1,0:T(8,128)S(1)}, u32[]{:S(2)}, u32[]{:S(2)}) %collective-permute-start.23) | collective-permute-done | bytes 262176 | tf_op jit(solution)/shard_map/ppermute | solution.py:32
  58.6 2.5 %collective-permute-start.25 = (f32[256,256]{1,0:T(8,128)S(1)}, f32[256,256]{1,0:T(8,128)S(1)}, u32[]{:S(2)}, u32[]{:S(2)}) collective-permute-start(f32[256,256]{1,0:T(8,128)S(1)} %get-tuple-element.193.refs_0_), channel_id=1, source_target_pairs={{0,16},{2,18},{4,20},{6,22},{8,24},{10,26},{12,28},{14,30},{16,0},... | collective-permute-start | bytes 786440 | tf_op jit(solution)/shard_map/ppermute | solution.py:32
  61.3 1.2 %finish.5 = (f32[512,1024]{1,0:T(8,128)}, f32[8,128]{1,0:T(8,128)S(1)}) custom-call(f32[256,256]{1,0:T(8,128)S(1)} %get-tuple-element.186.refs_0_, f32[256,256]{1,0:T(8,128)S(1)} %collective-permute-done.22.refs_1_, bf16[256,256]{1,0:T(8,128)(2,1)S(1)} %get-tuple-element.173.refs_2_, ...), custom_call_target="tpu_custom_call", output_to_operand_aliasing={{0}: (7, {})} | custom-call | flops 14949999616 | tf_op jit(solution)/shard_map/finish/pallas_call | solution.py:128
  62.5 5.9 %collective-permute-done.21.refs_1_ = f32[256,256]{1,0:T(8,128)S(1)} collective-permute-done((f32[256,256]{1,0:T(8,128)S(1)}, f32[256,256]{1,0:T(8,128)S(1)}, u32[]{:S(2)}, u32[]{:S(2)}) %collective-permute-start.21) | collective-permute-done | bytes 262176 | tf_op jit(solution)/shard_map/ppermute | solution.py:32
  68.8 0.6 collective-permute-start.24
  69.4 10.2 %collective-permute-done.25.refs_1_ = f32[256,256]{1,0:T(8,128)S(1)} collective-permute-done((f32[256,256]{1,0:T(8,128)S(1)}, f32[256,256]{1,0:T(8,128)S(1)}, u32[]{:S(2)}, u32[]{:S(2)}) %collective-permute-start.25) | collective-permute-done | bytes 262176 | tf_op jit(solution)/shard_map/ppermute | solution.py:32
  79.6 1.1 %finish.6 = (f32[512,1024]{1,0:T(8,128)}, f32[8,128]{1,0:T(8,128)S(1)}) custom-call(f32[256,256]{1,0:T(8,128)S(1)} %get-tuple-element.193.refs_0_, f32[256,256]{1,0:T(8,128)S(1)} %collective-permute-done.25.refs_1_, bf16[256,256]{1,0:T(8,128)(2,1)S(1)} %get-tuple-element.173.refs_2_, ...), custom_call_target="tpu_custom_call", output_to_operand_aliasing={{0}: (7, {})} | custom-call | flops 14949999616 | tf_op jit(solution)/shard_map/finish/pallas_call | solution.py:128
  80.7 3.3 %collective-permute-done.24.refs_1_ = f32[256,256]{1,0:T(8,128)S(1)} collective-permute-done((f32[256,256]{1,0:T(8,128)S(1)}, f32[256,256]{1,0:T(8,128)S(1)}, u32[]{:S(2)}, u32[]{:S(2)}) %collective-permute-start.24) | collective-permute-done | bytes 262176 | tf_op jit(solution)/shard_map/ppermute | solution.py:32
  84.1 1.2 %finish.7 = (f32[512,1024]{1,0:T(8,128)}, f32[8,128]{1,0:T(8,128)}) custom-call(f32[256,256]{1,0:T(8,128)S(1)} %get-tuple-element.192.refs_0_, f32[256,256]{1,0:T(8,128)S(1)} %collective-permute-done.24.refs_1_, bf16[256,256]{1,0:T(8,128)(2,1)S(1)} %get-tuple-element.173.refs_2_, ...), custom_call_target="tpu_custom_call", output_to_operand_aliasing={{0}: (7, {})} | custom-call | flops 14949999616 | tf_op jit(solution)/shard_map/finish/pallas_call | solution.py:128
  (43 shorter events, 4.4 us)
Async XLA Ops:
  0.0 10.4 %copy-start.1 = (f32[512,128]{1,0:T(8,128)S(1)}, f32[512,128]{1,0:T(8,128)}, u32[]{:S(2)}) copy-start(f32[512,128]{1,0:T(8,128)} %refs_0_.4) | copy-start | bytes 786436
  0.0 10.4 %copy-start = (f32[512,1024]{1,0:T(8,128)S(1)}, f32[512,1024]{1,0:T(8,128)}, u32[]{:S(2)}) copy-start(f32[512,1024]{1,0:T(8,128)} %refs_0_.5) | copy-start | bytes 6291460
  0.0 10.4 %collective-permute-start = (f32[512,128]{1,0:T(8,128)}, f32[512,128]{1,0:T(8,128)S(1)}, u32[]{:S(2)}, u32[]{:S(2)}) collective-permute-start(f32[512,128]{1,0:T(8,128)} %refs_0_.4), channel_id=1, source_target_pairs={{1,0},{0,1},{3,2},{2,3},{5,4},{4,5},{7,6},{6,7},{9,8},{8,9},{11,10... | collective-permute-start | bytes 786440 | tf_op jit(solution)/shard_map/ppermute | solution.py:38
  3.0 10.9 %collective-permute-start.1 = (f32[256,128]{1,0:T(8,128)}, f32[256,128]{1,0:T(8,128)S(1)}, u32[]{:S(2)}, u32[]{:S(2)}) collective-permute-start(f32[256,128]{1,0:T(8,128)} %refs_5_.1), channel_id=1, source_target_pairs={{1,0},{0,1},{3,2},{2,3},{5,4},{4,5},{7,6},{6,7},{9,8},{8,9},{11,10... | collective-permute-start | bytes 393224 | tf_op jit(solution)/shard_map/ppermute | solution.py:38
  4.2 10.6 %collective-permute-start.2 = (f32[256,128]{1,0:T(8,128)S(1)}, f32[256,128]{1,0:T(8,128)S(1)}, u32[]{:S(2)}, u32[]{:S(2)}) collective-permute-start(f32[256,128]{1,0:T(8,128)S(1)} %get-tuple-element.116.refs_7_), channel_id=1, source_target_pairs={{0,4},{2,6},{4,0},{6,2},{8,12},{10,14},{12,8},{14,10},{16,20},{18,... | collective-permute-start | bytes 393224 | tf_op jit(solution)/shard_map/ppermute | solution.py:32
  6.2 8.6 %collective-permute-start.3 = (f32[256,128]{1,0:T(8,128)S(1)}, f32[256,128]{1,0:T(8,128)S(1)}, u32[]{:S(2)}, u32[]{:S(2)}) collective-permute-start(f32[256,128]{1,0:T(8,128)S(1)} %get-tuple-element.117.refs_9_), channel_id=1, source_target_pairs={{0,8},{2,10},{4,12},{6,14},{8,0},{10,2},{12,4},{14,6},{16,24},{18,... | collective-permute-start | bytes 393224 | tf_op jit(solution)/shard_map/ppermute | solution.py:32
  7.7 8.2 %collective-permute-start.6 = (f32[256,128]{1,0:T(8,128)S(1)}, f32[256,128]{1,0:T(8,128)S(1)}, u32[]{:S(2)}, u32[]{:S(2)}) collective-permute-start(f32[256,128]{1,0:T(8,128)S(1)} %get-tuple-element.121.refs_2_), channel_id=1, source_target_pairs={{0,16},{2,18},{4,20},{6,22},{8,24},{10,26},{12,28},{14,30},{16,0},... | collective-permute-start | bytes 393224 | tf_op jit(solution)/shard_map/ppermute | solution.py:32
  10.9 5.0 %collective-permute-start.5 = (f32[256,128]{1,0:T(8,128)S(1)}, f32[256,128]{1,0:T(8,128)S(1)}, u32[]{:S(2)}, u32[]{:S(2)}) collective-permute-start(f32[256,128]{1,0:T(8,128)S(1)} %get-tuple-element.120.refs_0_), channel_id=1, source_target_pairs={{1,0},{0,1},{3,2},{2,3},{5,4},{4,5},{7,6},{6,7},{9,8},{8,9},{11,10... | collective-permute-start | bytes 393224 | tf_op jit(solution)/shard_map/ppermute | solution.py:38
  13.0 0.9 %copy-start.2 = (f32[256,128]{1,0:T(8,128)S(1)}, f32[256,128]{1,0:T(8,128)}, u32[]{:S(2)}) copy-start(f32[256,128]{1,0:T(8,128)} %refs_5_.1) | copy-start | bytes 393220
  14.7 3.9 %collective-permute-start.8 = (f32[256,256]{1,0:T(8,128)S(1)}, f32[256,256]{1,0:T(8,128)S(1)}, u32[]{:S(2)}, u32[]{:S(2)}) collective-permute-start(f32[256,256]{1,0:T(8,128)S(1)} %get-tuple-element.124.refs_0_), channel_id=1, source_target_pairs={{0,2},{2,0},{4,6},{6,4},{8,10},{10,8},{12,14},{14,12},{16,18},{18,... | collective-permute-start | bytes 786440 | tf_op jit(solution)/shard_map/ppermute | solution.py:32
  16.0 2.6 %collective-permute-start.7 = (f32[256,256]{1,0:T(8,128)S(1)}, f32[256,256]{1,0:T(8,128)S(1)}, u32[]{:S(2)}, u32[]{:S(2)}) collective-permute-start(f32[256,256]{1,0:T(8,128)S(1)} %get-tuple-element.123.refs_0_), channel_id=1, source_target_pairs={{0,2},{2,0},{4,6},{6,4},{8,10},{10,8},{12,14},{14,12},{16,18},{18,... | collective-permute-start | bytes 786440 | tf_op jit(solution)/shard_map/ppermute | solution.py:32
  16.6 5.2 %collective-permute-start.4 = (f32[768,256]{1,0:T(8,128)S(1)}, f32[768,256]{1,0:T(8,128)S(1)}, u32[]{:S(2)}, u32[]{:S(2)}) collective-permute-start(f32[768,256]{1,0:T(8,128)S(1)} %get-tuple-element.119.refs_0_), channel_id=1, source_target_pairs={{0,2},{2,0},{4,6},{6,4},{8,10},{10,8},{12,14},{14,12},{16,18},{18,... | collective-permute-start | bytes 2359304 | tf_op jit(solution)/shard_map/ppermute | solution.py:32
  16.7 8.7 %collective-permute-start.10 = (f32[512,128]{1,0:T(8,128)S(1)}, f32[512,128]{1,0:T(8,128)S(1)}, u32[]{:S(2)}, u32[]{:S(2)}) collective-permute-start(f32[512,128]{1,0:T(8,128)S(1)} %get-tuple-element.134.refs_0_), channel_id=1, source_target_pairs={{1,0},{0,1},{3,2},{2,3},{5,4},{4,5},{7,6},{6,7},{9,8},{8,9},{11,10... | collective-permute-start | bytes 786440 | tf_op jit(solution)/shard_map/ppermute | solution.py:38
  19.3 6.4 %collective-permute-start.9 = (f32[128,256]{1,0:T(8,128)S(1)}, f32[128,256]{1,0:T(8,128)S(1)}, u32[]{:S(2)}, u32[]{:S(2)}) collective-permute-start(f32[128,256]{1,0:T(8,128)S(1)} %get-tuple-element.133.refs_0_), channel_id=1, source_target_pairs={{0,4},{2,6},{4,0},{6,2},{8,12},{10,14},{12,8},{14,10},{16,20},{18,... | collective-permute-start | bytes 393224 | tf_op jit(solution)/shard_map/ppermute | solution.py:32
  21.1 8.2 %collective-permute-start.14 = (f32[128,256]{1,0:T(8,128)S(1)}, f32[128,256]{1,0:T(8,128)S(1)}, u32[]{:S(2)}, u32[]{:S(2)}) collective-permute-start(f32[128,256]{1,0:T(8,128)S(1)} %get-tuple-element.149.refs_0_), channel_id=1, source_target_pairs={{0,4},{2,6},{4,0},{6,2},{8,12},{10,14},{12,8},{14,10},{16,20},{18,... | collective-permute-start | bytes 393224 | tf_op jit(solution)/shard_map/ppermute | solution.py:32
  22.1 12.0 %collective-permute-start.13 = (f32[256,256]{1,0:T(8,128)S(1)}, f32[256,256]{1,0:T(8,128)S(1)}, u32[]{:S(2)}, u32[]{:S(2)}) collective-permute-start(f32[256,256]{1,0:T(8,128)S(1)} %get-tuple-element.148.refs_0_), channel_id=1, source_target_pairs={{0,4},{2,6},{4,0},{6,2},{8,12},{10,14},{12,8},{14,10},{16,20},{18,... | collective-permute-start | bytes 786440 | tf_op jit(solution)/shard_map/ppermute | solution.py:32
  26.1 10.1 %collective-permute-start.12 = (f32[512,128]{1,0:T(8,128)S(1)}, f32[512,128]{1,0:T(8,128)S(1)}, u32[]{:S(2)}, u32[]{:S(2)}) collective-permute-start(f32[512,128]{1,0:T(8,128)S(1)} %get-tuple-element.146.refs_0_), channel_id=1, source_target_pairs={{1,0},{0,1},{3,2},{2,3},{5,4},{4,5},{7,6},{6,7},{9,8},{8,9},{11,10... | collective-permute-start | bytes 786440 | tf_op jit(solution)/shard_map/ppermute | solution.py:38
  27.7 8.9 %collective-permute-start.11 = (f32[128,256]{1,0:T(8,128)S(1)}, f32[128,256]{1,0:T(8,128)S(1)}, u32[]{:S(2)}, u32[]{:S(2)}) collective-permute-start(f32[128,256]{1,0:T(8,128)S(1)} %get-tuple-element.143.refs_0_), channel_id=1, source_target_pairs={{0,8},{2,10},{4,12},{6,14},{8,0},{10,2},{12,4},{14,6},{16,24},{18,... | collective-permute-start | bytes 393224 | tf_op jit(solution)/shard_map/ppermute | solution.py:32
  29.6 7.1 %collective-permute-start.15 = (f32[128,256]{1,0:T(8,128)S(1)}, f32[128,256]{1,0:T(8,128)S(1)}, u32[]{:S(2)}, u32[]{:S(2)}) collective-permute-start(f32[128,256]{1,0:T(8,128)S(1)} %get-tuple-element.156.refs_2_), channel_id=1, source_target_pairs={{0,8},{2,10},{4,12},{6,14},{8,0},{10,2},{12,4},{14,6},{16,24},{18,... | collective-permute-start | bytes 393224 | tf_op jit(solution)/shard_map/ppermute | solution.py:32
  30.8 11.8 %collective-permute-start.19 = (f32[256,256]{1,0:T(8,128)S(1)}, f32[256,256]{1,0:T(8,128)S(1)}, u32[]{:S(2)}, u32[]{:S(2)}) collective-permute-start(f32[256,256]{1,0:T(8,128)S(1)} %get-tuple-element.166.refs_0_), channel_id=1, source_target_pairs={{0,4},{2,6},{4,0},{6,2},{8,12},{10,14},{12,8},{14,10},{16,20},{18,... | collective-permute-start | bytes 786440 | tf_op jit(solution)/shard_map/ppermute | solution.py:32
  34.5 12.5 %collective-permute-start.18 = (f32[256,256]{1,0:T(8,128)S(1)}, f32[256,256]{1,0:T(8,128)S(1)}, u32[]{:S(2)}, u32[]{:S(2)}) collective-permute-start(f32[256,256]{1,0:T(8,128)S(1)} %get-tuple-element.165.refs_0_), channel_id=1, source_target_pairs={{0,8},{2,10},{4,12},{6,14},{8,0},{10,2},{12,4},{14,6},{16,24},{18,... | collective-permute-start | bytes 786440 | tf_op jit(solution)/shard_map/ppermute | solution.py:32
  37.0 14.1 %collective-permute-start.17 = (f32[256,256]{1,0:T(8,128)S(1)}, f32[256,256]{1,0:T(8,128)S(1)}, u32[]{:S(2)}, u32[]{:S(2)}) collective-permute-start(f32[256,256]{1,0:T(8,128)S(1)} %get-tuple-element.164.refs_0_), channel_id=1, source_target_pairs={{0,16},{2,18},{4,20},{6,22},{8,24},{10,26},{12,28},{14,30},{16,0},... | collective-permute-start | bytes 786440 | tf_op jit(solution)/shard_map/ppermute | solution.py:32
  39.7 11.5 %collective-permute-start.20 = (f32[512,128]{1,0:T(8,128)S(1)}, f32[512,128]{1,0:T(8,128)S(1)}, u32[]{:S(2)}, u32[]{:S(2)}) collective-permute-start(f32[512,128]{1,0:T(8,128)S(1)} %get-tuple-element.171.refs_0_), channel_id=1, source_target_pairs={{1,0},{0,1},{3,2},{2,3},{5,4},{4,5},{7,6},{6,7},{9,8},{8,9},{11,10... | collective-permute-start | bytes 786440 | tf_op jit(solution)/shard_map/ppermute | solution.py:38
  41.0 13.5 %collective-permute-start.16 = (f32[256,256]{1,0:T(8,128)S(1)}, f32[256,256]{1,0:T(8,128)S(1)}, u32[]{:S(2)}, u32[]{:S(2)}) collective-permute-start(f32[256,256]{1,0:T(8,128)S(1)} %get-tuple-element.163.refs_0_), channel_id=1, source_target_pairs={{0,4},{2,6},{4,0},{6,2},{8,12},{10,14},{12,8},{14,10},{16,20},{18,... | collective-permute-start | bytes 786440 | tf_op jit(solution)/shard_map/ppermute | solution.py:32
  43.0 15.2 %collective-permute-start.23 = (f32[256,256]{1,0:T(8,128)S(1)}, f32[256,256]{1,0:T(8,128)S(1)}, u32[]{:S(2)}, u32[]{:S(2)}) collective-permute-start(f32[256,256]{1,0:T(8,128)S(1)} %get-tuple-element.187.refs_0_), channel_id=1, source_target_pairs={{0,8},{2,10},{4,12},{6,14},{8,0},{10,2},{12,4},{14,6},{16,24},{18,... | collective-permute-start | bytes 786440 | tf_op jit(solution)/shard_map/ppermute | solution.py:32
  47.4 13.9 %collective-permute-start.22 = (f32[256,256]{1,0:T(8,128)S(1)}, f32[256,256]{1,0:T(8,128)S(1)}, u32[]{:S(2)}, u32[]{:S(2)}) collective-permute-start(f32[256,256]{1,0:T(8,128)S(1)} %get-tuple-element.186.refs_0_), channel_id=1, source_target_pairs={{0,16},{2,18},{4,20},{6,22},{8,24},{10,26},{12,28},{14,30},{16,0},... | collective-permute-start | bytes 786440 | tf_op jit(solution)/shard_map/ppermute | solution.py:32
  54.9 13.5 %collective-permute-start.21 = (f32[256,256]{1,0:T(8,128)S(1)}, f32[256,256]{1,0:T(8,128)S(1)}, u32[]{:S(2)}, u32[]{:S(2)}) collective-permute-start(f32[256,256]{1,0:T(8,128)S(1)} %get-tuple-element.185.refs_0_), channel_id=1, source_target_pairs={{0,8},{2,10},{4,12},{6,14},{8,0},{10,2},{12,4},{14,6},{16,24},{18,... | collective-permute-start | bytes 786440 | tf_op jit(solution)/shard_map/ppermute | solution.py:32
  58.6 21.0 %collective-permute-start.25 = (f32[256,256]{1,0:T(8,128)S(1)}, f32[256,256]{1,0:T(8,128)S(1)}, u32[]{:S(2)}, u32[]{:S(2)}) collective-permute-start(f32[256,256]{1,0:T(8,128)S(1)} %get-tuple-element.193.refs_0_), channel_id=1, source_target_pairs={{0,16},{2,18},{4,20},{6,22},{8,24},{10,26},{12,28},{14,30},{16,0},... | collective-permute-start | bytes 786440 | tf_op jit(solution)/shard_map/ppermute | solution.py:32
  68.8 15.3 %collective-permute-start.24 = (f32[256,256]{1,0:T(8,128)S(1)}, f32[256,256]{1,0:T(8,128)S(1)}, u32[]{:S(2)}, u32[]{:S(2)}) collective-permute-start(f32[256,256]{1,0:T(8,128)S(1)} %get-tuple-element.192.refs_0_), channel_id=1, source_target_pairs={{0,16},{2,18},{4,20},{6,22},{8,24},{10,26},{12,28},{14,30},{16,0},... | collective-permute-start | bytes 786440 | tf_op jit(solution)/shard_map/ppermute | solution.py:32
